TPU v7x, 32 devices: a whole 2x2x4 slice. The times are simulated.
32 devices in a mesh: ctx: 16 (over z, y, x), fsdp: 2 (over core).
Axes of the slice: x: 2, y: 2, z: 4, core: 2. Of those that a mesh axis runs over, the one named last changes fastest.
Arguments:
- out_grad: bfloat16 [4096, 16384], P('fsdp', 'ctx'), may hold values from -6 to 6
- gate_values: bfloat16 [4096, 16384], P('fsdp', 'ctx'), may hold values from -6 to 6
- kv_product: bfloat16 [4096, 16384], P('fsdp', 'ctx'), may hold values from -6 to 6
- w_out: bfloat16 [4096, 4096], P('ctx', 'fsdp'), may hold values from -0.09375 to 0.09375
- filters: bfloat16 [2, 16, 128, 128], P('fsdp', 'ctx'), may hold values from -0.5 to 0.5
Outputs:
- gate_grad: float32 [4096, 16384], P('fsdp', 'ctx')
- kv_grad: bfloat16 [4096, 16384], P('fsdp', 'ctx')
- filter_grad: float32 [2, 16, 128, 128], P('fsdp', 'ctx')
- w_grad: float32 [4096, 4096], P('ctx', 'fsdp')
All inputs are finite; a program needn't handle non-finite values.
Results may differ from a plain program's by a relative error of at most 0.0049.
Values may be sent and summed in bfloat16 or wider, within the bound.
No kernel may reach another device: no remote copies, remote signals or barrier semaphores. Data moves between devices by JAX's collectives and lax.ppermute only.
A program may use at most 192 MiB of HBM per device.

v0:
```python
import math

import jax
import jax.numpy as jnp
import ml_dtypes
import numpy as np
from jax import lax
from jax.experimental import pallas as pl
from jax.experimental.pallas import tpu as pltpu
from jax.sharding import PartitionSpec as P

F32 = jnp.float32
BF16 = jnp.bfloat16
MIB = 1024 * 1024
PARTS = 2


def split_pair(matrix):
    high = matrix.astype(ml_dtypes.bfloat16)
    low = (matrix - high.astype(np.float64)).astype(ml_dtypes.bfloat16)
    return high, low


def dft_matrices(taps):
    points = 2 * taps
    place = np.arange(taps)
    angle = 2.0 * np.pi * ((place[:, None] * place[None, :]) % points) / points
    turn = (-1.0) ** place
    forward = np.concatenate([np.cos(angle), -np.sin(angle)], axis=1)
    forward[:, taps] = turn
    weight = np.full((taps, 1), 2.0 / points)
    weight[0] = 1.0 / points
    backward = np.concatenate([weight * np.cos(angle), -weight * np.sin(angle)], axis=0)
    backward[taps, :] = turn / points
    forward = np.concatenate(split_pair(forward), axis=0)
    backward = np.concatenate(split_pair(backward), axis=1)
    return forward, backward


def spectrum(block, forward):
    taps = block.shape[1]
    both = jnp.dot(jnp.concatenate([block, block], axis=1), forward, preferred_element_type=F32)
    return both[:, :taps], both[:, taps:]


def inverse(real, imag, backward):
    taps = real.shape[1]
    whole = jnp.concatenate([real, imag], axis=1)
    high = whole.astype(BF16)
    low = (whole - high.astype(F32)).astype(BF16)
    both = jnp.dot(high, backward, preferred_element_type=F32)
    rest = jnp.dot(low, backward[:, :taps], preferred_element_type=F32)
    return both[:, :taps] + both[:, taps:] + rest


def lane_facts(taps):
    lane = lax.broadcasted_iota(jnp.int32, (1, taps), 1)
    sign = jnp.where(lane % 2 == 0, 1.0, -1.0)
    return lane == 0, sign


def filter_spectrum(filt, forward, first):
    real, imag = spectrum(filt, forward)
    return real, jnp.where(first, imag, real), jnp.where(first, 0.0, imag)


def mix_kernel(filt_ref, kv_ref, prior_ref, gate_ref, forward_ref, backward_ref, mixed_ref, gated_ref):
    taps = filt_ref.shape[1]
    blocks = kv_ref.shape[1] // taps
    forward, backward = forward_ref[...], backward_ref[...]
    first, sign = lane_facts(taps)
    sign_imag = jnp.where(first, 1.0, sign)
    h_real, h_last, h_imag = filter_spectrum(filt_ref[...], forward, first)
    prev_real, prev_imag = spectrum(prior_ref[...], forward)
    for b in range(blocks):
        span = slice(b * taps, (b + 1) * taps)
        real, imag = spectrum(kv_ref[:, span], forward)
        win_real = real + sign * prev_real
        win_imag = imag + sign_imag * prev_imag
        mixed = inverse(
            h_real * win_real - h_imag * win_imag, h_last * win_imag + h_imag * win_real, backward
        ).astype(BF16)
        mixed_ref[:, span] = mixed
        gated_ref[:, span] = (gate_ref[:, span].astype(F32) * mixed.astype(F32)).astype(BF16)
        prev_real, prev_imag = real, imag


def run_mix(filters, kv, prior, gate, forward, backward):
    chan, seq_len = kv.shape
    taps = filters.shape[1]
    group = min(256, chan)
    rows = lambda width: pl.BlockSpec((group, width), lambda g: (g, 0))
    whole = lambda array: pl.BlockSpec(array.shape, lambda g: (0, 0))
    return pl.pallas_call(
        mix_kernel,
        grid=(chan // group,),
        in_specs=[rows(taps), rows(seq_len), rows(taps), rows(seq_len), whole(forward), whole(backward)],
        out_specs=[rows(seq_len), rows(seq_len)],
        out_shape=[jax.ShapeDtypeStruct((chan, seq_len), BF16)] * 2,
        compiler_params=pltpu.CompilerParams(vmem_limit_bytes=32 * MIB),
        cost_estimate=pl.CostEstimate(
            flops=14 * chan * seq_len * 2 * taps, bytes_accessed=8 * chan * seq_len, transcendentals=0
        ),
        name="mix_kernel",
    )(filters, kv, prior, gate, forward, backward)


def weight_kernel(place_ref, g00, g01, g10, g11, left_ref, right_ref, send_a, keep_a, send_b, keep_b):
    rows = g00.shape[0]
    stack = jnp.concatenate([g01[...], g11[...], g00[...], g10[...]], axis=0)
    contract = (((1,), (1,)), ((), ()))
    left = lax.dot_general(stack, left_ref[...], contract, preferred_element_type=F32).astype(BF16)
    send_a[0] = left[:rows]
    send_a[1] = left[rows : 2 * rows]
    keep_a[0] = left[2 * rows : 3 * rows]
    keep_a[1] = left[3 * rows :]
    right = lax.dot_general(stack, right_ref[...], contract, preferred_element_type=F32).astype(BF16)
    send_b[0] = right[3 * rows :]
    send_b[1] = right[rows : 2 * rows]
    keep_b[0] = right[2 * rows : 3 * rows]
    keep_b[1] = right[:rows]


def run_weight(place, grad_full, gated, rows):
    chan, seq_len = gated.shape
    width = chan // 4
    grad_spec = lambda k: pl.BlockSpec((rows, seq_len), lambda n, place: (place[k], 0))
    gated_spec = lambda first: pl.BlockSpec((width, seq_len), lambda n, place: (n + first, 0))
    out_spec = pl.BlockSpec((2, rows, width), lambda n, place: (0, 0, n))
    return pl.pallas_call(
        weight_kernel,
        grid_spec=pltpu.PrefetchScalarGridSpec(
            num_scalar_prefetch=1,
            grid=(2,),
            in_specs=[grad_spec(k) for k in range(4)] + [gated_spec(0), gated_spec(2)],
            out_specs=[out_spec] * 4,
        ),
        out_shape=[jax.ShapeDtypeStruct((2, rows, chan // 2), BF16)] * 4,
        compiler_params=pltpu.CompilerParams(vmem_limit_bytes=48 * MIB),
        cost_estimate=pl.CostEstimate(
            flops=8 * rows * chan * seq_len,
            bytes_accessed=2 * (4 * rows * (seq_len + chan) + chan * seq_len),
            transcendentals=0,
        ),
        name="weight_kernel",
    )(place, grad_full, grad_full, grad_full, grad_full, gated, gated)


def product_kernel(count, place_ref, grad_hbm, *refs):
    pieces = refs[:count]
    mixed_ref, gate_ref, kv_ref, prior_ref, filt_ref, forward_ref, backward_ref = refs[count : count + 7]
    gate_grad_ref, kv_grad_ref, last_ref, head_ref, filt_grad_ref, conv, grad, sems = refs[-8:]
    step = pl.program_id(0)
    rows = pieces[0].shape[1]

    @pl.when(step == 0)
    def _():
        copies = [
            pltpu.make_async_copy(
                grad_hbm.at[pl.ds(pl.multiple_of(place_ref[k] * rows, rows), rows)],
                grad.at[pl.ds(k * rows, rows)],
                sems.at[k],
            )
            for k in range(count)
        ]
        for copy in copies:
            copy.start()
        for copy in copies:
            copy.wait()

    wide = [piece[...] for piece in pieces]
    total = jnp.dot(jnp.concatenate(wide, axis=1), grad[...], preferred_element_type=F32)
    gate_grad_ref[...] = total * mixed_ref[...].astype(F32)
    conv[...] = (total * gate_ref[...].astype(F32)).astype(BF16)

    group, taps = filt_ref.shape
    blocks = kv_ref.shape[1] // taps
    forward, backward = forward_ref[...], backward_ref[...]
    first, sign = lane_facts(taps)
    sign_imag = jnp.where(first, 1.0, sign)
    part = min(256, group)
    for at in range(0, group, part):
        chans = slice(at, at + part)
        h_real, h_last, h_imag = filter_spectrum(filt_ref[chans, :], forward, first)

        def pull_back(win_real, win_imag):
            return inverse(
                h_real * win_real + h_imag * win_imag, h_last * win_imag - h_imag * win_real, backward
            )

        past_real, past_imag = spectrum(prior_ref[chans, :], forward)
        g_real = g_imag = sum_real = sum_imag = 0.0
        for b in range(blocks):
            span = slice(b * taps, (b + 1) * taps)
            now_real, now_imag = spectrum(conv[chans, span], forward)
            back = pull_back(g_real + sign * now_real, g_imag + sign_imag * now_imag).astype(BF16)
            if b == 0:
                head_ref[chans, :] = back
            else:
                kv_grad_ref[chans, (b - 1) * taps : b * taps] = back
            x_real, x_imag = spectrum(kv_ref[chans, span], forward)
            win_real = x_real + sign * past_real
            win_imag = x_imag + sign_imag * past_imag
            win_last, win_skew = jnp.where(first, win_imag, win_real), jnp.where(first, 0.0, win_imag)
            sum_real = sum_real + now_real * win_real + now_imag * win_skew
            sum_imag = sum_imag + now_imag * win_last - now_real * win_skew
            g_real, g_imag = now_real, now_imag
            past_real, past_imag = x_real, x_imag
        last = pull_back(g_real, g_imag)
        last_ref[chans, :] = last
        kv_grad_ref[chans, (blocks - 1) * taps :] = last.astype(BF16)
        filt_grad_ref[chans, :] = inverse(sum_real, sum_imag, backward)


def run_product(part, place, grad_full, pieces, mixed, gate, kv, prior, filters, forward, backward, written):
    chan, seq_len = mixed.shape
    taps = filters.shape[1]
    depth = grad_full.shape[0]
    rows = pieces[0].shape[1]
    count = len(pieces)
    group = min(512, chan // PARTS)
    steps = chan // PARTS // group
    offset = part * steps
    local_offset = offset % (chan // 2 // group)
    full = lambda width: pl.BlockSpec((group, width), lambda m, place: (m + offset, 0))
    local = pl.BlockSpec((group, rows), lambda m, place: (m + local_offset, 0))
    whole = lambda array: pl.BlockSpec(array.shape, lambda m, place: (0, 0))
    anywhere = pl.BlockSpec(memory_space=pl.ANY)
    return pl.pallas_call(
        lambda *refs: product_kernel(count, *refs),
        grid_spec=pltpu.PrefetchScalarGridSpec(
            num_scalar_prefetch=1,
            grid=(steps,),
            in_specs=[anywhere]
            + [local if piece.shape[0] < chan else full(rows) for piece in pieces]
            + [full(seq_len), full(seq_len), full(seq_len), full(taps), full(taps)]
            + [whole(forward), whole(backward)]
            + [anywhere] * len(written),
            out_specs=[full(seq_len), full(seq_len), full(taps), full(taps), full(taps)],
            scratch_shapes=[
                pltpu.VMEM((group, seq_len), BF16),
                pltpu.VMEM((depth, seq_len), BF16),
                pltpu.SemaphoreType.DMA((count,)),
            ],
        ),
        out_shape=[
            jax.ShapeDtypeStruct((chan, seq_len), F32),
            jax.ShapeDtypeStruct((chan, seq_len), BF16),
            jax.ShapeDtypeStruct((chan, taps), F32),
            jax.ShapeDtypeStruct((chan, taps), BF16),
            jax.ShapeDtypeStruct((chan, taps), F32),
        ],
        input_output_aliases={9 + count + k: k for k in range(len(written))},
        compiler_params=pltpu.CompilerParams(vmem_limit_bytes=50 * MIB),
        cost_estimate=pl.CostEstimate(
            flops=group * steps * seq_len * (2 * depth + 32 * taps),
            bytes_accessed=2 * depth * (seq_len + group * steps) + 12 * group * steps * seq_len,
            transcendentals=0,
        ),
        name="product_kernel",
    )(place, grad_full, *pieces, mixed, gate, kv, prior, filters, forward, backward, *written)


def after(array, *earlier):
    return lax.optimization_barrier((array,) + earlier)[0] if earlier else array


class Layout:
    def __init__(self):
        self.count = lax.axis_size("ctx")
        self.depth = self.count // 4
        index = lax.axis_index("ctx")
        self.z, self.y, self.x = index // 4, (index // 2) % 2, index % 2
        self.pairs_x = [(i, i ^ 1) for i in range(self.count)]
        self.pairs_y = [(i, i ^ 2) for i in range(self.count)]

    def pairs_z(self, by):
        return [(i, (i + 4 * by) % self.count) for i in range(self.count)]

    def places(self, by):
        base = 4 * ((self.z + by) % self.depth)
        return [base + 2 * (self.y ^ dy) + (self.x ^ dx) for dy in range(2) for dx in range(2)]


class Stages:
    def __init__(self, at):
        self.at = at
        self.arrived = [()] * 3
        self.now = []
        self.ready = self.next_ready = ()

    def advance(self):
        self.arrived.append(tuple(self.now))
        self.now, self.ready, self.next_ready = [], self.next_ready, ()

    def hold(self, array):
        return after(array, *self.arrived[-2])

    def finished(self, *arrays):
        self.next_ready += arrays

    def send(self, array, pairs, *earlier):
        got = lax.ppermute(after(array, *self.arrived[-2], *self.ready, *earlier), "ctx", pairs)
        self.now.append(got)
        return got

    def swap_x(self, array, *earlier):
        return self.send(array, self.at.pairs_x, *earlier)

    def swap_y(self, array, *earlier):
        return self.send(array, self.at.pairs_y, *earlier)


def pick(bit, array, axis):
    halves = [lax.index_in_dim(array, k, axis, keepdims=False) for k in range(2)]
    return jnp.where(bit == 0, halves[0], halves[1])


def gather_filters(at, own):
    def ordered(bit, mine, other):
        return jnp.stack([jnp.where(bit == 0, mine, other), jnp.where(bit == 0, other, mine)], axis=1)

    slots = [lax.ppermute(own, "ctx", at.pairs_z(by)) for by in range(at.depth - 1, 0, -1)]
    ring = jnp.stack((slots + [own]) * 2)
    column = lax.dynamic_slice_in_dim(ring, at.depth - 1 - at.z, at.depth, axis=0)
    from_x = lax.ppermute(column, "ctx", at.pairs_x)
    pair = ordered(at.x, column, from_x)
    from_y = lax.ppermute(pair, "ctx", at.pairs_y)
    whole = ordered(at.y, pair, from_y).reshape((at.count * own.shape[0],) + own.shape[1:])
    return whole, from_x, from_y


def reduce_filters(at, part, chan_count):
    taps = part.shape[1]
    part = part.reshape(at.depth, 2, 2, chan_count, taps)
    part = pick(at.x, part, 2) + lax.ppermute(pick(1 - at.x, part, 2), "ctx", at.pairs_x)
    part = pick(at.y, part, 1) + lax.ppermute(pick(1 - at.y, part, 1), "ctx", at.pairs_y)
    at_z = lambda by: lax.dynamic_index_in_dim(part, (at.z + by) % at.depth, 0, keepdims=False)
    total = at_z(0)
    for by in range(1, at.depth):
        total = total + lax.ppermute(at_z(by), "ctx", at.pairs_z(by))
    return total


def on_device(out_grad, gate_values, kv_product, w_out, filters):
    at = Layout()
    stages = Stages(at)
    chan_count = filters.shape[2]
    taps = filters.shape[3]
    seq_len = out_grad.shape[1]
    rows, chan = w_out.shape
    half = chan // 2
    norm_scale = 1.0 / math.sqrt(at.count * seq_len)
    to_right = [(i, i + 1) for i in range(at.count - 1)]
    to_left = [(i + 1, i) for i in range(at.count - 1)]
    forward, backward = (jnp.asarray(m) for m in dft_matrices(taps))

    prior = lax.ppermute(kv_product[:, seq_len - taps :], "ctx", to_right)
    all_filters, first_x, first_y = gather_filters(at, filters.reshape(chan_count, taps))
    grad_full = lax.all_gather(out_grad, "fsdp", axis=0, tiled=True)

    near = sorted(range(at.depth), key=lambda d: min(d, at.depth - d))
    far = near[::-1]
    own = w_out.T
    shards = [own]
    for by in near[1:]:
        shards.append(lax.ppermute(after(own, *shards[1:][-1:]), "ctx", at.pairs_z(by)))
    from_x, from_y, diag_a, diag_b = {}, {}, {}, {}
    kept, summed = {}, {}

    def gather_first(k):
        earlier = {1: (from_x.get(0), from_y.get(0)), 2: (first_x,), 3: (first_y,)}.get(k, ())
        from_x[k] = stages.swap_x(shards[k], *earlier)
        from_y[k] = stages.swap_y(shards[k], *earlier)

    def gather_second(k):
        diag_a[k] = stages.swap_x(from_y[k][:half])
        diag_b[k] = stages.swap_y(from_x[k][half:])

    def weight_part(k):
        place = jnp.stack(at.places(far[k])).astype(jnp.int32)
        kept[k] = run_weight(place, grad_full, stages.hold(gated), rows)

    def reduce_first(k):
        send_a, keep_a, send_b, keep_b = kept[k]
        kept[k] = (keep_a, stages.swap_x(send_a), keep_b, stages.swap_y(send_b))

    def reduce_second(k):
        keep_a, got_a, keep_b, got_b = kept[k]
        next_a = (keep_a[1].astype(F32) + got_a[1].astype(F32)).astype(BF16)
        next_b = (keep_b[1].astype(F32) + got_b[1].astype(F32)).astype(BF16)
        kept[k] = (keep_a, got_a, stages.swap_y(next_a), keep_b, got_b, stages.swap_x(next_b))

    def reduce_third(k):
        keep_a, got_a, last_a, keep_b, got_b, last_b = kept.pop(k)
        sum_a = keep_a[0].astype(F32) + got_a[0].astype(F32) + last_a.astype(F32)
        sum_b = keep_b[0].astype(F32) + got_b[0].astype(F32) + last_b.astype(F32)
        joint = jnp.concatenate([sum_a, sum_b], axis=1)
        by = far[k]
        summed[k] = joint if by == 0 else lax.ppermute(joint.astype(BF16), "ctx", at.pairs_z(by))

    mixed = gated = place = products = None

    def mix():
        nonlocal mixed, gated
        mixed, gated = run_mix(all_filters, stages.hold(kv_product), prior, gate_values, forward, backward)

    def product(part):
        nonlocal products
        diag = diag_a if 2 * part < PARTS else diag_b
        pieces = [p for k in range(at.depth) for p in (shards[k], from_x[k], from_y[k], diag[k])]
        places = jnp.stack([c for by in near for c in at.places(-by)]).astype(jnp.int32)
        products = run_product(
            part, places, grad_full, pieces, stages.hold(mixed), gate_values, kv_product, prior,
            all_filters, forward, backward, products or (),
        )
        stages.finished(products[3])

    depth = at.depth
    plan = {}
    for k in range(depth):
        plan.setdefault(k, []).append((gather_first, k))
        plan.setdefault(k + 2, []).append((gather_second, k))
        plan.setdefault(k + depth, []).append((reduce_first, k))
        plan.setdefault(k + depth + 2, []).append((reduce_second, k))
    for stage in range(max(2 * depth + 4, depth + 3 + PARTS)):
        if stage == 2:
            mix()
        for k in range(depth):
            if stage == max(3, k + depth - 1 + 0):
                weight_part(k)
            if stage == k + depth + 4:
                reduce_third(k)
        for part in range(PARTS):
            if stage == depth + 3 + part:
                product(part)
        for action, k in plan.get(stage, []):
            action(k)
        stages.advance()

    total = summed[depth - 1]
    for k in range(depth - 1):
        total = total + summed[k].astype(F32)
    w_grad = total * norm_scale

    gate_grad, kv_grad, last, head, filt_part = products
    tail = lax.ppermute(head, "ctx", to_left)
    kv_grad = lax.dynamic_update_slice(
        kv_grad, (last + tail.astype(F32)).astype(BF16), (0, seq_len - taps)
    )
    filter_grad = reduce_filters(at, filt_part, chan_count) * norm_scale
    return (gate_grad, kv_grad, filter_grad.reshape(filters.shape), w_grad)


def solution(mesh):
    in_specs = (
        P("fsdp", "ctx"),
        P("fsdp", "ctx"),
        P("fsdp", "ctx"),
        P("ctx", "fsdp"),
        P("fsdp", "ctx", None, None),
    )
    out_specs = (P("fsdp", "ctx"), P("fsdp", "ctx"), P("fsdp", "ctx", None, None), P("ctx", "fsdp"))
    return jax.shard_map(
        on_device, mesh=mesh, in_specs=in_specs, out_specs=out_specs, check_vma=False
    )
```

profile of v0, /device:TPU:0, one launch (start us, length us, event | category | flops | bytes accessed | tf_op | source)
XLA Modules:
  0.0 404.6 jit_solution(7362055718372069815)
XLA Ops:
  7.9 5.1 %collective-permute-start.8 = (bf16[128,128]{1,0:T(8,128)(2,1)S(1)}, bf16[128,128]{1,0:T(8,128)(2,1)S(1)}, u32[]{:S(2)}, u32[]{:S(2)}) collective-permute-start(bf16[128,128]{1,0:T(8,128)(2,1)S(1)} %bitcast.158), channel_id=1, source_target_pairs={{0,24},{2,26},{4,28},{6,30},{8,0},{10,2},{12,4},{14,6},{16,8},{18,... | collective-permute-start | bytes 98312 | tf_op jit(solution)/shard_map/ppermute | solution.py:323
  17.7 2.5 collective-permute-start.3
  24.5 18.6 %collective-permute-done.3.refs_6_ = bf16[2048,256]{1,0:T(8,128)(2,1)} collective-permute-done((bf16[2048,256]{1,0:T(8,128)(2,1)S(1)}, bf16[2048,256]{1,0:T(8,128)(2,1)}, u32[]{:S(2)}, u32[]{:S(2)}) %collective-permute-start.3) | collective-permute-done | bytes 1048608 | tf_op jit(solution)/shard_map/ppermute | solution.py:367
  48.6 3.8 collective-permute-done.11
  56.4 2.7 collective-permute-start.22
  59.3 6.7 %collective-permute-done.7.refs_10_ = bf16[2048,256]{1,0:T(8,128)(2,1)} collective-permute-done((bf16[2048,256]{1,0:T(8,128)(2,1)S(1)}, bf16[2048,256]{1,0:T(8,128)(2,1)}, u32[]{:S(2)}, u32[]{:S(2)}) %collective-permute-start.7) | collective-permute-done | bytes 1048608 | tf_op jit(solution)/shard_map/ppermute | solution.py:367
  66.4 20.9 %collective-permute-done.17 = bf16[4,2,128,128]{3,2,0,1:T(8,128)(2,1)} collective-permute-done((bf16[4,2,128,128]{3,2,0,1:T(8,128)(2,1)}, bf16[4,2,128,128]{3,2,0,1:T(8,128)(2,1)}, u32[]{:S(2)}, u32[]{:S(2)}) %collective-permute-start.17) | collective-permute-done | bytes 262176 | tf_op jit(solution)/shard_map/ppermute | solution.py:328
  90.6 2.5 collective-permute-start.2
  97.4 15.9 %mix_kernel.1 = (bf16[2048,1024]{1,0:T(8,128)(2,1)S(1)}, bf16[2048,1024]{1,0:T(8,128)(2,1)S(1)}) custom-call(bf16[2048,128]{1,0:T(8,128)(2,1)S(1)} %bitcast.146, bf16[2048,1024]{1,0:T(8,128)(2,1)S(1)} %copy-done.1, bf16[2048,128]{1,0:T(8,128)(2,1)S(1)} %collective-permute-done.22.prior_ref.refs_21_, bf16[2048,1024]{1,0:T(8,128)(2,1)S(1)} %copy-done.2, ...), custom_call_target="tpu_custom_call" | custom-call | flops 7516192768 | bytes 16777216 | tf_op jit(solution)/shard_map/mix_kernel/pallas_call | solution.py:94
  120.3 7.8 %weight_kernel.4 = (bf16[2,256,1024]{2,1,0:T(8,128)(2,1)}, bf16[2,256,1024]{2,1,0:T(8,128)(2,1)S(1)}, bf16[2,256,1024]{2,1,0:T(8,128)(2,1)S(1)}, bf16[2,256,1024]{2,1,0:T(8,128)(2,1)S(1)}) custom-call(s32[4]{0:T(128)S(1)} %get-tuple-element.139.place_ref, bf16[4096,1024]{1,0:T(8,128)(2,1)} %all-gather.2.cloned.1.call-done.g00.g01.g10.g11.refs_1_, ...), custom_call_target="tpu_custom_call" | custom-call | flops 4294967296 | bytes 10485760 | tf_op jit(solution)/shard_map/weight_kernel/pallas_call | solution.py:130
  135.1 20.4 %collective-permute-done.6.refs_9_ = bf16[1024,256]{1,0:T(8,128)(2,1)} collective-permute-done((bf16[1024,256]{1,0:T(8,128)(2,1)}, bf16[1024,256]{1,0:T(8,128)(2,1)}, u32[]{:S(2)}, u32[]{:S(2)}) %collective-permute-start.6) | collective-permute-done | bytes 524320 | tf_op jit(solution)/shard_map/ppermute | solution.py:303
  155.5 2.5 collective-permute-start.24
  158.0 7.8 %weight_kernel.6 = (bf16[2,256,1024]{2,1,0:T(8,128)(2,1)}, bf16[2,256,1024]{2,1,0:T(8,128)(2,1)S(1)}, bf16[2,256,1024]{2,1,0:T(8,128)(2,1)S(1)}, bf16[2,256,1024]{2,1,0:T(8,128)(2,1)S(1)}) custom-call(s32[4]{0:T(128)S(1)} %get-tuple-element.141.place_ref, bf16[4096,1024]{1,0:T(8,128)(2,1)} %all-gather.2.cloned.1.call-done.g00.g01.g10.g11.refs_1_, ...), custom_call_target="tpu_custom_call" | custom-call | flops 4294967296 | bytes 10485760 | tf_op jit(solution)/shard_map/weight_kernel/pallas_call | solution.py:130
  168.8 5.7 %collective-permute-done.20.refs_9_ = bf16[1024,256]{1,0:T(8,128)(2,1)} collective-permute-done((bf16[1024,256]{1,0:T(8,128)(2,1)}, bf16[1024,256]{1,0:T(8,128)(2,1)}, u32[]{:S(2)}, u32[]{:S(2)}) %collective-permute-start.20) | collective-permute-done | bytes 524320 | tf_op jit(solution)/shard_map/ppermute | solution.py:303
  183.3 7.8 %weight_kernel.5 = (bf16[2,256,1024]{2,1,0:T(8,128)(2,1)S(1)}, bf16[2,256,1024]{2,1,0:T(8,128)(2,1)S(1)}, bf16[2,256,1024]{2,1,0:T(8,128)(2,1)S(1)}, bf16[2,256,1024]{2,1,0:T(8,128)(2,1)S(1)}) custom-call(s32[4]{0:T(128)S(1)} %get-tuple-element.140.place_ref, bf16[4096,1024]{1,0:T(8,128)(2,1)} %all-gather.2.cloned.1.call-done.g00.g01.g10.g11.refs_1_, ...), custom_call_target="tpu_custom_call" | custom-call | flops 4294967296 | bytes 10485760 | tf_op jit(solution)/shard_map/weight_kernel/pallas_call | solution.py:130
  193.5 15.7 %collective-permute-done.25.refs_13_ = bf16[1024,256]{1,0:T(8,128)(2,1)S(1)} collective-permute-done((bf16[1024,256]{1,0:T(8,128)(2,1)S(1)}, bf16[1024,256]{1,0:T(8,128)(2,1)S(1)}, u32[]{:S(2)}, u32[]{:S(2)}) %collective-permute-start.25) | collective-permute-done | bytes 524320 | tf_op jit(solution)/shard_map/ppermute | solution.py:303
  215.3 9.3 %collective-permute-done.21.refs_17_ = bf16[1024,256]{1,0:T(8,128)(2,1)S(1)} collective-permute-done((bf16[1024,256]{1,0:T(8,128)(2,1)S(1)}, bf16[1024,256]{1,0:T(8,128)(2,1)S(1)}, u32[]{:S(2)}, u32[]{:S(2)}) %collective-permute-start.21) | collective-permute-done | bytes 524320 | tf_op jit(solution)/shard_map/ppermute | solution.py:303
  225.5 2.5 collective-permute-start.40
  231.1 36.1 %product_kernel.2 = (f32[2048,1024]{1,0:T(8,128)}, bf16[2048,1024]{1,0:T(8,128)(2,1)}, f32[2048,128]{1,0:T(8,128)}, bf16[2048,128]{1,0:T(8,128)(2,1)S(1)}, f32[2048,128]{1,0:T(8,128)}) custom-call(s32[16]{0:T(128)S(1)} %stack.169.refs_0_, bf16[4096,1024]{1,0:T(8,128)(2,1)} %all-gather.2.cloned.1.call-done.g00.g01.g10.g11.refs_1_, ...), custom_call_target="tpu_custom_call" | custom-call | flops 12884901888 | bytes 29360128 | tf_op jit(solution)/shard_map/product_kernel/pallas_call | solution.py:229
  267.2 7.8 %weight_kernel.7 = (bf16[2,256,1024]{2,1,0:T(8,128)(2,1)}, bf16[2,256,1024]{2,1,0:T(8,128)(2,1)S(1)}, bf16[2,256,1024]{2,1,0:T(8,128)(2,1)S(1)}, bf16[2,256,1024]{2,1,0:T(8,128)(2,1)S(1)}) custom-call(s32[4]{0:T(128)S(1)} %get-tuple-element.142.place_ref, bf16[4096,1024]{1,0:T(8,128)(2,1)} %all-gather.2.cloned.1.call-done.g00.g01.g10.g11.refs_1_, ...), custom_call_target="tpu_custom_call" | custom-call | flops 4294967296 | bytes 10485760 | tf_op jit(solution)/shard_map/weight_kernel/pallas_call | solution.py:130
  282.8 6.1 %collective-permute-start.45 = (bf16[256,2048]{1,0:T(8,128)(2,1)}, bf16[256,2048]{1,0:T(8,128)(2,1)S(1)}, u32[]{:S(2)}, u32[]{:S(2)}) collective-permute-start(bf16[256,2048]{1,0:T(8,128)(2,1)} %pad_maximum_fusion), channel_id=1, source_target_pairs={{0,16},{2,18},{4,20},{6,22},{8,24},{10,26},{12,28},{14,30},{16,0},... | collective-permute-start | bytes 3145736 | tf_op jit(solution)/shard_map/ppermute | solution.py:400
  291.3 2.6 collective-permute-start.46
  295.2 6.0 %collective-permute-done.29 = bf16[2,256,1024]{2,1,0:T(8,128)(2,1)S(1)} collective-permute-done((bf16[2,256,1024]{2,1,0:T(8,128)(2,1)S(1)}, bf16[2,256,1024]{2,1,0:T(8,128)(2,1)S(1)}, u32[]{:S(2)}, u32[]{:S(2)}) %collective-permute-start.29) | collective-permute-done | bytes 1048608 | tf_op jit(solution)/shard_map/ppermute | solution.py:303
  302.2 28.0 %product_kernel.3 = (f32[2048,1024]{1,0:T(8,128)}, bf16[2048,1024]{1,0:T(8,128)(2,1)}, f32[2048,128]{1,0:T(8,128)}, bf16[2048,128]{1,0:T(8,128)(2,1)S(1)}, f32[2048,128]{1,0:T(8,128)}) custom-call(s32[16]{0:T(128)S(1)} %stack.169.refs_0_, ...), custom_call_target="tpu_custom_call", output_to_operand_aliasing={{0}: (25, {}), {1}: (26, {}), {2}: (27, {}), {3}: (28, {}),... | custom-call | flops 12884901888 | bytes 29360128 | tf_op jit(solution)/shard_map/product_kernel/pallas_call | solution.py:229
  336.0 17.0 %collective-permute-done.34 = f32[4,2,128,128]{3,2,1,0:T(8,128)S(1)} collective-permute-done((f32[4,2,128,128]{3,2,1,0:T(8,128)S(1)}, f32[4,2,128,128]{3,2,1,0:T(8,128)S(1)}, u32[]{:S(2)}, u32[]{:S(2)}) %collective-permute-start.34) | collective-permute-done | bytes 524320 | tf_op jit(solution)/shard_map/ppermute | solution.py:336
  353.0 2.5 collective-permute-start.48
  359.1 4.2 %collective-permute-done.48 = bf16[256,1024]{1,0:T(8,128)(2,1)S(1)} collective-permute-done((bf16[256,1024]{1,0:T(8,128)(2,1)S(1)}, bf16[256,1024]{1,0:T(8,128)(2,1)S(1)}, u32[]{:S(2)}, u32[]{:S(2)}) %collective-permute-start.48) | collective-permute-done | bytes 524320 | tf_op jit(solution)/shard_map/ppermute | solution.py:303
  363.7 6.0 %collective-permute-done.35 = f32[4,128,128]{2,1,0:T(8,128)S(1)} collective-permute-done((f32[4,128,128]{2,1,0:T(8,128)S(1)}, f32[4,128,128]{2,1,0:T(8,128)S(1)}, u32[]{:S(2)}, u32[]{:S(2)}) %collective-permute-start.35) | collective-permute-done | bytes 262176 | tf_op jit(solution)/shard_map/ppermute | solution.py:337
  369.7 4.6 %collective-permute-start.49 = (bf16[256,2048]{1,0:T(8,128)(2,1)S(1)}, bf16[256,2048]{1,0:T(8,128)(2,1)S(1)}, u32[]{:S(2)}, u32[]{:S(2)}) collective-permute-start(bf16[256,2048]{1,0:T(8,128)(2,1)S(1)} %pad_maximum_fusion.2), channel_id=1, source_target_pairs={{0,8},{2,10},{4,12},{6,14},{8,16},{10,18},{12,20},{14,22},{16,24},... | collective-permute-start | bytes 3145736 | tf_op jit(solution)/shard_map/ppermute | solution.py:400
  375.7 3.1 collective-permute-start.37
  378.8 11.5 %collective-permute-done.36 = f32[128,128]{1,0:T(8,128)S(1)} collective-permute-done((f32[128,128]{1,0:T(8,128)S(1)}, f32[128,128]{1,0:T(8,128)S(1)}, u32[]{:S(2)}, u32[]{:S(2)}) %collective-permute-start.36) | collective-permute-done | bytes 65568 | tf_op jit(solution)/shard_map/ppermute | solution.py:341
  390.3 2.6 collective-permute-start.38
  (188 shorter events, 93.1 us)
Async XLA Ops:
  7.2 113.1 %all-gather.2.cloned.1.call-start = ((), (), s32[]{:S(2)}) async-start(), calls=%async_computation | async-start | bytes 12582912 | tf_op jit(solution)/shard_map/all_gather | solution.py:360
  14.6 31.9 %collective-permute-start = (bf16[2048,256]{1,0:T(8,128)(2,1)S(1)}, bf16[2048,256]{1,0:T(8,128)(2,1)S(1)}, u32[]{:S(2)}, u32[]{:S(2)}) collective-permute-start(bf16[2048,256]{1,0:T(8,128)(2,1)S(1)} %bitcast.151), channel_id=1, source_target_pairs={{0,2},{2,0},{4,6},{6,4},{8,10},{10,8},{12,14},{14,12},{16,18},{18,... | collective-permute-start | bytes 3145736 | tf_op jit(solution)/shard_map/ppermute | solution.py:303
  16.1 30.4 %collective-permute-start.1 = (bf16[2048,256]{1,0:T(8,128)(2,1)S(1)}, bf16[2048,256]{1,0:T(8,128)(2,1)S(1)}, u32[]{:S(2)}, u32[]{:S(2)}) collective-permute-start(bf16[2048,256]{1,0:T(8,128)(2,1)S(1)} %bitcast.152), channel_id=1, source_target_pairs={{0,4},{2,6},{4,0},{6,2},{8,12},{10,14},{12,8},{14,10},{16,20},{18,... | collective-permute-start | bytes 3145736 | tf_op jit(solution)/shard_map/ppermute | solution.py:303
  46.5 46.6 %collective-permute-start.4 = (bf16[2048,256]{1,0:T(8,128)(2,1)}, bf16[2048,256]{1,0:T(8,128)(2,1)}, u32[]{:S(2)}, u32[]{:S(2)}) collective-permute-start(bf16[2048,256]{1,0:T(8,128)(2,1)} %collective-permute-done.3.refs_6_), channel_id=1, source_target_pairs={{0,2},{2,0},{4,6},{6,4},{8,10},{10,8},{12,14},{14,12},{16,18},{18,... | collective-permute-start | bytes 3145736 | tf_op jit(solution)/shard_map/ppermute | solution.py:303
  48.1 47.1 %collective-permute-start.5 = (bf16[2048,256]{1,0:T(8,128)(2,1)}, bf16[2048,256]{1,0:T(8,128)(2,1)}, u32[]{:S(2)}, u32[]{:S(2)}) collective-permute-start(bf16[2048,256]{1,0:T(8,128)(2,1)} %collective-permute-done.3.refs_6_), channel_id=1, source_target_pairs={{0,4},{2,6},{4,0},{6,2},{8,12},{10,14},{12,8},{14,10},{16,20},{18,... | collective-permute-start | bytes 3145736 | tf_op jit(solution)/shard_map/ppermute | solution.py:303
  54.1 33.3 %collective-permute-start.17 = (bf16[4,2,128,128]{3,2,0,1:T(8,128)(2,1)}, bf16[4,2,128,128]{3,2,0,1:T(8,128)(2,1)}, u32[]{:S(2)}, u32[]{:S(2)}) collective-permute-start(bf16[4,2,128,128]{3,2,0,1:T(8,128)(2,1)} %pad_maximum_fusion.4), channel_id=1, source_target_pairs={{0,4},{2,6},{4,0},{6,2},{8,12},{10,14},{12,8},{14,10},{16,20},{18,... | collective-permute-start | bytes 786440 | tf_op jit(solution)/shard_map/ppermute | solution.py:328
  56.4 34.2 %collective-permute-start.22 = (bf16[2048,128]{1,0:T(8,128)(2,1)}, bf16[2048,128]{1,0:T(8,128)(2,1)S(1)}, u32[]{:S(2)}, u32[]{:S(2)}) collective-permute-start(bf16[2048,128]{1,0:T(8,128)(2,1)} %slice.145), channel_id=1, source_target_pairs={{0,2},{2,4},{4,6},{6,8},{8,10},{10,12},{12,14},{14,16},{16,18},{18... | collective-permute-start | bytes 1572872 | tf_op jit(solution)/shard_map/ppermute | solution.py:358
  66.0 51.4 %collective-permute-start.16 = (bf16[2048,256]{1,0:T(8,128)(2,1)S(1)}, bf16[2048,256]{1,0:T(8,128)(2,1)}, u32[]{:S(2)}, u32[]{:S(2)}) collective-permute-start(bf16[2048,256]{1,0:T(8,128)(2,1)S(1)} %bitcast.155), channel_id=1, source_target_pairs={{0,16},{2,18},{4,20},{6,22},{8,24},{10,26},{12,28},{14,30},{16,0},... | collective-permute-start | bytes 3145736 | tf_op jit(solution)/shard_map/ppermute | solution.py:367
  89.7 27.8 %collective-permute-start.14 = (bf16[1024,256]{1,0:T(8,128)(2,1)S(1)}, bf16[1024,256]{1,0:T(8,128)(2,1)S(1)}, u32[]{:S(2)}, u32[]{:S(2)}) collective-permute-start(bf16[1024,256]{1,0:T(8,128)(2,1)S(1)} %slice.187), channel_id=1, source_target_pairs={{0,2},{2,0},{4,6},{6,4},{8,10},{10,8},{12,14},{14,12},{16,18},{18,... | collective-permute-start | bytes 1572872 | tf_op jit(solution)/shard_map/ppermute | solution.py:303
  90.6 38.4 %collective-permute-start.2 = (bf16[1024,256]{1,0:T(8,128)(2,1)}, bf16[1024,256]{1,0:T(8,128)(2,1)}, u32[]{:S(2)}, u32[]{:S(2)}) collective-permute-start(bf16[1024,256]{1,0:T(8,128)(2,1)} %slice.184), channel_id=1, source_target_pairs={{0,4},{2,6},{4,0},{6,2},{8,12},{10,14},{12,8},{14,10},{16,20},{18,... | collective-permute-start | bytes 1572872 | tf_op jit(solution)/shard_map/ppermute | solution.py:303
  93.1 35.9 %collective-permute-start.12 = (bf16[2048,256]{1,0:T(8,128)(2,1)}, bf16[2048,256]{1,0:T(8,128)(2,1)}, u32[]{:S(2)}, u32[]{:S(2)}) collective-permute-start(bf16[2048,256]{1,0:T(8,128)(2,1)} %collective-permute-done.7.refs_10_), channel_id=1, source_target_pairs={{0,2},{2,0},{4,6},{6,4},{8,10},{10,8},{12,14},{14,12},{16,18},{18,... | collective-permute-start | bytes 3145736 | tf_op jit(solution)/shard_map/ppermute | solution.py:303
  95.1 33.9 %collective-permute-start.13 = (bf16[2048,256]{1,0:T(8,128)(2,1)}, bf16[2048,256]{1,0:T(8,128)(2,1)}, u32[]{:S(2)}, u32[]{:S(2)}) collective-permute-start(bf16[2048,256]{1,0:T(8,128)(2,1)} %collective-permute-done.7.refs_10_), channel_id=1, source_target_pairs={{0,4},{2,6},{4,0},{6,2},{8,12},{10,14},{12,8},{14,10},{16,20},{18,... | collective-permute-start | bytes 3145736 | tf_op jit(solution)/shard_map/ppermute | solution.py:303
  117.5 57.0 %collective-permute-start.18 = (bf16[2048,256]{1,0:T(8,128)(2,1)}, bf16[2048,256]{1,0:T(8,128)(2,1)}, u32[]{:S(2)}, u32[]{:S(2)}) collective-permute-start(bf16[2048,256]{1,0:T(8,128)(2,1)} %collective-permute-done.16.refs_14_), channel_id=1, source_target_pairs={{0,2},{2,0},{4,6},{6,4},{8,10},{10,8},{12,14},{14,12},{16,18},{18,... | collective-permute-start | bytes 3145736 | tf_op jit(solution)/shard_map/ppermute | solution.py:303
  118.4 56.1 %collective-permute-start.19 = (bf16[2048,256]{1,0:T(8,128)(2,1)}, bf16[2048,256]{1,0:T(8,128)(2,1)}, u32[]{:S(2)}, u32[]{:S(2)}) collective-permute-start(bf16[2048,256]{1,0:T(8,128)(2,1)} %collective-permute-done.16.refs_14_), channel_id=1, source_target_pairs={{0,4},{2,6},{4,0},{6,2},{8,12},{10,14},{12,8},{14,10},{16,20},{18,... | collective-permute-start | bytes 3145736 | tf_op jit(solution)/shard_map/ppermute | solution.py:303
  129.1 52.2 %collective-permute-start.23 = (bf16[2,256,1024]{2,1,0:T(8,128)(2,1)}, bf16[2,256,1024]{2,1,0:T(8,128)(2,1)}, u32[]{:S(2)}, u32[]{:S(2)}) collective-permute-start(bf16[2,256,1024]{2,1,0:T(8,128)(2,1)} %get-tuple-element.85), channel_id=1, source_target_pairs={{0,2},{2,0},{4,6},{6,4},{8,10},{10,8},{12,14},{14,12},{16,18},{18,... | collective-permute-start | bytes 3145736 | tf_op jit(solution)/shard_map/ppermute | solution.py:303
  134.9 39.6 %collective-permute-start.20 = (bf16[1024,256]{1,0:T(8,128)(2,1)}, bf16[1024,256]{1,0:T(8,128)(2,1)}, u32[]{:S(2)}, u32[]{:S(2)}) collective-permute-start(bf16[1024,256]{1,0:T(8,128)(2,1)} %slice.189), channel_id=1, source_target_pairs={{0,2},{2,0},{4,6},{6,4},{8,10},{10,8},{12,14},{14,12},{16,18},{18,... | collective-permute-start | bytes 1572872 | tf_op jit(solution)/shard_map/ppermute | solution.py:303
  155.5 53.8 %collective-permute-start.24 = (bf16[2,256,1024]{2,1,0:T(8,128)(2,1)}, bf16[2,256,1024]{2,1,0:T(8,128)(2,1)}, u32[]{:S(2)}, u32[]{:S(2)}) collective-permute-start(bf16[2,256,1024]{2,1,0:T(8,128)(2,1)} %copy-done.12), channel_id=1, source_target_pairs={{0,4},{2,6},{4,0},{6,2},{8,12},{10,14},{12,8},{14,10},{16,20},{18,... | collective-permute-start | bytes 3145736 | tf_op jit(solution)/shard_map/ppermute | solution.py:303
  174.5 38.8 %collective-permute-start.31 = (bf16[2,256,1024]{2,1,0:T(8,128)(2,1)}, bf16[2,256,1024]{2,1,0:T(8,128)(2,1)}, u32[]{:S(2)}, u32[]{:S(2)}) collective-permute-start(bf16[2,256,1024]{2,1,0:T(8,128)(2,1)} %get-tuple-element.101), channel_id=1, source_target_pairs={{0,2},{2,0},{4,6},{6,4},{8,10},{10,8},{12,14},{14,12},{16,18},{18,... | collective-permute-start | bytes 3145736 | tf_op jit(solution)/shard_map/ppermute | solution.py:303
  178.9 30.2 %collective-permute-start.25 = (bf16[1024,256]{1,0:T(8,128)(2,1)S(1)}, bf16[1024,256]{1,0:T(8,128)(2,1)S(1)}, u32[]{:S(2)}, u32[]{:S(2)}) collective-permute-start(bf16[1024,256]{1,0:T(8,128)(2,1)S(1)} %slice.191), channel_id=1, source_target_pairs={{0,2},{2,0},{4,6},{6,4},{8,10},{10,8},{12,14},{14,12},{16,18},{18,... | collective-permute-start | bytes 1572872 | tf_op jit(solution)/shard_map/ppermute | solution.py:303
  181.3 44.2 %collective-permute-start.32 = (bf16[2,256,1024]{2,1,0:T(8,128)(2,1)S(1)}, bf16[2,256,1024]{2,1,0:T(8,128)(2,1)S(1)}, u32[]{:S(2)}, u32[]{:S(2)}) collective-permute-start(bf16[2,256,1024]{2,1,0:T(8,128)(2,1)S(1)} %copy-done.14), channel_id=1, source_target_pairs={{0,4},{2,6},{4,0},{6,2},{8,12},{10,14},{12,8},{14,10},{16,20},{18,... | collective-permute-start | bytes 3145736 | tf_op jit(solution)/shard_map/ppermute | solution.py:303
  193.3 31.3 %collective-permute-start.21 = (bf16[1024,256]{1,0:T(8,128)(2,1)S(1)}, bf16[1024,256]{1,0:T(8,128)(2,1)S(1)}, u32[]{:S(2)}, u32[]{:S(2)}) collective-permute-start(bf16[1024,256]{1,0:T(8,128)(2,1)S(1)} %slice.188), channel_id=1, source_target_pairs={{0,4},{2,6},{4,0},{6,2},{8,12},{10,14},{12,8},{14,10},{16,20},{18,... | collective-permute-start | bytes 1572872 | tf_op jit(solution)/shard_map/ppermute | solution.py:303
  209.4 65.7 %collective-permute-start.26 = (bf16[256,1024]{1,0:T(8,128)(2,1)}, bf16[256,1024]{1,0:T(8,128)(2,1)}, u32[]{:S(2)}, u32[]{:S(2)}) collective-permute-start(bf16[256,1024]{1,0:T(8,128)(2,1)} %fusion.9), channel_id=1, source_target_pairs={{0,4},{2,6},{4,0},{6,2},{8,12},{10,14},{12,8},{14,10},{16,20},{18,... | collective-permute-start | bytes 1572872 | tf_op jit(solution)/shard_map/ppermute | solution.py:303
  213.3 63.4 %collective-permute-start.27 = (bf16[256,1024]{1,0:T(8,128)(2,1)}, bf16[256,1024]{1,0:T(8,128)(2,1)}, u32[]{:S(2)}, u32[]{:S(2)}) collective-permute-start(bf16[256,1024]{1,0:T(8,128)(2,1)} %fusion.10), channel_id=1, source_target_pairs={{0,2},{2,0},{4,6},{6,4},{8,10},{10,8},{12,14},{14,12},{16,18},{18,... | collective-permute-start | bytes 1572872 | tf_op jit(solution)/shard_map/ppermute | solution.py:303
  225.5 53.9 %collective-permute-start.40 = (bf16[256,1024]{1,0:T(8,128)(2,1)}, bf16[256,1024]{1,0:T(8,128)(2,1)}, u32[]{:S(2)}, u32[]{:S(2)}) collective-permute-start(bf16[256,1024]{1,0:T(8,128)(2,1)} %fusion.13), channel_id=1, source_target_pairs={{0,4},{2,6},{4,0},{6,2},{8,12},{10,14},{12,8},{14,10},{16,20},{18,... | collective-permute-start | bytes 1572872 | tf_op jit(solution)/shard_map/ppermute | solution.py:303
  229.0 53.8 %collective-permute-start.41 = (bf16[256,1024]{1,0:T(8,128)(2,1)}, bf16[256,1024]{1,0:T(8,128)(2,1)}, u32[]{:S(2)}, u32[]{:S(2)}) collective-permute-start(bf16[256,1024]{1,0:T(8,128)(2,1)} %fusion.14), channel_id=1, source_target_pairs={{0,2},{2,0},{4,6},{6,4},{8,10},{10,8},{12,14},{14,12},{16,18},{18,... | collective-permute-start | bytes 1572872 | tf_op jit(solution)/shard_map/ppermute | solution.py:303
  229.0 62.3 %collective-permute-start.28 = (bf16[2,256,1024]{2,1,0:T(8,128)(2,1)S(1)}, bf16[2,256,1024]{2,1,0:T(8,128)(2,1)}, u32[]{:S(2)}, u32[]{:S(2)}) collective-permute-start(bf16[2,256,1024]{2,1,0:T(8,128)(2,1)S(1)} %get-tuple-element.94), channel_id=1, source_target_pairs={{0,2},{2,0},{4,6},{6,4},{8,10},{10,8},{12,14},{14,12},{16,18},{18,... | collective-permute-start | bytes 3145736 | tf_op jit(solution)/shard_map/ppermute | solution.py:303
  275.0 26.2 %collective-permute-start.29 = (bf16[2,256,1024]{2,1,0:T(8,128)(2,1)S(1)}, bf16[2,256,1024]{2,1,0:T(8,128)(2,1)S(1)}, u32[]{:S(2)}, u32[]{:S(2)}) collective-permute-start(bf16[2,256,1024]{2,1,0:T(8,128)(2,1)S(1)} %get-tuple-element.96), channel_id=1, source_target_pairs={{0,4},{2,6},{4,0},{6,2},{8,12},{10,14},{12,8},{14,10},{16,20},{18,... | collective-permute-start | bytes 3145736 | tf_op jit(solution)/shard_map/ppermute | solution.py:303
  276.7 54.9 %collective-permute-start.39 = (bf16[2,256,1024]{2,1,0:T(8,128)(2,1)}, bf16[2,256,1024]{2,1,0:T(8,128)(2,1)}, u32[]{:S(2)}, u32[]{:S(2)}) collective-permute-start(bf16[2,256,1024]{2,1,0:T(8,128)(2,1)} %get-tuple-element.118), channel_id=1, source_target_pairs={{0,2},{2,0},{4,6},{6,4},{8,10},{10,8},{12,14},{14,12},{16,18},{18,... | collective-permute-start | bytes 3145736 | tf_op jit(solution)/shard_map/ppermute | solution.py:303
  279.4 54.0 %collective-permute-start.42 = (bf16[2,256,1024]{2,1,0:T(8,128)(2,1)S(1)}, bf16[2,256,1024]{2,1,0:T(8,128)(2,1)}, u32[]{:S(2)}, u32[]{:S(2)}) collective-permute-start(bf16[2,256,1024]{2,1,0:T(8,128)(2,1)S(1)} %get-tuple-element.124), channel_id=1, source_target_pairs={{0,4},{2,6},{4,0},{6,2},{8,12},{10,14},{12,8},{14,10},{16,20},{18,... | collective-permute-start | bytes 3145736 | tf_op jit(solution)/shard_map/ppermute | solution.py:303
  282.8 112.7 %collective-permute-start.45 = (bf16[256,2048]{1,0:T(8,128)(2,1)}, bf16[256,2048]{1,0:T(8,128)(2,1)S(1)}, u32[]{:S(2)}, u32[]{:S(2)}) collective-permute-start(bf16[256,2048]{1,0:T(8,128)(2,1)} %pad_maximum_fusion), channel_id=1, source_target_pairs={{0,16},{2,18},{4,20},{6,22},{8,24},{10,26},{12,28},{14,30},{16,0},... | collective-permute-start | bytes 3145736 | tf_op jit(solution)/shard_map/ppermute | solution.py:400
  291.3 104.2 %collective-permute-start.46 = (bf16[256,2048]{1,0:T(8,128)(2,1)}, bf16[256,2048]{1,0:T(8,128)(2,1)S(1)}, u32[]{:S(2)}, u32[]{:S(2)}) collective-permute-start(bf16[256,2048]{1,0:T(8,128)(2,1)} %pad_maximum_fusion.1), channel_id=1, source_target_pairs={{0,24},{2,26},{4,28},{6,30},{8,0},{10,2},{12,4},{14,6},{16,8},{18,... | collective-permute-start | bytes 3145736 | tf_op jit(solution)/shard_map/ppermute | solution.py:400
  301.2 54.4 %collective-permute-start.47 = (bf16[256,1024]{1,0:T(8,128)(2,1)S(1)}, bf16[256,1024]{1,0:T(8,128)(2,1)S(1)}, u32[]{:S(2)}, u32[]{:S(2)}) collective-permute-start(bf16[256,1024]{1,0:T(8,128)(2,1)S(1)} %fusion.16), channel_id=1, source_target_pairs={{0,4},{2,6},{4,0},{6,2},{8,12},{10,14},{12,8},{14,10},{16,20},{18,... | collective-permute-start | bytes 1572872 | tf_op jit(solution)/shard_map/ppermute | solution.py:303
  (47 other events, 672.3 us)
Sparse Core Ops, SparseCore 0:
  9.6 22.5 all-gather.1
where the time goes:
time: 411 us; the launch traced here: 405 us
  waiting for transfers between devices  147 us (36%)
  Pallas kernels  111 us (27%)
  starting transfers between devices  68.5 us (17%)
  local copies, waits for them, and re-layouts  31.3 us (8%)
  other arithmetic  31.3 us (8%)
  between operations  15.1 us (4%)
    pallas_call x2, Pallas kernels, run_product(): pl.pallas_call(lambda *refs: product_kernel(count, *refs), grid_spec=pltp...  64.1 us
    ppermute x32, waiting for transfers between devices, send(): lax.ppermute(after(array, *self.arrived[-2], *self.ready, *earlier), 'ctx...  61.4 us
    ppermute x32, starting transfers between devices, send(): lax.ppermute(after(array, *self.arrived[-2], *self.ready, *earlier), 'ctx...  33.4 us
    pallas_call x4, Pallas kernels, run_weight(): pl.pallas_call(weight_kernel, grid_spec=pltpu.PrefetchScalarGridSpec(num_...  31.1 us
    ppermute x3, waiting for transfers between devices, on_device(): lax.ppermute(after(own, *shards[1:][-1:]), 'ctx', at.pairs_z(by))  25.3 us
    ppermute x1, waiting for transfers between devices, gather_filters(): from_y = lax.ppermute(pair, 'ctx', at.pairs_y)  20.9 us
    unnamed x64, local copies, waits for them, and re-layouts  17.5 us
    ppermute x1, waiting for transfers between devices, reduce_filters(): lax.ppermute(pick(1 - at.x, part, 2), 'ctx', at.pairs_x)  17 us
  transfers between devices with their start and end apart: 51, of which 14 were waited for; matrix products, arithmetic and copies ran while one was open for 12% of the time, Pallas kernels for 27%

commit v1 on v0

--- a/solution.py
+++ b/solution.py
@@ -11,7 +11,7 @@
 
 F32 = jnp.float32
 BF16 = jnp.bfloat16
-MIB = 1024 * 1024
+VMEM = 58 * 1024 * 1024
 PARTS = 2
 
 
@@ -97,7 +97,7 @@
         in_specs=[rows(taps), rows(seq_len), rows(taps), rows(seq_len), whole(forward), whole(backward)],
         out_specs=[rows(seq_len), rows(seq_len)],
         out_shape=[jax.ShapeDtypeStruct((chan, seq_len), BF16)] * 2,
-        compiler_params=pltpu.CompilerParams(vmem_limit_bytes=32 * MIB),
+        compiler_params=pltpu.CompilerParams(vmem_limit_bytes=VMEM),
         cost_estimate=pl.CostEstimate(
             flops=14 * chan * seq_len * 2 * taps, bytes_accessed=8 * chan * seq_len, transcendentals=0
         ),
@@ -136,7 +136,7 @@
             out_specs=[out_spec] * 4,
         ),
         out_shape=[jax.ShapeDtypeStruct((2, rows, chan // 2), BF16)] * 4,
-        compiler_params=pltpu.CompilerParams(vmem_limit_bytes=48 * MIB),
+        compiler_params=pltpu.CompilerParams(vmem_limit_bytes=VMEM),
         cost_estimate=pl.CostEstimate(
             flops=8 * rows * chan * seq_len,
             bytes_accessed=2 * (4 * rows * (seq_len + chan) + chan * seq_len),
@@ -251,9 +251,9 @@
             jax.ShapeDtypeStruct((chan, taps), F32),
         ],
         input_output_aliases={9 + count + k: k for k in range(len(written))},
-        compiler_params=pltpu.CompilerParams(vmem_limit_bytes=50 * MIB),
+        compiler_params=pltpu.CompilerParams(vmem_limit_bytes=VMEM),
         cost_estimate=pl.CostEstimate(
-            flops=group * steps * seq_len * (2 * depth + 32 * taps),
+            flops=2 * group * steps * seq_len * (depth + 16 * taps),
             bytes_accessed=2 * depth * (seq_len + group * steps) + 12 * group * steps * seq_len,
             transcendentals=0,
         ),
@@ -288,6 +288,7 @@
         self.arrived = [()] * 3
         self.now = []
         self.ready = self.next_ready = ()
+        self.back = 2
 
     def advance(self):
         self.arrived.append(tuple(self.now))
@@ -300,7 +301,7 @@
         self.next_ready += arrays
 
     def send(self, array, pairs, *earlier):
-        got = lax.ppermute(after(array, *self.arrived[-2], *self.ready, *earlier), "ctx", pairs)
+        got = lax.ppermute(after(array, *self.arrived[-self.back], *self.ready, *earlier), "ctx", pairs)
         self.now.append(got)
         return got
 
@@ -316,18 +317,8 @@
     return jnp.where(bit == 0, halves[0], halves[1])
 
 
-def gather_filters(at, own):
-    def ordered(bit, mine, other):
-        return jnp.stack([jnp.where(bit == 0, mine, other), jnp.where(bit == 0, other, mine)], axis=1)
-
-    slots = [lax.ppermute(own, "ctx", at.pairs_z(by)) for by in range(at.depth - 1, 0, -1)]
-    ring = jnp.stack((slots + [own]) * 2)
-    column = lax.dynamic_slice_in_dim(ring, at.depth - 1 - at.z, at.depth, axis=0)
-    from_x = lax.ppermute(column, "ctx", at.pairs_x)
-    pair = ordered(at.x, column, from_x)
-    from_y = lax.ppermute(pair, "ctx", at.pairs_y)
-    whole = ordered(at.y, pair, from_y).reshape((at.count * own.shape[0],) + own.shape[1:])
-    return whole, from_x, from_y
+def ordered(bit, mine, other):
+    return jnp.stack([jnp.where(bit == 0, mine, other), jnp.where(bit == 0, other, mine)])
 
 
 def reduce_filters(at, part, chan_count):
@@ -355,23 +346,35 @@
     to_left = [(i + 1, i) for i in range(at.count - 1)]
     forward, backward = (jnp.asarray(m) for m in dft_matrices(taps))
 
-    prior = lax.ppermute(kv_product[:, seq_len - taps :], "ctx", to_right)
-    all_filters, first_x, first_y = gather_filters(at, filters.reshape(chan_count, taps))
     grad_full = lax.all_gather(out_grad, "fsdp", axis=0, tiled=True)
 
     near = sorted(range(at.depth), key=lambda d: min(d, at.depth - d))
     far = near[::-1]
-    own = w_out.T
+    own, own_filters = w_out.T, filters.reshape(chan_count, taps)
+    filters_x = lax.ppermute(own_filters, "ctx", at.pairs_x)
+    pair = ordered(at.x, own_filters, filters_x)
+    filters_y = lax.ppermute(pair, "ctx", at.pairs_y)
+    plane = ordered(at.y, pair, filters_y)
     shards = [own]
-    for by in near[1:]:
-        shards.append(lax.ppermute(after(own, *shards[1:][-1:]), "ctx", at.pairs_z(by)))
+    for by in near[1:2]:
+        shards.append(lax.ppermute(after(own, filters_y), "ctx", at.pairs_z(by)))
+    ring = [
+        lax.ppermute(after(plane, *shards[1:]), "ctx", at.pairs_z(by)) for by in range(at.depth - 1, 0, -1)
+    ]
+    for by in near[2:]:
+        shards.append(lax.ppermute(after(own, *(ring if len(shards) == 2 else shards[-1:])), "ctx", at.pairs_z(by)))
+    ring = jnp.stack((ring + [plane]) * 2)
+    ring = lax.dynamic_slice_in_dim(ring, at.depth - 1 - at.z, at.depth, axis=0)
+    all_filters = ring.reshape(chan, taps)
+    prior = lax.ppermute(after(kv_product[:, seq_len - taps :], shards[1]), "ctx", to_right)
+
     from_x, from_y, diag_a, diag_b = {}, {}, {}, {}
     kept, summed = {}, {}
 
     def gather_first(k):
-        earlier = {1: (from_x.get(0), from_y.get(0)), 2: (first_x,), 3: (first_y,)}.get(k, ())
-        from_x[k] = stages.swap_x(shards[k], *earlier)
-        from_y[k] = stages.swap_y(shards[k], *earlier)
+        both = (from_x[0], from_y[0]) if k == 1 else ()
+        from_x[k] = stages.swap_x(shards[k], *(both if k else (filters_x,)))
+        from_y[k] = stages.swap_y(shards[k], *(both if k else (filters_y,)))
 
     def gather_second(k):
         diag_a[k] = stages.swap_x(from_y[k][:half])
@@ -380,6 +383,7 @@
     def weight_part(k):
         place = jnp.stack(at.places(far[k])).astype(jnp.int32)
         kept[k] = run_weight(place, grad_full, stages.hold(gated), rows)
+        stages.finished(kept[k][0])
 
     def reduce_first(k):
         send_a, keep_a, send_b, keep_b = kept[k]
@@ -398,12 +402,15 @@
         joint = jnp.concatenate([sum_a, sum_b], axis=1)
         by = far[k]
         summed[k] = joint if by == 0 else lax.ppermute(joint.astype(BF16), "ctx", at.pairs_z(by))
+        if k + 2 < depth:
+            stages.finished(summed[k])
 
     mixed = gated = place = products = None
 
     def mix():
         nonlocal mixed, gated
         mixed, gated = run_mix(all_filters, stages.hold(kv_product), prior, gate_values, forward, backward)
+        stages.finished(mixed)
 
     def product(part):
         nonlocal products
@@ -414,25 +421,27 @@
             part, places, grad_full, pieces, stages.hold(mixed), gate_values, kv_product, prior,
             all_filters, forward, backward, products or (),
         )
-        stages.finished(products[3])
+        stages.finished(*products[3:4])
 
     depth = at.depth
     plan = {}
     for k in range(depth):
         plan.setdefault(k, []).append((gather_first, k))
         plan.setdefault(k + 2, []).append((gather_second, k))
-        plan.setdefault(k + depth, []).append((reduce_first, k))
-        plan.setdefault(k + depth + 2, []).append((reduce_second, k))
-    for stage in range(max(2 * depth + 4, depth + 3 + PARTS)):
+        plan.setdefault(depth + [0, 1, 2, 2][min(k, 3)] + max(0, k - 3), []).append((reduce_first, k))
+        plan.setdefault(depth + [2, 3, 4, 5][min(k, 3)] + max(0, k - 3), []).append((reduce_second, k))
+    for stage in range(2 * depth + 4 + 0):
+        if stage >= 2 * depth:
+            stages.back = 1
         if stage == 2:
             mix()
         for k in range(depth):
-            if stage == max(3, k + depth - 1 + 0):
+            if stage == (2, 3, 4, 5)[min(k, 3)] + max(0, k - 3):
                 weight_part(k)
-            if stage == k + depth + 4:
+            if stage == k + depth + 3:
                 reduce_third(k)
         for part in range(PARTS):
-            if stage == depth + 3 + part:
+            if stage == depth + [2, 3][part]:
                 product(part)
         for action, k in plan.get(stage, []):
             action(k)

time: 411 us -> 398 us (0.968); the launches traced: 405 us -> 397 us
  starting transfers between devices: 68.5 us -> 107 us
  waiting for transfers between devices: 147 us -> 125 us
  local copies, waits for them, and re-layouts: 31.3 us -> 12.7 us
  other arithmetic: 31.3 us -> 26.4 us
    ppermute x3, waiting for transfers between devices: 0.01 us -> 22 us  [reduce_third(): lax.ppermute(joint.astype(BF16), 'ctx', at.pairs_z(by))]
    ppermute x3, starting transfers between devices: 13.3 us -> 31.7 us  [reduce_third(): lax.ppermute(joint.astype(BF16), 'ctx', at.pairs_z(by))]
    ppermute x41, starting transfers between devices: 47.4 us -> 63.7 us  [the longest x32 49.6 us: send(): lax.ppermute(after(array, *self.arrived[-self.back], *self.ready, *earlie...]
    unnamed x64 -> x61, local copies, waits for them, and re-layouts: 17.5 us -> 2.54 us
    ppermute x41, waiting for transfers between devices: 111 us -> 97.5 us  [the longest x32 45.8 us: send(): lax.ppermute(after(array, *self.arrived[-self.back], *self.ready, *earlie...]
    ppermute x1, waiting for transfers between devices: 17 us -> 4.66 us  [reduce_filters(): lax.ppermute(pick(1 - at.x, part, 2), 'ctx', at.pairs_x)]
    ppermute x3, waiting for transfers between devices: 12.1 us -> 0.01 us  [reduce_filters(): total = total + lax.ppermute(at_z(by), 'ctx', at.pairs_z(by))]
    ppermute x1, waiting for transfers between devices: 6 us -> 0.01 us  [reduce_filters(): lax.ppermute(pick(1 - at.y, part, 1), 'ctx', at.pairs_y)]
  transfers between devices with their start and end apart: 51 -> 51, of which waited for: 14 -> 16; matrix products, arithmetic and copies ran while one was open for 12% -> 9% of each run, Pallas kernels for 27% -> 28%
where the time goes in v1:
time: 398 us; the launch traced here: 397 us
  waiting for transfers between devices  125 us (31%)
  Pallas kernels  112 us (28%)
  starting transfers between devices  107 us (27%)
  other arithmetic  26.4 us (7%)
  between operations  14.7 us (4%)
  local copies, waits for them, and re-layouts  12.7 us (3%)
    pallas_call x2, Pallas kernels, run_product(): pl.pallas_call(lambda *refs: product_kernel(count, *refs), grid_spec=pltp...  58.5 us
    ppermute x32, starting transfers between devices, send(): lax.ppermute(after(array, *self.arrived[-self.back], *self.ready, *earlie...  49.6 us
    ppermute x32, waiting for transfers between devices, send(): lax.ppermute(after(array, *self.arrived[-self.back], *self.ready, *earlie...  45.8 us
    pallas_call x4, Pallas kernels, run_weight(): pl.pallas_call(weight_kernel, grid_spec=pltpu.PrefetchScalarGridSpec(num_...  34.6 us
    ppermute x3, starting transfers between devices, reduce_third(): lax.ppermute(joint.astype(BF16), 'ctx', at.pairs_z(by))  31.7 us
    ppermute x3, waiting for transfers between devices, reduce_third(): lax.ppermute(joint.astype(BF16), 'ctx', at.pairs_z(by))  22 us
    ppermute x2, waiting for transfers between devices, on_device(): lax.ppermute(after(own, *(ring if len(shards) == 2 else shards[-1:])), 'c...  21.9 us
    ppermute x1, waiting for transfers between devices, on_device(): shards.append(lax.ppermute(after(own, filters_y), 'ctx', at.pairs_z(by)))  19.3 us
  transfers between devices with their start and end apart: 51, of which 16 were waited for; matrix products, arithmetic and copies ran while one was open for 9% of the time, Pallas kernels for 28%

profile of v1, /device:TPU:0, one launch (start us, length us, event | category | flops | bytes accessed | tf_op | source)
XLA Modules:
  0.0 397.3 jit_solution(10007960075808496581)
XLA Ops:
  7.9 3.0 collective-permute-start
  12.9 2.1 collective-permute-start.2
  23.0 19.3 %collective-permute-done.5.refs_6_ = bf16[2048,256]{1,0:T(8,128)(2,1)} collective-permute-done((bf16[2048,256]{1,0:T(8,128)(2,1)S(1)}, bf16[2048,256]{1,0:T(8,128)(2,1)}, u32[]{:S(2)}, u32[]{:S(2)}) %collective-permute-start.5) | collective-permute-done | bytes 1048608 | tf_op jit(solution)/shard_map/ppermute | solution.py:360
  42.3 2.7 collective-permute-start.9
  53.6 2.5 collective-permute-start.11
  60.8 20.2 %collective-permute-done.13.refs_10_ = bf16[2048,256]{1,0:T(8,128)(2,1)} collective-permute-done((bf16[2048,256]{1,0:T(8,128)(2,1)S(1)}, bf16[2048,256]{1,0:T(8,128)(2,1)}, u32[]{:S(2)}, u32[]{:S(2)}) %collective-permute-start.13) | collective-permute-done | bytes 1048608 | tf_op jit(solution)/shard_map/ppermute | solution.py:365
  81.0 6.9 %collective-permute-done.11.prior_ref.refs_21_ = bf16[2048,128]{1,0:T(8,128)(2,1)S(1)} collective-permute-done((bf16[2048,128]{1,0:T(8,128)(2,1)S(1)}, bf16[2048,128]{1,0:T(8,128)(2,1)S(1)}, u32[]{:S(2)}, u32[]{:S(2)}) %collective-permute-start.11) | collective-permute-done | bytes 524320 | tf_op jit(solution)/shard_map/ppermute | solution.py:369
  87.9 4.4 %collective-permute-start.15 = (bf16[2048,256]{1,0:T(8,128)(2,1)}, bf16[2048,256]{1,0:T(8,128)(2,1)S(1)}, u32[]{:S(2)}, u32[]{:S(2)}) collective-permute-start(bf16[2048,256]{1,0:T(8,128)(2,1)} %collective-permute-done.13.refs_10_), channel_id=1, source_target_pairs={{0,4},{2,6},{4,0},{6,2},{8,12},{10,14},{12,8},{14,10},{16,20},{18,... | collective-permute-start | bytes 3145736 | tf_op jit(solution)/shard_map/ppermute | solution.py:304
  92.3 18.8 %mix_kernel.1 = (bf16[2048,1024]{1,0:T(8,128)(2,1)}, bf16[2048,1024]{1,0:T(8,128)(2,1)}) custom-call(bf16[2048,128]{1,0:T(8,128)(2,1)} %bitcast.157, bf16[2048,1024]{1,0:T(8,128)(2,1)} %refs_20_.3, bf16[2048,128]{1,0:T(8,128)(2,1)} %copy-done.18, bf16[2048,1024]{1,0:T(8,128)(2,1)} %refs_19_.3, bf16[256,256]{1,0:T(8,128)(2,1)} %constant.124.clone.forward_ref.refs_23_, ...), custom_call_target="tpu_custom_call" | custom-call | flops 7516192768 | bytes 16777216 | tf_op jit(solution)/shard_map/mix_kernel/pallas_call | solution.py:94
  112.9 8.6 %weight_kernel.4 = (bf16[2,256,1024]{2,1,0:T(8,128)(2,1)}, bf16[2,256,1024]{2,1,0:T(8,128)(2,1)}, bf16[2,256,1024]{2,1,0:T(8,128)(2,1)}, bf16[2,256,1024]{2,1,0:T(8,128)(2,1)}) custom-call(s32[4]{0:T(128)} %get-tuple-element.147.place_ref, bf16[4096,1024]{1,0:T(8,128)(2,1)} %all-gather.2.cloned.1.call-done.g00.g01.g10.g11.refs_1_, ...), custom_call_target="tpu_custom_call" | custom-call | flops 4294967296 | bytes 10485760 | tf_op jit(solution)/shard_map/weight_kernel/pallas_call | solution.py:130
  126.3 6.0 %collective-permute-start.19 = (bf16[2048,256]{1,0:T(8,128)(2,1)}, bf16[2048,256]{1,0:T(8,128)(2,1)}, u32[]{:S(2)}, u32[]{:S(2)}) collective-permute-start(bf16[2048,256]{1,0:T(8,128)(2,1)} %collective-permute-done.18.refs_14_), channel_id=1, source_target_pairs={{0,2},{2,0},{4,6},{6,4},{8,10},{10,8},{12,14},{14,12},{16,18},{18,... | collective-permute-start | bytes 3145736 | tf_op jit(solution)/shard_map/ppermute | solution.py:304
  134.3 8.6 %weight_kernel.5 = (bf16[2,256,1024]{2,1,0:T(8,128)(2,1)}, bf16[2,256,1024]{2,1,0:T(8,128)(2,1)}, bf16[2,256,1024]{2,1,0:T(8,128)(2,1)}, bf16[2,256,1024]{2,1,0:T(8,128)(2,1)}) custom-call(s32[4]{0:T(128)} %get-tuple-element.148.place_ref, bf16[4096,1024]{1,0:T(8,128)(2,1)} %all-gather.2.cloned.1.call-done.g00.g01.g10.g11.refs_1_, ...), custom_call_target="tpu_custom_call" | custom-call | flops 4294967296 | bytes 10485760 | tf_op jit(solution)/shard_map/weight_kernel/pallas_call | solution.py:130
  145.0 13.8 %collective-permute-done.12.refs_9_ = bf16[1024,256]{1,0:T(8,128)(2,1)} collective-permute-done((bf16[1024,256]{1,0:T(8,128)(2,1)S(1)}, bf16[1024,256]{1,0:T(8,128)(2,1)}, u32[]{:S(2)}, u32[]{:S(2)}) %collective-permute-start.12) | collective-permute-done | bytes 524320 | tf_op jit(solution)/shard_map/ppermute | solution.py:304
  160.8 7.1 %collective-permute-done.21.refs_9_ = bf16[1024,256]{1,0:T(8,128)(2,1)} collective-permute-done((bf16[1024,256]{1,0:T(8,128)(2,1)}, bf16[1024,256]{1,0:T(8,128)(2,1)}, u32[]{:S(2)}, u32[]{:S(2)}) %collective-permute-start.21) | collective-permute-done | bytes 524320 | tf_op jit(solution)/shard_map/ppermute | solution.py:304
  171.9 8.6 %weight_kernel.6 = (bf16[2,256,1024]{2,1,0:T(8,128)(2,1)}, bf16[2,256,1024]{2,1,0:T(8,128)(2,1)}, bf16[2,256,1024]{2,1,0:T(8,128)(2,1)}, bf16[2,256,1024]{2,1,0:T(8,128)(2,1)}) custom-call(s32[4]{0:T(128)} %get-tuple-element.149.place_ref, bf16[4096,1024]{1,0:T(8,128)(2,1)} %all-gather.2.cloned.1.call-done.g00.g01.g10.g11.refs_1_, ...), custom_call_target="tpu_custom_call" | custom-call | flops 4294967296 | bytes 10485760 | tf_op jit(solution)/shard_map/weight_kernel/pallas_call | solution.py:130
  182.6 8.7 %weight_kernel.7 = (bf16[2,256,1024]{2,1,0:T(8,128)(2,1)}, bf16[2,256,1024]{2,1,0:T(8,128)(2,1)}, bf16[2,256,1024]{2,1,0:T(8,128)(2,1)}, bf16[2,256,1024]{2,1,0:T(8,128)(2,1)}) custom-call(s32[4]{0:T(128)} %get-tuple-element.150.place_ref, bf16[4096,1024]{1,0:T(8,128)(2,1)} %all-gather.2.cloned.1.call-done.g00.g01.g10.g11.refs_1_, ...), custom_call_target="tpu_custom_call" | custom-call | flops 4294967296 | bytes 10485760 | tf_op jit(solution)/shard_map/weight_kernel/pallas_call | solution.py:130
  191.4 5.0 %collective-permute-done.17.refs_13_ = bf16[1024,256]{1,0:T(8,128)(2,1)S(1)} collective-permute-done((bf16[1024,256]{1,0:T(8,128)(2,1)S(1)}, bf16[1024,256]{1,0:T(8,128)(2,1)S(1)}, u32[]{:S(2)}, u32[]{:S(2)}) %collective-permute-start.17) | collective-permute-done | bytes 524320 | tf_op jit(solution)/shard_map/ppermute | solution.py:304
  196.3 5.4 %collective-permute-start.25 = (bf16[1024,256]{1,0:T(8,128)(2,1)S(1)}, bf16[1024,256]{1,0:T(8,128)(2,1)S(1)}, u32[]{:S(2)}, u32[]{:S(2)}) collective-permute-start(bf16[1024,256]{1,0:T(8,128)(2,1)S(1)} %slice.190), channel_id=1, source_target_pairs={{0,2},{2,0},{4,6},{6,4},{8,10},{10,8},{12,14},{14,12},{16,18},{18,... | collective-permute-start | bytes 1572872 | tf_op jit(solution)/shard_map/ppermute | solution.py:304
  208.2 6.4 %collective-permute-done.25.refs_17_ = bf16[1024,256]{1,0:T(8,128)(2,1)S(1)} collective-permute-done((bf16[1024,256]{1,0:T(8,128)(2,1)S(1)}, bf16[1024,256]{1,0:T(8,128)(2,1)S(1)}, u32[]{:S(2)}, u32[]{:S(2)}) %collective-permute-start.25) | collective-permute-done | bytes 524320 | tf_op jit(solution)/shard_map/ppermute | solution.py:304
  216.3 29.1 %product_kernel.2 = (f32[2048,1024]{1,0:T(8,128)}, bf16[2048,1024]{1,0:T(8,128)(2,1)}, f32[2048,128]{1,0:T(8,128)}, bf16[2048,128]{1,0:T(8,128)(2,1)}, f32[2048,128]{1,0:T(8,128)}) custom-call(s32[16]{0:T(128)} %stack.173.refs_0_, bf16[4096,1024]{1,0:T(8,128)(2,1)} %all-gather.2.cloned.1.call-done.g00.g01.g10.g11.refs_1_, bf16[2048,256]{1,0:T(8,128)(2,1)} %bitcast.155, ...), custom_call_target="tpu_custom_call" | custom-call | flops 12884901888 | bytes 29360128 | tf_op jit(solution)/shard_map/product_kernel/pallas_call | solution.py:229
  253.6 22.8 %collective-permute-start.41 = (bf16[256,2048]{1,0:T(8,128)(2,1)}, bf16[256,2048]{1,0:T(8,128)(2,1)S(1)}, u32[]{:S(2)}, u32[]{:S(2)}) collective-permute-start(bf16[256,2048]{1,0:T(8,128)(2,1)} %pad_maximum_fusion), channel_id=1, source_target_pairs={{0,16},{2,18},{4,20},{6,22},{8,24},{10,26},{12,28},{14,30},{16,0},... | collective-permute-start | bytes 3145736 | tf_op jit(solution)/shard_map/ppermute | solution.py:404
  280.5 29.3 %product_kernel.3 = (f32[2048,1024]{1,0:T(8,128)}, bf16[2048,1024]{1,0:T(8,128)(2,1)}, f32[2048,128]{1,0:T(8,128)}, bf16[2048,128]{1,0:T(8,128)(2,1)}, f32[2048,128]{1,0:T(8,128)}) custom-call(s32[16]{0:T(128)} %stack.173.refs_0_, ...), custom_call_target="tpu_custom_call", output_to_operand_aliasing={{0}: (25, {}), {1}: (26, {}), {2}: (27, {}), {3}: (28, {}),... | custom-call | flops 12884901888 | bytes 29360128 | tf_op jit(solution)/shard_map/product_kernel/pallas_call | solution.py:229
  315.9 2.7 collective-permute-start.37
  320.8 4.7 %collective-permute-done.30 = f32[4,2,128,128]{3,2,1,0:T(8,128)S(1)} collective-permute-done((f32[4,2,128,128]{3,2,1,0:T(8,128)S(1)}, f32[4,2,128,128]{3,2,1,0:T(8,128)S(1)}, u32[]{:S(2)}, u32[]{:S(2)}) %collective-permute-start.30) | collective-permute-done | bytes 524320 | tf_op jit(solution)/shard_map/ppermute | solution.py:327
  325.7 6.1 %collective-permute-done.38 = bf16[256,1024]{1,0:T(8,128)(2,1)S(1)} collective-permute-done((bf16[256,1024]{1,0:T(8,128)(2,1)S(1)}, bf16[256,1024]{1,0:T(8,128)(2,1)S(1)}, u32[]{:S(2)}, u32[]{:S(2)}) %collective-permute-start.38) | collective-permute-done | bytes 524320 | tf_op jit(solution)/shard_map/ppermute | solution.py:304
  336.7 6.0 %collective-permute-start.45 = (bf16[256,2048]{1,0:T(8,128)(2,1)S(1)}, bf16[256,2048]{1,0:T(8,128)(2,1)S(1)}, u32[]{:S(2)}, u32[]{:S(2)}) collective-permute-start(bf16[256,2048]{1,0:T(8,128)(2,1)S(1)} %pad_maximum_fusion.1), channel_id=1, source_target_pairs={{0,24},{2,26},{4,28},{6,30},{8,0},{10,2},{12,4},{14,6},{16,8},{18,... | collective-permute-start | bytes 3145736 | tf_op jit(solution)/shard_map/ppermute | solution.py:404
  342.8 5.0 %collective-permute-start.32 = (f32[128,128]{1,0:T(8,128)S(1)}, f32[128,128]{1,0:T(8,128)S(1)}, u32[]{:S(2)}, u32[]{:S(2)}) collective-permute-start(f32[128,128]{1,0:T(8,128)S(1)} %get-tuple-element.140), channel_id=1, source_target_pairs={{0,8},{2,10},{4,12},{6,14},{8,16},{10,18},{12,20},{14,22},{16,24},... | collective-permute-start | bytes 196616 | tf_op jit(solution)/shard_map/ppermute | solution.py:332
  349.1 3.5 collective-permute-start.33
  354.1 17.9 %collective-permute-done.45 = bf16[256,2048]{1,0:T(8,128)(2,1)S(1)} collective-permute-done((bf16[256,2048]{1,0:T(8,128)(2,1)S(1)}, bf16[256,2048]{1,0:T(8,128)(2,1)S(1)}, u32[]{:S(2)}, u32[]{:S(2)}) %collective-permute-start.45) | collective-permute-done | bytes 1048608 | tf_op jit(solution)/shard_map/ppermute | solution.py:404
  372.0 2.9 collective-permute-start.49
  376.7 7.3 %collective-permute-done.46 = bf16[256,1024]{1,0:T(8,128)(2,1)S(1)} collective-permute-done((bf16[256,1024]{1,0:T(8,128)(2,1)S(1)}, bf16[256,1024]{1,0:T(8,128)(2,1)S(1)}, u32[]{:S(2)}, u32[]{:S(2)}) %collective-permute-start.46) | collective-permute-done | bytes 524320 | tf_op jit(solution)/shard_map/ppermute | solution.py:304
  384.6 4.0 %collective-permute-done.49 = bf16[256,2048]{1,0:T(8,128)(2,1)S(1)} collective-permute-done((bf16[256,2048]{1,0:T(8,128)(2,1)S(1)}, bf16[256,2048]{1,0:T(8,128)(2,1)S(1)}, u32[]{:S(2)}, u32[]{:S(2)}) %collective-permute-start.49) | collective-permute-done | bytes 1048608 | tf_op jit(solution)/shard_map/ppermute | solution.py:404
  (185 shorter events, 83.3 us)
Async XLA Ops:
  7.2 105.7 %all-gather.2.cloned.1.call-start = ((), (), s32[]{:S(2)}) async-start(), calls=%async_computation | async-start | bytes 12582912 | tf_op jit(solution)/shard_map/all_gather | solution.py:349
  19.3 29.6 %collective-permute-start.1 = (bf16[2048,256]{1,0:T(8,128)(2,1)S(1)}, bf16[2048,256]{1,0:T(8,128)(2,1)S(1)}, u32[]{:S(2)}, u32[]{:S(2)}) collective-permute-start(bf16[2048,256]{1,0:T(8,128)(2,1)S(1)} %bitcast.151), channel_id=1, source_target_pairs={{0,2},{2,0},{4,6},{6,4},{8,10},{10,8},{12,14},{14,12},{16,18},{18,... | collective-permute-start | bytes 3145736 | tf_op jit(solution)/shard_map/ppermute | solution.py:304
  20.8 29.0 %collective-permute-start.3 = (bf16[2048,256]{1,0:T(8,128)(2,1)S(1)}, bf16[2048,256]{1,0:T(8,128)(2,1)S(1)}, u32[]{:S(2)}, u32[]{:S(2)}) collective-permute-start(bf16[2048,256]{1,0:T(8,128)(2,1)S(1)} %bitcast.152), channel_id=1, source_target_pairs={{0,4},{2,6},{4,0},{6,2},{8,12},{10,14},{12,8},{14,10},{16,20},{18,... | collective-permute-start | bytes 3145736 | tf_op jit(solution)/shard_map/ppermute | solution.py:304
  49.8 61.3 %collective-permute-start.7 = (bf16[2048,256]{1,0:T(8,128)(2,1)}, bf16[2048,256]{1,0:T(8,128)(2,1)}, u32[]{:S(2)}, u32[]{:S(2)}) collective-permute-start(bf16[2048,256]{1,0:T(8,128)(2,1)} %collective-permute-done.5.refs_6_), channel_id=1, source_target_pairs={{0,4},{2,6},{4,0},{6,2},{8,12},{10,14},{12,8},{14,10},{16,20},{18,... | collective-permute-start | bytes 3145736 | tf_op jit(solution)/shard_map/ppermute | solution.py:304
  51.3 60.4 %collective-permute-start.6 = (bf16[2048,256]{1,0:T(8,128)(2,1)}, bf16[2048,256]{1,0:T(8,128)(2,1)}, u32[]{:S(2)}, u32[]{:S(2)}) collective-permute-start(bf16[2048,256]{1,0:T(8,128)(2,1)} %collective-permute-done.5.refs_6_), channel_id=1, source_target_pairs={{0,2},{2,0},{4,6},{6,4},{8,10},{10,8},{12,14},{14,12},{16,18},{18,... | collective-permute-start | bytes 3145736 | tf_op jit(solution)/shard_map/ppermute | solution.py:304
  53.6 34.2 %collective-permute-start.11 = (bf16[2048,128]{1,0:T(8,128)(2,1)S(1)}, bf16[2048,128]{1,0:T(8,128)(2,1)S(1)}, u32[]{:S(2)}, u32[]{:S(2)}) collective-permute-start(bf16[2048,128]{1,0:T(8,128)(2,1)S(1)} %copy-done.24), channel_id=1, source_target_pairs={{0,2},{2,4},{4,6},{6,8},{8,10},{10,12},{12,14},{14,16},{16,18},{18... | collective-permute-start | bytes 1572872 | tf_op jit(solution)/shard_map/ppermute | solution.py:369
  56.1 70.1 %collective-permute-start.16 = (bf16[1024,256]{1,0:T(8,128)(2,1)}, bf16[1024,256]{1,0:T(8,128)(2,1)}, u32[]{:S(2)}, u32[]{:S(2)}) collective-permute-start(bf16[1024,256]{1,0:T(8,128)(2,1)} %slice.187), channel_id=1, source_target_pairs={{0,2},{2,0},{4,6},{6,4},{8,10},{10,8},{12,14},{14,12},{16,18},{18,... | collective-permute-start | bytes 1572872 | tf_op jit(solution)/shard_map/ppermute | solution.py:304
  81.0 42.1 %collective-permute-start.18 = (bf16[2048,256]{1,0:T(8,128)(2,1)S(1)}, bf16[2048,256]{1,0:T(8,128)(2,1)}, u32[]{:S(2)}, u32[]{:S(2)}) collective-permute-start(bf16[2048,256]{1,0:T(8,128)(2,1)S(1)} %bitcast.154), channel_id=1, source_target_pairs={{0,16},{2,18},{4,20},{6,22},{8,24},{10,26},{12,28},{14,30},{16,0},... | collective-permute-start | bytes 3145736 | tf_op jit(solution)/shard_map/ppermute | solution.py:365
  87.9 46.4 %collective-permute-start.15 = (bf16[2048,256]{1,0:T(8,128)(2,1)}, bf16[2048,256]{1,0:T(8,128)(2,1)S(1)}, u32[]{:S(2)}, u32[]{:S(2)}) collective-permute-start(bf16[2048,256]{1,0:T(8,128)(2,1)} %collective-permute-done.13.refs_10_), channel_id=1, source_target_pairs={{0,4},{2,6},{4,0},{6,2},{8,12},{10,14},{12,8},{14,10},{16,20},{18,... | collective-permute-start | bytes 3145736 | tf_op jit(solution)/shard_map/ppermute | solution.py:304
  111.7 31.2 %collective-permute-start.14 = (bf16[2048,256]{1,0:T(8,128)(2,1)}, bf16[2048,256]{1,0:T(8,128)(2,1)S(1)}, u32[]{:S(2)}, u32[]{:S(2)}) collective-permute-start(bf16[2048,256]{1,0:T(8,128)(2,1)} %collective-permute-done.13.refs_10_), channel_id=1, source_target_pairs={{0,2},{2,0},{4,6},{6,4},{8,10},{10,8},{12,14},{14,12},{16,18},{18,... | collective-permute-start | bytes 3145736 | tf_op jit(solution)/shard_map/ppermute | solution.py:304
  123.1 46.8 %collective-permute-start.20 = (bf16[2048,256]{1,0:T(8,128)(2,1)}, bf16[2048,256]{1,0:T(8,128)(2,1)S(1)}, u32[]{:S(2)}, u32[]{:S(2)}) collective-permute-start(bf16[2048,256]{1,0:T(8,128)(2,1)} %collective-permute-done.18.refs_14_), channel_id=1, source_target_pairs={{0,4},{2,6},{4,0},{6,2},{8,12},{10,14},{12,8},{14,10},{16,20},{18,... | collective-permute-start | bytes 3145736 | tf_op jit(solution)/shard_map/ppermute | solution.py:304
  126.3 32.5 %collective-permute-start.12 = (bf16[1024,256]{1,0:T(8,128)(2,1)S(1)}, bf16[1024,256]{1,0:T(8,128)(2,1)}, u32[]{:S(2)}, u32[]{:S(2)}) collective-permute-start(bf16[1024,256]{1,0:T(8,128)(2,1)S(1)} %slice.185), channel_id=1, source_target_pairs={{0,4},{2,6},{4,0},{6,2},{8,12},{10,14},{12,8},{14,10},{16,20},{18,... | collective-permute-start | bytes 1572872 | tf_op jit(solution)/shard_map/ppermute | solution.py:304
  126.3 54.2 %collective-permute-start.19 = (bf16[2048,256]{1,0:T(8,128)(2,1)}, bf16[2048,256]{1,0:T(8,128)(2,1)}, u32[]{:S(2)}, u32[]{:S(2)}) collective-permute-start(bf16[2048,256]{1,0:T(8,128)(2,1)} %collective-permute-done.18.refs_14_), channel_id=1, source_target_pairs={{0,2},{2,0},{4,6},{6,4},{8,10},{10,8},{12,14},{14,12},{16,18},{18,... | collective-permute-start | bytes 3145736 | tf_op jit(solution)/shard_map/ppermute | solution.py:304
  134.2 33.7 %collective-permute-start.21 = (bf16[1024,256]{1,0:T(8,128)(2,1)}, bf16[1024,256]{1,0:T(8,128)(2,1)}, u32[]{:S(2)}, u32[]{:S(2)}) collective-permute-start(bf16[1024,256]{1,0:T(8,128)(2,1)} %slice.189), channel_id=1, source_target_pairs={{0,2},{2,0},{4,6},{6,4},{8,10},{10,8},{12,14},{14,12},{16,18},{18,... | collective-permute-start | bytes 1572872 | tf_op jit(solution)/shard_map/ppermute | solution.py:304
  142.9 60.5 %collective-permute-start.27 = (bf16[2,256,1024]{2,1,0:T(8,128)(2,1)}, bf16[2,256,1024]{2,1,0:T(8,128)(2,1)}, u32[]{:S(2)}, u32[]{:S(2)}) collective-permute-start(bf16[2,256,1024]{2,1,0:T(8,128)(2,1)} %get-tuple-element.102), channel_id=1, source_target_pairs={{0,2},{2,0},{4,6},{6,4},{8,10},{10,8},{12,14},{14,12},{16,18},{18,... | collective-permute-start | bytes 3145736 | tf_op jit(solution)/shard_map/ppermute | solution.py:304
  158.8 44.6 %collective-permute-start.28 = (bf16[2,256,1024]{2,1,0:T(8,128)(2,1)}, bf16[2,256,1024]{2,1,0:T(8,128)(2,1)}, u32[]{:S(2)}, u32[]{:S(2)}) collective-permute-start(bf16[2,256,1024]{2,1,0:T(8,128)(2,1)} %get-tuple-element.104), channel_id=1, source_target_pairs={{0,4},{2,6},{4,0},{6,2},{8,12},{10,14},{12,8},{14,10},{16,20},{18,... | collective-permute-start | bytes 3145736 | tf_op jit(solution)/shard_map/ppermute | solution.py:304
  168.0 28.4 %collective-permute-start.17 = (bf16[1024,256]{1,0:T(8,128)(2,1)S(1)}, bf16[1024,256]{1,0:T(8,128)(2,1)S(1)}, u32[]{:S(2)}, u32[]{:S(2)}) collective-permute-start(bf16[1024,256]{1,0:T(8,128)(2,1)S(1)} %slice.186), channel_id=1, source_target_pairs={{0,4},{2,6},{4,0},{6,2},{8,12},{10,14},{12,8},{14,10},{16,20},{18,... | collective-permute-start | bytes 1572872 | tf_op jit(solution)/shard_map/ppermute | solution.py:304
  169.9 31.8 %collective-permute-start.26 = (bf16[1024,256]{1,0:T(8,128)(2,1)S(1)}, bf16[1024,256]{1,0:T(8,128)(2,1)}, u32[]{:S(2)}, u32[]{:S(2)}) collective-permute-start(bf16[1024,256]{1,0:T(8,128)(2,1)S(1)} %slice.191), channel_id=1, source_target_pairs={{0,2},{2,0},{4,6},{6,4},{8,10},{10,8},{12,14},{14,12},{16,18},{18,... | collective-permute-start | bytes 1572872 | tf_op jit(solution)/shard_map/ppermute | solution.py:304
  182.5 69.1 %collective-permute-start.22 = (bf16[1024,256]{1,0:T(8,128)(2,1)}, bf16[1024,256]{1,0:T(8,128)(2,1)S(1)}, u32[]{:S(2)}, u32[]{:S(2)}) collective-permute-start(bf16[1024,256]{1,0:T(8,128)(2,1)} %slice.188), channel_id=1, source_target_pairs={{0,4},{2,6},{4,0},{6,2},{8,12},{10,14},{12,8},{14,10},{16,20},{18,... | collective-permute-start | bytes 1572872 | tf_op jit(solution)/shard_map/ppermute | solution.py:304
  201.7 51.4 %collective-permute-start.23 = (bf16[2,256,1024]{2,1,0:T(8,128)(2,1)}, bf16[2,256,1024]{2,1,0:T(8,128)(2,1)}, u32[]{:S(2)}, u32[]{:S(2)}) collective-permute-start(bf16[2,256,1024]{2,1,0:T(8,128)(2,1)} %get-tuple-element.96), channel_id=1, source_target_pairs={{0,2},{2,0},{4,6},{6,4},{8,10},{10,8},{12,14},{14,12},{16,18},{18,... | collective-permute-start | bytes 3145736 | tf_op jit(solution)/shard_map/ppermute | solution.py:304
  205.9 39.5 %collective-permute-start.40 = (bf16[256,1024]{1,0:T(8,128)(2,1)S(1)}, bf16[256,1024]{1,0:T(8,128)(2,1)S(1)}, u32[]{:S(2)}, u32[]{:S(2)}) collective-permute-start(bf16[256,1024]{1,0:T(8,128)(2,1)S(1)} %fusion.15), channel_id=1, source_target_pairs={{0,2},{2,0},{4,6},{6,4},{8,10},{10,8},{12,14},{14,12},{16,18},{18,... | collective-permute-start | bytes 1572872 | tf_op jit(solution)/shard_map/ppermute | solution.py:304
  206.3 42.6 %collective-permute-start.39 = (bf16[256,1024]{1,0:T(8,128)(2,1)S(1)}, bf16[256,1024]{1,0:T(8,128)(2,1)}, u32[]{:S(2)}, u32[]{:S(2)}) collective-permute-start(bf16[256,1024]{1,0:T(8,128)(2,1)S(1)} %fusion.14), channel_id=1, source_target_pairs={{0,4},{2,6},{4,0},{6,2},{8,12},{10,14},{12,8},{14,10},{16,20},{18,... | collective-permute-start | bytes 1572872 | tf_op jit(solution)/shard_map/ppermute | solution.py:304
  214.5 39.1 %collective-permute-start.24 = (bf16[2,256,1024]{2,1,0:T(8,128)(2,1)}, bf16[2,256,1024]{2,1,0:T(8,128)(2,1)}, u32[]{:S(2)}, u32[]{:S(2)}) collective-permute-start(bf16[2,256,1024]{2,1,0:T(8,128)(2,1)} %get-tuple-element.98), channel_id=1, source_target_pairs={{0,4},{2,6},{4,0},{6,2},{8,12},{10,14},{12,8},{14,10},{16,20},{18,... | collective-permute-start | bytes 3145736 | tf_op jit(solution)/shard_map/ppermute | solution.py:304
  245.4 65.9 %collective-permute-start.35 = (bf16[2,256,1024]{2,1,0:T(8,128)(2,1)}, bf16[2,256,1024]{2,1,0:T(8,128)(2,1)S(1)}, u32[]{:S(2)}, u32[]{:S(2)}) collective-permute-start(bf16[2,256,1024]{2,1,0:T(8,128)(2,1)} %get-tuple-element.119), channel_id=1, source_target_pairs={{0,2},{2,0},{4,6},{6,4},{8,10},{10,8},{12,14},{14,12},{16,18},{18,... | collective-permute-start | bytes 3145736 | tf_op jit(solution)/shard_map/ppermute | solution.py:304
  248.9 64.2 %collective-permute-start.36 = (bf16[2,256,1024]{2,1,0:T(8,128)(2,1)}, bf16[2,256,1024]{2,1,0:T(8,128)(2,1)}, u32[]{:S(2)}, u32[]{:S(2)}) collective-permute-start(bf16[2,256,1024]{2,1,0:T(8,128)(2,1)} %get-tuple-element.121), channel_id=1, source_target_pairs={{0,2},{2,0},{4,6},{6,4},{8,10},{10,8},{12,14},{14,12},{16,18},{18,... | collective-permute-start | bytes 3145736 | tf_op jit(solution)/shard_map/ppermute | solution.py:304
  251.6 64.3 %collective-permute-start.43 = (bf16[2,256,1024]{2,1,0:T(8,128)(2,1)}, bf16[2,256,1024]{2,1,0:T(8,128)(2,1)}, u32[]{:S(2)}, u32[]{:S(2)}) collective-permute-start(bf16[2,256,1024]{2,1,0:T(8,128)(2,1)} %get-tuple-element.133), channel_id=1, source_target_pairs={{0,4},{2,6},{4,0},{6,2},{8,12},{10,14},{12,8},{14,10},{16,20},{18,... | collective-permute-start | bytes 3145736 | tf_op jit(solution)/shard_map/ppermute | solution.py:304
  253.1 66.7 %collective-permute-start.47 = (bf16[2,256,1024]{2,1,0:T(8,128)(2,1)}, bf16[2,256,1024]{2,1,0:T(8,128)(2,1)S(1)}, u32[]{:S(2)}, u32[]{:S(2)}) collective-permute-start(bf16[2,256,1024]{2,1,0:T(8,128)(2,1)} %get-tuple-element.138), channel_id=1, source_target_pairs={{0,4},{2,6},{4,0},{6,2},{8,12},{10,14},{12,8},{14,10},{16,20},{18,... | collective-permute-start | bytes 3145736 | tf_op jit(solution)/shard_map/ppermute | solution.py:304
  253.6 72.0 %collective-permute-start.41 = (bf16[256,2048]{1,0:T(8,128)(2,1)}, bf16[256,2048]{1,0:T(8,128)(2,1)S(1)}, u32[]{:S(2)}, u32[]{:S(2)}) collective-permute-start(bf16[256,2048]{1,0:T(8,128)(2,1)} %pad_maximum_fusion), channel_id=1, source_target_pairs={{0,16},{2,18},{4,20},{6,22},{8,24},{10,26},{12,28},{14,30},{16,0},... | collective-permute-start | bytes 3145736 | tf_op jit(solution)/shard_map/ppermute | solution.py:404
  313.1 61.8 %collective-permute-start.29 = (bf16[2048,128]{1,0:T(8,128)(2,1)S(1)}, bf16[2048,128]{1,0:T(8,128)(2,1)S(1)}, u32[]{:S(2)}, u32[]{:S(2)}) collective-permute-start(bf16[2048,128]{1,0:T(8,128)(2,1)S(1)} %copy-done.21), channel_id=1, source_target_pairs={{2,0},{4,2},{6,4},{8,6},{10,8},{12,10},{14,12},{16,14},{18,16},{20... | collective-permute-start | bytes 1572872 | tf_op jit(solution)/shard_map/ppermute | solution.py:456
  336.7 35.3 %collective-permute-start.45 = (bf16[256,2048]{1,0:T(8,128)(2,1)S(1)}, bf16[256,2048]{1,0:T(8,128)(2,1)S(1)}, u32[]{:S(2)}, u32[]{:S(2)}) collective-permute-start(bf16[256,2048]{1,0:T(8,128)(2,1)S(1)} %pad_maximum_fusion.1), channel_id=1, source_target_pairs={{0,24},{2,26},{4,28},{6,30},{8,0},{10,2},{12,4},{14,6},{16,8},{18,... | collective-permute-start | bytes 3145736 | tf_op jit(solution)/shard_map/ppermute | solution.py:404
  342.8 32.3 %collective-permute-start.32 = (f32[128,128]{1,0:T(8,128)S(1)}, f32[128,128]{1,0:T(8,128)S(1)}, u32[]{:S(2)}, u32[]{:S(2)}) collective-permute-start(f32[128,128]{1,0:T(8,128)S(1)} %get-tuple-element.140), channel_id=1, source_target_pairs={{0,8},{2,10},{4,12},{6,14},{8,16},{10,18},{12,20},{14,22},{16,24},... | collective-permute-start | bytes 196616 | tf_op jit(solution)/shard_map/ppermute | solution.py:332
  347.8 28.2 %collective-permute-start.34 = (f32[128,128]{1,0:T(8,128)S(1)}, f32[128,128]{1,0:T(8,128)S(1)}, u32[]{:S(2)}, u32[]{:S(2)}) collective-permute-start(f32[128,128]{1,0:T(8,128)S(1)} %get-tuple-element.141), channel_id=1, source_target_pairs={{0,24},{2,26},{4,28},{6,30},{8,0},{10,2},{12,4},{14,6},{16,8},{18,... | collective-permute-start | bytes 196616 | tf_op jit(solution)/shard_map/ppermute | solution.py:332
  (46 other events, 755.4 us)
Sparse Core Ops, SparseCore 0:
  9.6 22.5 all-gather.1

commit v2 on v1

--- a/solution.py
+++ b/solution.py
@@ -324,8 +324,9 @@
 def reduce_filters(at, part, chan_count):
     taps = part.shape[1]
     part = part.reshape(at.depth, 2, 2, chan_count, taps)
-    part = pick(at.x, part, 2) + lax.ppermute(pick(1 - at.x, part, 2), "ctx", at.pairs_x)
-    part = pick(at.y, part, 1) + lax.ppermute(pick(1 - at.y, part, 1), "ctx", at.pairs_y)
+    for bit, pairs, axis in ((at.x, at.pairs_x, 2), (at.y, at.pairs_y, 1)):
+        got = lax.ppermute(pick(1 - bit, part, axis).astype(BF16), "ctx", pairs)
+        part = pick(bit, part, axis) + got.astype(F32)
     at_z = lambda by: lax.dynamic_index_in_dim(part, (at.z + by) % at.depth, 0, keepdims=False)
     total = at_z(0)
     for by in range(1, at.depth):
@@ -355,21 +356,30 @@
     pair = ordered(at.x, own_filters, filters_x)
     filters_y = lax.ppermute(pair, "ctx", at.pairs_y)
     plane = ordered(at.y, pair, filters_y)
-    shards = [own]
-    for by in near[1:2]:
-        shards.append(lax.ppermute(after(own, filters_y), "ctx", at.pairs_z(by)))
-    ring = [
-        lax.ppermute(after(plane, *shards[1:]), "ctx", at.pairs_z(by)) for by in range(at.depth - 1, 0, -1)
-    ]
-    for by in near[2:]:
-        shards.append(lax.ppermute(after(own, *(ring if len(shards) == 2 else shards[-1:])), "ctx", at.pairs_z(by)))
+    shards = {0: own}
+    ring = {0: plane}
+
+    def step_z(held, by, *earlier):
+        way = 1 if by <= at.depth // 2 else -1
+        return lax.ppermute(after(held[(by - way) % at.depth], *earlier), "ctx", at.pairs_z(way))
+
+    before = filters_y
+    for by in near[1:]:
+        shards[by] = step_z(shards, by, before)
+        if by == near[1]:
+            for way in near[1:]:
+                ring[way] = step_z(ring, way, shards[by])
+        before = (shards[by], ring[near[-1]])[by == near[1]]
+    ring = [ring[by] for by in range(at.depth - 1, 0, -1)]
+    shards = [shards[by] for by in near]
     ring = jnp.stack((ring + [plane]) * 2)
     ring = lax.dynamic_slice_in_dim(ring, at.depth - 1 - at.z, at.depth, axis=0)
     all_filters = ring.reshape(chan, taps)
     prior = lax.ppermute(after(kv_product[:, seq_len - taps :], shards[1]), "ctx", to_right)
 
     from_x, from_y, diag_a, diag_b = {}, {}, {}, {}
-    kept, summed = {}, {}
+    kept, summed, carried = {}, {}, {}
+    depth = at.depth
 
     def gather_first(k):
         both = (from_x[0], from_y[0]) if k == 1 else ()
@@ -401,9 +411,16 @@
         sum_b = keep_b[0].astype(F32) + got_b[0].astype(F32) + last_b.astype(F32)
         joint = jnp.concatenate([sum_a, sum_b], axis=1)
         by = far[k]
-        summed[k] = joint if by == 0 else lax.ppermute(joint.astype(BF16), "ctx", at.pairs_z(by))
-        if k + 2 < depth:
-            stages.finished(summed[k])
+        for piece in carried.pop(by, ()):
+            joint = joint + piece.astype(F32)
+        if by == 0:
+            summed[0] = joint
+            return
+        way = 1 if by <= depth // 2 else -1
+        got = lax.ppermute(joint.astype(BF16), "ctx", at.pairs_z(way))
+        carried.setdefault((by - way) % depth, []).append(got)
+        if k < 2:
+            stages.finished(got)
 
     mixed = gated = place = products = None
 
@@ -438,7 +455,7 @@
         for k in range(depth):
             if stage == (2, 3, 4, 5)[min(k, 3)] + max(0, k - 3):
                 weight_part(k)
-            if stage == k + depth + 3:
+            if stage == depth + [3, 4, 5, 6][min(k, 3)] + max(0, k - 3):
                 reduce_third(k)
         for part in range(PARTS):
             if stage == depth + [2, 3][part]:
@@ -447,10 +464,7 @@
             action(k)
         stages.advance()
 
-    total = summed[depth - 1]
-    for k in range(depth - 1):
-        total = total + summed[k].astype(F32)
-    w_grad = total * norm_scale
+    w_grad = summed[0] * norm_scale
 
     gate_grad, kv_grad, last, head, filt_part = products
     tail = lax.ppermute(head, "ctx", to_left)

time: 398 us -> 373 us (0.937)
  starting transfers between devices: 107 us -> 64 us
  waiting for transfers between devices: 125 us -> 145 us
    ppermute x11, starting transfers between devices: 39.8 us -> 15.9 us  [the longest x3 7.19 us: reduce_third(): got = lax.ppermute(joint.astype(BF16), 'ctx', at.pairs_z(way))]
    ppermute x11, waiting for transfers between devices: 67.8 us -> 87.8 us  [the longest x6 56.6 us: step_z(): lax.ppermute(after(held[(by - way) % at.depth], *earlier), 'ctx', at.pair...]
    ppermute x32, starting transfers between devices: 49.6 us -> 33.8 us  [send(): lax.ppermute(after(array, *self.arrived[-self.back], *self.ready, *earlie...]
    ppermute x32, waiting for transfers between devices: 45.8 us -> 52.8 us  [send(): lax.ppermute(after(array, *self.arrived[-self.back], *self.ready, *earlie...]
    ppermute x1, waiting for transfers between devices: 6.85 us -> 0.01 us  [on_device(): lax.ppermute(after(kv_product[:, seq_len - taps:], shards[1]), 'ctx', to_...]
    another operation x6 -> x4, other arithmetic: 8.06 us -> 5.71 us
  transfers between devices with their start and end apart: 51 -> 51, of which waited for: 16 -> 18; matrix products, arithmetic and copies ran while one was open for 9% -> 9% of each run, Pallas kernels for 28% -> 30%
where the time goes in v2:
time: 373 us; the launch traced here: 372 us
  waiting for transfers between devices  145 us (39%)
  Pallas kernels  111 us (30%)
  starting transfers between devices  64 us (17%)
  other arithmetic  24.4 us (7%)
  between operations  14.7 us (4%)
  local copies, waits for them, and re-layouts  12.5 us (3%)
    pallas_call x2, Pallas kernels, run_product(): pl.pallas_call(lambda *refs: product_kernel(count, *refs), grid_spec=pltp...  58.4 us
    ppermute x6, waiting for transfers between devices, step_z(): lax.ppermute(after(held[(by - way) % at.depth], *earlier), 'ctx', at.pair...  56.6 us
    ppermute x32, waiting for transfers between devices, send(): lax.ppermute(after(array, *self.arrived[-self.back], *self.ready, *earlie...  52.8 us
    pallas_call x4, Pallas kernels, run_weight(): pl.pallas_call(weight_kernel, grid_spec=pltpu.PrefetchScalarGridSpec(num_...  34.5 us
    ppermute x32, starting transfers between devices, send(): lax.ppermute(after(array, *self.arrived[-self.back], *self.ready, *earlie...  33.8 us
    ppermute x3, waiting for transfers between devices, reduce_third(): got = lax.ppermute(joint.astype(BF16), 'ctx', at.pairs_z(way))  21 us
    pallas_call x1, Pallas kernels, run_mix(): pl.pallas_call(mix_kernel, grid=(chan // group,), in_specs=[rows(taps), r...  18.6 us
    ppermute x2, waiting for transfers between devices, reduce_filters(): got = lax.ppermute(pick(1 - bit, part, axis).astype(BF16), 'ctx', pairs)  10.2 us
  transfers between devices with their start and end apart: 51, of which 18 were waited for; matrix products, arithmetic and copies ran while one was open for 9% of the time, Pallas kernels for 30%

profile of v2, /device:TPU:0, one launch (start us, length us, event | category | flops | bytes accessed | tf_op | source)
XLA Modules:
  0.0 371.9 jit_solution(14021629211403127972)
XLA Ops:
  7.9 3.0 collective-permute-start
  12.9 2.1 collective-permute-start.2
  17.2 2.1 collective-permute-start.5
  23.0 19.3 %collective-permute-done.5.refs_6_ = bf16[2048,256]{1,0:T(8,128)(2,1)} collective-permute-done((bf16[2048,256]{1,0:T(8,128)(2,1)S(1)}, bf16[2048,256]{1,0:T(8,128)(2,1)}, u32[]{:S(2)}, u32[]{:S(2)}) %collective-permute-start.5) | collective-permute-done | bytes 1048608 | tf_op jit(solution)/shard_map/ppermute | solution.py:364
  42.3 3.8 %collective-permute-start.8 = (bf16[2,2,128,128]{3,2,1,0:T(8,128)(2,1)}, bf16[2,2,128,128]{3,2,1,0:T(8,128)(2,1)S(1)}, u32[]{:S(2)}, u32[]{:S(2)}) collective-permute-start(bf16[2,2,128,128]{3,2,1,0:T(8,128)(2,1)} %pad_maximum_fusion.2), channel_id=1, source_target_pairs={{0,24},{2,26},{4,28},{6,30},{8,0},{10,2},{12,4},{14,6},{16,8},{18,... | collective-permute-start | bytes 393224 | tf_op jit(solution)/shard_map/ppermute | solution.py:364
  52.5 2.5 collective-permute-start.11
  57.3 8.2 %collective-permute-done.10 = bf16[2,2,128,128]{3,2,1,0:T(8,128)(2,1)S(1)} collective-permute-done((bf16[2,2,128,128]{3,2,1,0:T(8,128)(2,1)S(1)}, bf16[2,2,128,128]{3,2,1,0:T(8,128)(2,1)S(1)}, u32[]{:S(2)}, u32[]{:S(2)}) %collective-permute-start.10) | collective-permute-done | bytes 131104 | tf_op jit(solution)/shard_map/ppermute | solution.py:364
  66.6 29.1 %collective-permute-done.13.refs_10_ = bf16[2048,256]{1,0:T(8,128)(2,1)} collective-permute-done((bf16[2048,256]{1,0:T(8,128)(2,1)S(1)}, bf16[2048,256]{1,0:T(8,128)(2,1)}, u32[]{:S(2)}, u32[]{:S(2)}) %collective-permute-start.13) | collective-permute-done | bytes 1048608 | tf_op jit(solution)/shard_map/ppermute | solution.py:364
  96.4 18.6 %mix_kernel.1 = (bf16[2048,1024]{1,0:T(8,128)(2,1)}, bf16[2048,1024]{1,0:T(8,128)(2,1)}) custom-call(bf16[2048,128]{1,0:T(8,128)(2,1)} %bitcast.152, bf16[2048,1024]{1,0:T(8,128)(2,1)} %refs_20_.3, bf16[2048,128]{1,0:T(8,128)(2,1)} %copy-done.20, bf16[2048,1024]{1,0:T(8,128)(2,1)} %refs_19_.3, bf16[256,256]{1,0:T(8,128)(2,1)} %constant.124.clone.forward_ref.refs_23_, ...), custom_call_target="tpu_custom_call" | custom-call | flops 7516192768 | bytes 16777216 | tf_op jit(solution)/shard_map/mix_kernel/pallas_call | solution.py:94
  117.0 8.6 %weight_kernel.4 = (bf16[2,256,1024]{2,1,0:T(8,128)(2,1)}, bf16[2,256,1024]{2,1,0:T(8,128)(2,1)}, bf16[2,256,1024]{2,1,0:T(8,128)(2,1)}, bf16[2,256,1024]{2,1,0:T(8,128)(2,1)}) custom-call(s32[4]{0:T(128)} %get-tuple-element.149.place_ref, bf16[4096,1024]{1,0:T(8,128)(2,1)} %all-gather.2.cloned.1.call-done.g00.g01.g10.g11.refs_1_, ...), custom_call_target="tpu_custom_call" | custom-call | flops 4294967296 | bytes 10485760 | tf_op jit(solution)/shard_map/weight_kernel/pallas_call | solution.py:130
  134.1 8.5 %weight_kernel.5 = (bf16[2,256,1024]{2,1,0:T(8,128)(2,1)}, bf16[2,256,1024]{2,1,0:T(8,128)(2,1)}, bf16[2,256,1024]{2,1,0:T(8,128)(2,1)}, bf16[2,256,1024]{2,1,0:T(8,128)(2,1)}) custom-call(s32[4]{0:T(128)} %get-tuple-element.150.place_ref, bf16[4096,1024]{1,0:T(8,128)(2,1)} %all-gather.2.cloned.1.call-done.g00.g01.g10.g11.refs_1_, ...), custom_call_target="tpu_custom_call" | custom-call | flops 4294967296 | bytes 10485760 | tf_op jit(solution)/shard_map/weight_kernel/pallas_call | solution.py:130
  143.7 17.4 %collective-permute-done.12.refs_9_ = bf16[1024,256]{1,0:T(8,128)(2,1)} collective-permute-done((bf16[1024,256]{1,0:T(8,128)(2,1)S(1)}, bf16[1024,256]{1,0:T(8,128)(2,1)}, u32[]{:S(2)}, u32[]{:S(2)}) %collective-permute-start.12) | collective-permute-done | bytes 524320 | tf_op jit(solution)/shard_map/ppermute | solution.py:304
  162.5 14.0 %collective-permute-done.21.refs_9_ = bf16[1024,256]{1,0:T(8,128)(2,1)} collective-permute-done((bf16[1024,256]{1,0:T(8,128)(2,1)}, bf16[1024,256]{1,0:T(8,128)(2,1)}, u32[]{:S(2)}, u32[]{:S(2)}) %collective-permute-start.21) | collective-permute-done | bytes 524320 | tf_op jit(solution)/shard_map/ppermute | solution.py:304
  177.8 8.7 %weight_kernel.6 = (bf16[2,256,1024]{2,1,0:T(8,128)(2,1)}, bf16[2,256,1024]{2,1,0:T(8,128)(2,1)}, bf16[2,256,1024]{2,1,0:T(8,128)(2,1)}, bf16[2,256,1024]{2,1,0:T(8,128)(2,1)}) custom-call(s32[4]{0:T(128)} %get-tuple-element.151.place_ref, bf16[4096,1024]{1,0:T(8,128)(2,1)} %all-gather.2.cloned.1.call-done.g00.g01.g10.g11.refs_1_, ...), custom_call_target="tpu_custom_call" | custom-call | flops 4294967296 | bytes 10485760 | tf_op jit(solution)/shard_map/weight_kernel/pallas_call | solution.py:130
  189.8 8.8 %weight_kernel.7 = (bf16[2,256,1024]{2,1,0:T(8,128)(2,1)}, bf16[2,256,1024]{2,1,0:T(8,128)(2,1)}, bf16[2,256,1024]{2,1,0:T(8,128)(2,1)}, bf16[2,256,1024]{2,1,0:T(8,128)(2,1)}) custom-call(s32[4]{0:T(128)} %get-tuple-element.152.place_ref, bf16[4096,1024]{1,0:T(8,128)(2,1)} %all-gather.2.cloned.1.call-done.g00.g01.g10.g11.refs_1_, ...), custom_call_target="tpu_custom_call" | custom-call | flops 4294967296 | bytes 10485760 | tf_op jit(solution)/shard_map/weight_kernel/pallas_call | solution.py:130
  200.1 7.5 %collective-permute-done.26.refs_13_ = bf16[1024,256]{1,0:T(8,128)(2,1)} collective-permute-done((bf16[1024,256]{1,0:T(8,128)(2,1)S(1)}, bf16[1024,256]{1,0:T(8,128)(2,1)}, u32[]{:S(2)}, u32[]{:S(2)}) %collective-permute-start.26) | collective-permute-done | bytes 524320 | tf_op jit(solution)/shard_map/ppermute | solution.py:304
  207.5 2.6 collective-permute-start.23
  210.1 2.1 fusion.12
  215.0 3.8 %collective-permute-done.25.refs_17_ = bf16[1024,256]{1,0:T(8,128)(2,1)S(1)} collective-permute-done((bf16[1024,256]{1,0:T(8,128)(2,1)S(1)}, bf16[1024,256]{1,0:T(8,128)(2,1)S(1)}, u32[]{:S(2)}, u32[]{:S(2)}) %collective-permute-start.25) | collective-permute-done | bytes 524320 | tf_op jit(solution)/shard_map/ppermute | solution.py:304
  220.4 29.1 %product_kernel.2 = (f32[2048,1024]{1,0:T(8,128)}, bf16[2048,1024]{1,0:T(8,128)(2,1)}, f32[2048,128]{1,0:T(8,128)}, bf16[2048,128]{1,0:T(8,128)(2,1)}, f32[2048,128]{1,0:T(8,128)}) custom-call(s32[16]{0:T(128)} %stack.173.refs_0_, bf16[4096,1024]{1,0:T(8,128)(2,1)} %all-gather.2.cloned.1.call-done.g00.g01.g10.g11.refs_1_, bf16[2048,256]{1,0:T(8,128)(2,1)} %bitcast.150, ...), custom_call_target="tpu_custom_call" | custom-call | flops 12884901888 | bytes 29360128 | tf_op jit(solution)/shard_map/product_kernel/pallas_call | solution.py:229
  249.5 2.5 collective-permute-start.35
  259.0 2.0 fusion.11
  261.0 2.0 fusion.10
  263.1 29.3 %product_kernel.3 = (f32[2048,1024]{1,0:T(8,128)}, bf16[2048,1024]{1,0:T(8,128)(2,1)}, f32[2048,128]{1,0:T(8,128)}, bf16[2048,128]{1,0:T(8,128)(2,1)}, f32[2048,128]{1,0:T(8,128)}) custom-call(s32[16]{0:T(128)} %stack.173.refs_0_, ...), custom_call_target="tpu_custom_call", output_to_operand_aliasing={{0}: (25, {}), {1}: (26, {}), {2}: (27, {}), {3}: (28, {}),... | custom-call | flops 12884901888 | bytes 29360128 | tf_op jit(solution)/shard_map/product_kernel/pallas_call | solution.py:229
  297.0 3.2 collective-permute-done.30
  303.3 7.0 %collective-permute-done.31 = bf16[4,128,128]{2,1,0:T(8,128)(2,1)S(1)} collective-permute-done((bf16[4,128,128]{2,1,0:T(8,128)(2,1)S(1)}, bf16[4,128,128]{2,1,0:T(8,128)(2,1)S(1)}, u32[]{:S(2)}, u32[]{:S(2)}) %collective-permute-start.31) | collective-permute-done | bytes 131104 | tf_op jit(solution)/shard_map/ppermute | solution.py:328
  310.8 3.5 collective-permute-start.34
  320.7 5.8 %collective-permute-start.45 = (bf16[256,2048]{1,0:T(8,128)(2,1)S(1)}, bf16[256,2048]{1,0:T(8,128)(2,1)S(1)}, u32[]{:S(2)}, u32[]{:S(2)}) collective-permute-start(bf16[256,2048]{1,0:T(8,128)(2,1)S(1)} %pad_maximum_fusion.1), channel_id=1, source_target_pairs={{0,24},{2,26},{4,28},{6,30},{8,0},{10,2},{12,4},{14,6},{16,8},{18,... | collective-permute-start | bytes 3145736 | tf_op jit(solution)/shard_map/ppermute | solution.py:420
  330.7 14.5 %collective-permute-done.45 = bf16[256,2048]{1,0:T(8,128)(2,1)S(1)} collective-permute-done((bf16[256,2048]{1,0:T(8,128)(2,1)S(1)}, bf16[256,2048]{1,0:T(8,128)(2,1)S(1)}, u32[]{:S(2)}, u32[]{:S(2)}) %collective-permute-start.45) | collective-permute-done | bytes 1048608 | tf_op jit(solution)/shard_map/ppermute | solution.py:420
  348.3 6.1 %collective-permute-done.46 = bf16[256,1024]{1,0:T(8,128)(2,1)S(1)} collective-permute-done((bf16[256,1024]{1,0:T(8,128)(2,1)S(1)}, bf16[256,1024]{1,0:T(8,128)(2,1)S(1)}, u32[]{:S(2)}, u32[]{:S(2)}) %collective-permute-start.46) | collective-permute-done | bytes 524320 | tf_op jit(solution)/shard_map/ppermute | solution.py:304
  354.6 2.0 collective-permute-done.48
  356.8 6.5 %collective-permute-done.49 = bf16[256,2048]{1,0:T(8,128)(2,1)S(1)} collective-permute-done((bf16[256,2048]{1,0:T(8,128)(2,1)S(1)}, bf16[256,2048]{1,0:T(8,128)(2,1)S(1)}, u32[]{:S(2)}, u32[]{:S(2)}) %collective-permute-start.49) | collective-permute-done | bytes 1048608 | tf_op jit(solution)/shard_map/ppermute | solution.py:420
  (185 shorter events, 73.4 us)
Async XLA Ops:
  7.2 109.8 %all-gather.2.cloned.1.call-start = ((), (), s32[]{:S(2)}) async-start(), calls=%async_computation | async-start | bytes 12582912 | tf_op jit(solution)/shard_map/all_gather | solution.py:350
  17.2 25.1 %collective-permute-start.5 = (bf16[2048,256]{1,0:T(8,128)(2,1)S(1)}, bf16[2048,256]{1,0:T(8,128)(2,1)}, u32[]{:S(2)}, u32[]{:S(2)}) collective-permute-start(bf16[2048,256]{1,0:T(8,128)(2,1)S(1)} %bitcast.146), channel_id=1, source_target_pairs={{0,8},{2,10},{4,12},{6,14},{8,16},{10,18},{12,20},{14,22},{16,24},... | collective-permute-start | bytes 3145736 | tf_op jit(solution)/shard_map/ppermute | solution.py:364
  19.3 29.3 %collective-permute-start.1 = (bf16[2048,256]{1,0:T(8,128)(2,1)S(1)}, bf16[2048,256]{1,0:T(8,128)(2,1)S(1)}, u32[]{:S(2)}, u32[]{:S(2)}) collective-permute-start(bf16[2048,256]{1,0:T(8,128)(2,1)S(1)} %bitcast.147), channel_id=1, source_target_pairs={{0,2},{2,0},{4,6},{6,4},{8,10},{10,8},{12,14},{14,12},{16,18},{18,... | collective-permute-start | bytes 3145736 | tf_op jit(solution)/shard_map/ppermute | solution.py:304
  20.8 28.7 %collective-permute-start.3 = (bf16[2048,256]{1,0:T(8,128)(2,1)S(1)}, bf16[2048,256]{1,0:T(8,128)(2,1)S(1)}, u32[]{:S(2)}, u32[]{:S(2)}) collective-permute-start(bf16[2048,256]{1,0:T(8,128)(2,1)S(1)} %bitcast.148), channel_id=1, source_target_pairs={{0,4},{2,6},{4,0},{6,2},{8,12},{10,14},{12,8},{14,10},{16,20},{18,... | collective-permute-start | bytes 3145736 | tf_op jit(solution)/shard_map/ppermute | solution.py:304
  49.5 65.5 %collective-permute-start.7 = (bf16[2048,256]{1,0:T(8,128)(2,1)}, bf16[2048,256]{1,0:T(8,128)(2,1)}, u32[]{:S(2)}, u32[]{:S(2)}) collective-permute-start(bf16[2048,256]{1,0:T(8,128)(2,1)} %collective-permute-done.5.refs_6_), channel_id=1, source_target_pairs={{0,4},{2,6},{4,0},{6,2},{8,12},{10,14},{12,8},{14,10},{16,20},{18,... | collective-permute-start | bytes 3145736 | tf_op jit(solution)/shard_map/ppermute | solution.py:304
  51.0 65.3 %collective-permute-start.6 = (bf16[2048,256]{1,0:T(8,128)(2,1)}, bf16[2048,256]{1,0:T(8,128)(2,1)}, u32[]{:S(2)}, u32[]{:S(2)}) collective-permute-start(bf16[2048,256]{1,0:T(8,128)(2,1)} %collective-permute-done.5.refs_6_), channel_id=1, source_target_pairs={{0,2},{2,0},{4,6},{6,4},{8,10},{10,8},{12,14},{14,12},{16,18},{18,... | collective-permute-start | bytes 3145736 | tf_op jit(solution)/shard_map/ppermute | solution.py:304
  52.5 43.1 %collective-permute-start.11 = (bf16[2048,128]{1,0:T(8,128)(2,1)}, bf16[2048,128]{1,0:T(8,128)(2,1)S(1)}, u32[]{:S(2)}, u32[]{:S(2)}) collective-permute-start(bf16[2048,128]{1,0:T(8,128)(2,1)} %slice.141), channel_id=1, source_target_pairs={{0,2},{2,4},{4,6},{6,8},{8,10},{10,12},{12,14},{14,16},{16,18},{18... | collective-permute-start | bytes 1572872 | tf_op jit(solution)/shard_map/ppermute | solution.py:378
  55.8 72.5 %collective-permute-start.16 = (bf16[1024,256]{1,0:T(8,128)(2,1)}, bf16[1024,256]{1,0:T(8,128)(2,1)}, u32[]{:S(2)}, u32[]{:S(2)}) collective-permute-start(bf16[1024,256]{1,0:T(8,128)(2,1)} %slice.187), channel_id=1, source_target_pairs={{0,2},{2,0},{4,6},{6,4},{8,10},{10,8},{12,14},{14,12},{16,18},{18,... | collective-permute-start | bytes 1572872 | tf_op jit(solution)/shard_map/ppermute | solution.py:304
  65.5 30.1 %collective-permute-start.13 = (bf16[2048,256]{1,0:T(8,128)(2,1)S(1)}, bf16[2048,256]{1,0:T(8,128)(2,1)}, u32[]{:S(2)}, u32[]{:S(2)}) collective-permute-start(bf16[2048,256]{1,0:T(8,128)(2,1)S(1)} %bitcast.149), channel_id=1, source_target_pairs={{0,24},{2,26},{4,28},{6,30},{8,0},{10,2},{12,4},{14,6},{16,8},{18,... | collective-permute-start | bytes 3145736 | tf_op jit(solution)/shard_map/ppermute | solution.py:364
  95.6 29.9 %collective-permute-start.18 = (bf16[2048,256]{1,0:T(8,128)(2,1)}, bf16[2048,256]{1,0:T(8,128)(2,1)S(1)}, u32[]{:S(2)}, u32[]{:S(2)}) collective-permute-start(bf16[2048,256]{1,0:T(8,128)(2,1)} %collective-permute-done.5.refs_6_), channel_id=1, source_target_pairs={{0,8},{2,10},{4,12},{6,14},{8,16},{10,18},{12,20},{14,22},{16,24},... | collective-permute-start | bytes 3145736 | tf_op jit(solution)/shard_map/ppermute | solution.py:364
  95.6 37.4 %collective-permute-start.15 = (bf16[2048,256]{1,0:T(8,128)(2,1)}, bf16[2048,256]{1,0:T(8,128)(2,1)S(1)}, u32[]{:S(2)}, u32[]{:S(2)}) collective-permute-start(bf16[2048,256]{1,0:T(8,128)(2,1)} %collective-permute-done.13.refs_10_), channel_id=1, source_target_pairs={{0,4},{2,6},{4,0},{6,2},{8,12},{10,14},{12,8},{14,10},{16,20},{18,... | collective-permute-start | bytes 3145736 | tf_op jit(solution)/shard_map/ppermute | solution.py:304
  116.4 26.3 %collective-permute-start.14 = (bf16[2048,256]{1,0:T(8,128)(2,1)}, bf16[2048,256]{1,0:T(8,128)(2,1)S(1)}, u32[]{:S(2)}, u32[]{:S(2)}) collective-permute-start(bf16[2048,256]{1,0:T(8,128)(2,1)} %collective-permute-done.13.refs_10_), channel_id=1, source_target_pairs={{0,2},{2,0},{4,6},{6,4},{8,10},{10,8},{12,14},{14,12},{16,18},{18,... | collective-permute-start | bytes 3145736 | tf_op jit(solution)/shard_map/ppermute | solution.py:304
  126.5 50.7 %collective-permute-start.20 = (bf16[2048,256]{1,0:T(8,128)(2,1)}, bf16[2048,256]{1,0:T(8,128)(2,1)S(1)}, u32[]{:S(2)}, u32[]{:S(2)}) collective-permute-start(bf16[2048,256]{1,0:T(8,128)(2,1)} %copy-done.19), channel_id=1, source_target_pairs={{0,4},{2,6},{4,0},{6,2},{8,12},{10,14},{12,8},{14,10},{16,20},{18,... | collective-permute-start | bytes 3145736 | tf_op jit(solution)/shard_map/ppermute | solution.py:304
  128.4 32.8 %collective-permute-start.12 = (bf16[1024,256]{1,0:T(8,128)(2,1)S(1)}, bf16[1024,256]{1,0:T(8,128)(2,1)}, u32[]{:S(2)}, u32[]{:S(2)}) collective-permute-start(bf16[1024,256]{1,0:T(8,128)(2,1)S(1)} %slice.185), channel_id=1, source_target_pairs={{0,4},{2,6},{4,0},{6,2},{8,12},{10,14},{12,8},{14,10},{16,20},{18,... | collective-permute-start | bytes 1572872 | tf_op jit(solution)/shard_map/ppermute | solution.py:304
  130.2 56.3 %collective-permute-start.19 = (bf16[2048,256]{1,0:T(8,128)(2,1)}, bf16[2048,256]{1,0:T(8,128)(2,1)}, u32[]{:S(2)}, u32[]{:S(2)}) collective-permute-start(bf16[2048,256]{1,0:T(8,128)(2,1)} %copy-done.19), channel_id=1, source_target_pairs={{0,2},{2,0},{4,6},{6,4},{8,10},{10,8},{12,14},{14,12},{16,18},{18,... | collective-permute-start | bytes 3145736 | tf_op jit(solution)/shard_map/ppermute | solution.py:304
  133.0 43.5 %collective-permute-start.21 = (bf16[1024,256]{1,0:T(8,128)(2,1)}, bf16[1024,256]{1,0:T(8,128)(2,1)}, u32[]{:S(2)}, u32[]{:S(2)}) collective-permute-start(bf16[1024,256]{1,0:T(8,128)(2,1)} %slice.189), channel_id=1, source_target_pairs={{0,2},{2,0},{4,6},{6,4},{8,10},{10,8},{12,14},{14,12},{16,18},{18,... | collective-permute-start | bytes 1572872 | tf_op jit(solution)/shard_map/ppermute | solution.py:304
  142.7 67.4 %collective-permute-start.27 = (bf16[2,256,1024]{2,1,0:T(8,128)(2,1)}, bf16[2,256,1024]{2,1,0:T(8,128)(2,1)}, u32[]{:S(2)}, u32[]{:S(2)}) collective-permute-start(bf16[2,256,1024]{2,1,0:T(8,128)(2,1)} %get-tuple-element.104), channel_id=1, source_target_pairs={{0,2},{2,0},{4,6},{6,4},{8,10},{10,8},{12,14},{14,12},{16,18},{18,... | collective-permute-start | bytes 3145736 | tf_op jit(solution)/shard_map/ppermute | solution.py:304
  161.1 49.0 %collective-permute-start.28 = (bf16[2,256,1024]{2,1,0:T(8,128)(2,1)}, bf16[2,256,1024]{2,1,0:T(8,128)(2,1)}, u32[]{:S(2)}, u32[]{:S(2)}) collective-permute-start(bf16[2,256,1024]{2,1,0:T(8,128)(2,1)} %get-tuple-element.106), channel_id=1, source_target_pairs={{0,4},{2,6},{4,0},{6,2},{8,12},{10,14},{12,8},{14,10},{16,20},{18,... | collective-permute-start | bytes 3145736 | tf_op jit(solution)/shard_map/ppermute | solution.py:304
  176.5 22.2 %collective-permute-start.17 = (bf16[1024,256]{1,0:T(8,128)(2,1)S(1)}, bf16[1024,256]{1,0:T(8,128)(2,1)S(1)}, u32[]{:S(2)}, u32[]{:S(2)}) collective-permute-start(bf16[1024,256]{1,0:T(8,128)(2,1)S(1)} %slice.186), channel_id=1, source_target_pairs={{0,4},{2,6},{4,0},{6,2},{8,12},{10,14},{12,8},{14,10},{16,20},{18,... | collective-permute-start | bytes 1572872 | tf_op jit(solution)/shard_map/ppermute | solution.py:304
  177.2 30.3 %collective-permute-start.26 = (bf16[1024,256]{1,0:T(8,128)(2,1)S(1)}, bf16[1024,256]{1,0:T(8,128)(2,1)}, u32[]{:S(2)}, u32[]{:S(2)}) collective-permute-start(bf16[1024,256]{1,0:T(8,128)(2,1)S(1)} %slice.191), channel_id=1, source_target_pairs={{0,2},{2,0},{4,6},{6,4},{8,10},{10,8},{12,14},{14,12},{16,18},{18,... | collective-permute-start | bytes 1572872 | tf_op jit(solution)/shard_map/ppermute | solution.py:304
  188.5 67.7 %collective-permute-start.22 = (bf16[1024,256]{1,0:T(8,128)(2,1)}, bf16[1024,256]{1,0:T(8,128)(2,1)S(1)}, u32[]{:S(2)}, u32[]{:S(2)}) collective-permute-start(bf16[1024,256]{1,0:T(8,128)(2,1)} %slice.188), channel_id=1, source_target_pairs={{0,4},{2,6},{4,0},{6,2},{8,12},{10,14},{12,8},{14,10},{16,20},{18,... | collective-permute-start | bytes 1572872 | tf_op jit(solution)/shard_map/ppermute | solution.py:304
  207.5 50.1 %collective-permute-start.23 = (bf16[2,256,1024]{2,1,0:T(8,128)(2,1)}, bf16[2,256,1024]{2,1,0:T(8,128)(2,1)}, u32[]{:S(2)}, u32[]{:S(2)}) collective-permute-start(bf16[2,256,1024]{2,1,0:T(8,128)(2,1)} %get-tuple-element.98), channel_id=1, source_target_pairs={{0,2},{2,0},{4,6},{6,4},{8,10},{10,8},{12,14},{14,12},{16,18},{18,... | collective-permute-start | bytes 3145736 | tf_op jit(solution)/shard_map/ppermute | solution.py:304
  213.4 36.0 %collective-permute-start.40 = (bf16[256,1024]{1,0:T(8,128)(2,1)S(1)}, bf16[256,1024]{1,0:T(8,128)(2,1)}, u32[]{:S(2)}, u32[]{:S(2)}) collective-permute-start(bf16[256,1024]{1,0:T(8,128)(2,1)S(1)} %fusion.13), channel_id=1, source_target_pairs={{0,2},{2,0},{4,6},{6,4},{8,10},{10,8},{12,14},{14,12},{16,18},{18,... | collective-permute-start | bytes 1572872 | tf_op jit(solution)/shard_map/ppermute | solution.py:304
  213.5 39.9 %collective-permute-start.39 = (bf16[256,1024]{1,0:T(8,128)(2,1)}, bf16[256,1024]{1,0:T(8,128)(2,1)}, u32[]{:S(2)}, u32[]{:S(2)}) collective-permute-start(bf16[256,1024]{1,0:T(8,128)(2,1)} %fusion.12), channel_id=1, source_target_pairs={{0,4},{2,6},{4,0},{6,2},{8,12},{10,14},{12,8},{14,10},{16,20},{18,... | collective-permute-start | bytes 1572872 | tf_op jit(solution)/shard_map/ppermute | solution.py:304
  218.8 39.5 %collective-permute-start.24 = (bf16[2,256,1024]{2,1,0:T(8,128)(2,1)}, bf16[2,256,1024]{2,1,0:T(8,128)(2,1)}, u32[]{:S(2)}, u32[]{:S(2)}) collective-permute-start(bf16[2,256,1024]{2,1,0:T(8,128)(2,1)} %get-tuple-element.100), channel_id=1, source_target_pairs={{0,4},{2,6},{4,0},{6,2},{8,12},{10,14},{12,8},{14,10},{16,20},{18,... | collective-permute-start | bytes 3145736 | tf_op jit(solution)/shard_map/ppermute | solution.py:304
  249.5 44.3 %collective-permute-start.35 = (bf16[2,256,1024]{2,1,0:T(8,128)(2,1)}, bf16[2,256,1024]{2,1,0:T(8,128)(2,1)S(1)}, u32[]{:S(2)}, u32[]{:S(2)}) collective-permute-start(bf16[2,256,1024]{2,1,0:T(8,128)(2,1)} %get-tuple-element.121), channel_id=1, source_target_pairs={{0,2},{2,0},{4,6},{6,4},{8,10},{10,8},{12,14},{14,12},{16,18},{18,... | collective-permute-start | bytes 3145736 | tf_op jit(solution)/shard_map/ppermute | solution.py:304
  253.5 42.0 %collective-permute-start.36 = (bf16[2,256,1024]{2,1,0:T(8,128)(2,1)}, bf16[2,256,1024]{2,1,0:T(8,128)(2,1)S(1)}, u32[]{:S(2)}, u32[]{:S(2)}) collective-permute-start(bf16[2,256,1024]{2,1,0:T(8,128)(2,1)} %get-tuple-element.123), channel_id=1, source_target_pairs={{0,2},{2,0},{4,6},{6,4},{8,10},{10,8},{12,14},{14,12},{16,18},{18,... | collective-permute-start | bytes 3145736 | tf_op jit(solution)/shard_map/ppermute | solution.py:304
  256.2 45.5 %collective-permute-start.43 = (bf16[2,256,1024]{2,1,0:T(8,128)(2,1)}, bf16[2,256,1024]{2,1,0:T(8,128)(2,1)S(1)}, u32[]{:S(2)}, u32[]{:S(2)}) collective-permute-start(bf16[2,256,1024]{2,1,0:T(8,128)(2,1)} %get-tuple-element.135), channel_id=1, source_target_pairs={{0,4},{2,6},{4,0},{6,2},{8,12},{10,14},{12,8},{14,10},{16,20},{18,... | collective-permute-start | bytes 3145736 | tf_op jit(solution)/shard_map/ppermute | solution.py:304
  257.6 61.8 %collective-permute-start.47 = (bf16[2,256,1024]{2,1,0:T(8,128)(2,1)}, bf16[2,256,1024]{2,1,0:T(8,128)(2,1)S(1)}, u32[]{:S(2)}, u32[]{:S(2)}) collective-permute-start(bf16[2,256,1024]{2,1,0:T(8,128)(2,1)} %get-tuple-element.140), channel_id=1, source_target_pairs={{0,4},{2,6},{4,0},{6,2},{8,12},{10,14},{12,8},{14,10},{16,20},{18,... | collective-permute-start | bytes 3145736 | tf_op jit(solution)/shard_map/ppermute | solution.py:304
  258.2 52.5 %collective-permute-start.41 = (bf16[256,2048]{1,0:T(8,128)(2,1)}, bf16[256,2048]{1,0:T(8,128)(2,1)}, u32[]{:S(2)}, u32[]{:S(2)}) collective-permute-start(bf16[256,2048]{1,0:T(8,128)(2,1)} %pad_maximum_fusion), channel_id=1, source_target_pairs={{0,8},{2,10},{4,12},{6,14},{8,16},{10,18},{12,20},{14,22},{16,24},... | collective-permute-start | bytes 3145736 | tf_op jit(solution)/shard_map/ppermute | solution.py:420
  320.7 24.5 %collective-permute-start.45 = (bf16[256,2048]{1,0:T(8,128)(2,1)S(1)}, bf16[256,2048]{1,0:T(8,128)(2,1)S(1)}, u32[]{:S(2)}, u32[]{:S(2)}) collective-permute-start(bf16[256,2048]{1,0:T(8,128)(2,1)S(1)} %pad_maximum_fusion.1), channel_id=1, source_target_pairs={{0,24},{2,26},{4,28},{6,30},{8,0},{10,2},{12,4},{14,6},{16,8},{18,... | collective-permute-start | bytes 3145736 | tf_op jit(solution)/shard_map/ppermute | solution.py:420
  326.7 20.7 %collective-permute-start.29 = (bf16[2048,128]{1,0:T(8,128)(2,1)S(1)}, bf16[2048,128]{1,0:T(8,128)(2,1)S(1)}, u32[]{:S(2)}, u32[]{:S(2)}) collective-permute-start(bf16[2048,128]{1,0:T(8,128)(2,1)S(1)} %copy-done.23), channel_id=1, source_target_pairs={{2,0},{4,2},{6,4},{8,6},{10,8},{12,10},{14,12},{16,14},{18,16},{20... | collective-permute-start | bytes 1572872 | tf_op jit(solution)/shard_map/ppermute | solution.py:470
  (46 other events, 643.5 us)
Sparse Core Ops, SparseCore 0:
  9.6 22.5 all-gather.1

commit v3 on v2

--- a/solution.py
+++ b/solution.py
@@ -13,6 +13,15 @@
 BF16 = jnp.bfloat16
 VMEM = 58 * 1024 * 1024
 PARTS = 2
+MIX_STAGE = 2
+WEIGHT_STAGE = (2, 3, 4, 6)
+THIRD_STAGE = (7, 7, 8, 9)
+PRODUCT_STAGE = (6, 7)
+GATHER_SECOND = (2, 4, 4, 5)
+REDUCE_FIRST = (4, 4, 5, 7)
+REDUCE_SECOND = (6, 6, 6, 8)
+CLOSE_STAGE = 8
+Z_PINNED = 2
 
 
 def split_pair(matrix):
@@ -105,37 +114,61 @@
     )(filters, kv, prior, gate, forward, backward)
 
 
-def weight_kernel(place_ref, g00, g01, g10, g11, left_ref, right_ref, send_a, keep_a, send_b, keep_b):
+def weight_kernel(place_ref, g00, g01, g10, g11, left_ref, right_ref, *refs):
+    added, (send_a, keep_a, send_b, keep_b) = refs[:-4], refs[-4:]
     rows = g00.shape[0]
     stack = jnp.concatenate([g01[...], g11[...], g00[...], g10[...]], axis=0)
     contract = (((1,), (1,)), ((), ()))
-    left = lax.dot_general(stack, left_ref[...], contract, preferred_element_type=F32).astype(BF16)
-    send_a[0] = left[:rows]
-    send_a[1] = left[rows : 2 * rows]
-    keep_a[0] = left[2 * rows : 3 * rows]
-    keep_a[1] = left[3 * rows :]
-    right = lax.dot_general(stack, right_ref[...], contract, preferred_element_type=F32).astype(BF16)
-    send_b[0] = right[3 * rows :]
-    send_b[1] = right[rows : 2 * rows]
-    keep_b[0] = right[2 * rows : 3 * rows]
-    keep_b[1] = right[:rows]
-
-
-def run_weight(place, grad_full, gated, rows):
+    left = lax.dot_general(stack, left_ref[...], contract, preferred_element_type=F32)
+    diag = left[rows : 2 * rows]
+    for piece in added[0::2]:
+        diag = diag + piece[...].astype(F32)
+    send_a[0] = left[:rows].astype(BF16)
+    send_a[1] = diag.astype(BF16)
+    keep_a[0] = left[2 * rows : 3 * rows].astype(BF16)
+    keep_a[1] = left[3 * rows :].astype(BF16)
+    right = lax.dot_general(stack, right_ref[...], contract, preferred_element_type=F32)
+    diag = right[rows : 2 * rows]
+    for piece in added[1::2]:
+        diag = diag + piece[...].astype(F32)
+    send_b[0] = right[3 * rows :].astype(BF16)
+    send_b[1] = diag.astype(BF16)
+    keep_b[0] = right[2 * rows : 3 * rows].astype(BF16)
+    keep_b[1] = right[:rows].astype(BF16)
+
+
+def direct_kernel(place_ref, g00, g01, g10, g11, gated_ref, keep, send_x, send_y, send_z):
+    rows = g00.shape[0]
+    stack = jnp.concatenate([g00[...], g01[...], g10[...], g11[...]], axis=0)
+    both = lax.dot_general(stack, gated_ref[...], (((1,), (1,)), ((), ())), preferred_element_type=F32)
+    for k, ref in enumerate((keep, send_x, send_y, send_z)):
+        ref[...] = both[k * rows : (k + 1) * rows].astype(BF16)
+
+
+def run_weight(place, grad_full, gated, rows, direct, added=()):
     chan, seq_len = gated.shape
     width = chan // 4
     grad_spec = lambda k: pl.BlockSpec((rows, seq_len), lambda n, place: (place[k], 0))
     gated_spec = lambda first: pl.BlockSpec((width, seq_len), lambda n, place: (n + first, 0))
-    out_spec = pl.BlockSpec((2, rows, width), lambda n, place: (0, 0, n))
+    added_spec = lambda first: pl.BlockSpec((rows, width), lambda n, place: (0, n + first))
+    grads = [grad_spec(k) for k in range(4)]
+    if direct:
+        kernel, steps, in_specs, operands = direct_kernel, 4, grads + [gated_spec(0)], [gated]
+        out_spec = pl.BlockSpec((rows, width), lambda n, place: (0, n))
+        out_shape = jax.ShapeDtypeStruct((rows, chan), BF16)
+    else:
+        kernel, steps, in_specs, operands = weight_kernel, 2, grads + [gated_spec(0), gated_spec(2)], [gated, gated]
+        for piece in added:
+            in_specs += [added_spec(0), added_spec(2)]
+            operands += [piece, piece]
+        out_spec = pl.BlockSpec((2, rows, width), lambda n, place: (0, 0, n))
+        out_shape = jax.ShapeDtypeStruct((2, rows, chan // 2), BF16)
     return pl.pallas_call(
-        weight_kernel,
+        kernel,
         grid_spec=pltpu.PrefetchScalarGridSpec(
-            num_scalar_prefetch=1,
-            grid=(2,),
-            in_specs=[grad_spec(k) for k in range(4)] + [gated_spec(0), gated_spec(2)],
-            out_specs=[out_spec] * 4,
+            num_scalar_prefetch=1, grid=(steps,), in_specs=in_specs, out_specs=[out_spec] * 4
         ),
-        out_shape=[jax.ShapeDtypeStruct((2, rows, chan // 2), BF16)] * 4,
+        out_shape=[out_shape] * 4,
         compiler_params=pltpu.CompilerParams(vmem_limit_bytes=VMEM),
         cost_estimate=pl.CostEstimate(
             flops=8 * rows * chan * seq_len,
@@ -143,7 +176,7 @@
             transcendentals=0,
         ),
         name="weight_kernel",
-    )(place, grad_full, grad_full, grad_full, grad_full, gated, gated)
+    )(place, grad_full, grad_full, grad_full, grad_full, *operands)
 
 
 def product_kernel(count, place_ref, grad_hbm, *refs):
@@ -356,122 +389,143 @@
     pair = ordered(at.x, own_filters, filters_x)
     filters_y = lax.ppermute(pair, "ctx", at.pairs_y)
     plane = ordered(at.y, pair, filters_y)
+    depth = at.depth
     shards = {0: own}
     ring = {0: plane}
+    beside = {1, depth - 1} if depth > 2 else set()
 
     def step_z(held, by, *earlier):
-        way = 1 if by <= at.depth // 2 else -1
-        return lax.ppermute(after(held[(by - way) % at.depth], *earlier), "ctx", at.pairs_z(way))
+        way = 1 if by <= depth // 2 else -1
+        return lax.ppermute(after(held[(by - way) % depth], *earlier), "ctx", at.pairs_z(way))
 
     before = filters_y
     for by in near[1:]:
-        shards[by] = step_z(shards, by, before)
+        shards[by] = before = step_z(shards, by, before)
         if by == near[1]:
             for way in near[1:]:
                 ring[way] = step_z(ring, way, shards[by])
-        before = (shards[by], ring[near[-1]])[by == near[1]]
-    ring = [ring[by] for by in range(at.depth - 1, 0, -1)]
+    ring = [ring[by] for by in range(depth - 1, 0, -1)]
     shards = [shards[by] for by in near]
     ring = jnp.stack((ring + [plane]) * 2)
-    ring = lax.dynamic_slice_in_dim(ring, at.depth - 1 - at.z, at.depth, axis=0)
+    ring = lax.dynamic_slice_in_dim(ring, depth - 1 - at.z, depth, axis=0)
     all_filters = ring.reshape(chan, taps)
     prior = lax.ppermute(after(kv_product[:, seq_len - taps :], shards[1]), "ctx", to_right)
 
     from_x, from_y, diag_a, diag_b = {}, {}, {}, {}
-    kept, summed, carried = {}, {}, {}
-    depth = at.depth
+    kept, carried, crossed, last_sent = {}, {}, [], []
+    mixed = gated = products = w_grad = None
 
     def gather_first(k):
         both = (from_x[0], from_y[0]) if k == 1 else ()
-        from_x[k] = stages.swap_x(shards[k], *(both if k else (filters_x,)))
-        from_y[k] = stages.swap_y(shards[k], *(both if k else (filters_y,)))
+        from_x[k] = stages.swap_x(shards[k], *both)
+        from_y[k] = stages.swap_y(shards[k], *both)
 
     def gather_second(k):
-        diag_a[k] = stages.swap_x(from_y[k][:half])
-        diag_b[k] = stages.swap_y(from_x[k][half:])
+        if near[k] in beside:
+            pairs = at.pairs_z(1 if near[k] == 1 else -1)
+            diag_a[k] = lax.ppermute(diag_a[0], "ctx", pairs)
+            diag_b[k] = lax.ppermute(diag_b[0], "ctx", pairs)
+            stages.finished(diag_a[k], diag_b[k])
+        else:
+            diag_a[k] = stages.swap_x(from_y[k][:half])
+            diag_b[k] = stages.swap_y(from_x[k][half:])
+
+    def mix():
+        nonlocal mixed, gated
+        mixed, gated = run_mix(all_filters, stages.hold(kv_product), prior, gate_values, forward, backward)
+        stages.finished(mixed)
 
     def weight_part(k):
         place = jnp.stack(at.places(far[k])).astype(jnp.int32)
-        kept[k] = run_weight(place, grad_full, stages.hold(gated), rows)
+        added = crossed if far[k] == 0 else ()
+        kept[k] = run_weight(place, grad_full, stages.hold(gated), rows, far[k] in beside, added)
         stages.finished(kept[k][0])
 
     def reduce_first(k):
-        send_a, keep_a, send_b, keep_b = kept[k]
-        kept[k] = (keep_a, stages.swap_x(send_a), keep_b, stages.swap_y(send_b))
+        by = far[k]
+        if by in beside:
+            keep, send_x, send_y, send_z = kept[k]
+            kept[k] = (keep, stages.swap_x(send_x), stages.swap_y(send_y))
+            crossed.append(lax.ppermute(send_z, "ctx", at.pairs_z(1 if by == 1 else -1)))
+        else:
+            send_a, keep_a, send_b, keep_b = kept[k]
+            kept[k] = (keep_a, stages.swap_x(send_a), keep_b, stages.swap_y(send_b))
+            if by == 0:
+                last_sent.extend((kept[k][1], kept[k][3]))
 
     def reduce_second(k):
+        if far[k] in beside:
+            return
         keep_a, got_a, keep_b, got_b = kept[k]
         next_a = (keep_a[1].astype(F32) + got_a[1].astype(F32)).astype(BF16)
         next_b = (keep_b[1].astype(F32) + got_b[1].astype(F32)).astype(BF16)
         kept[k] = (keep_a, got_a, stages.swap_y(next_a), keep_b, got_b, stages.swap_x(next_b))
 
     def reduce_third(k):
-        keep_a, got_a, last_a, keep_b, got_b, last_b = kept.pop(k)
-        sum_a = keep_a[0].astype(F32) + got_a[0].astype(F32) + last_a.astype(F32)
-        sum_b = keep_b[0].astype(F32) + got_b[0].astype(F32) + last_b.astype(F32)
-        joint = jnp.concatenate([sum_a, sum_b], axis=1)
+        nonlocal w_grad
         by = far[k]
+        if by in beside:
+            joint = sum(piece.astype(F32) for piece in kept.pop(k))
+        else:
+            keep_a, got_a, last_a, keep_b, got_b, last_b = kept.pop(k)
+            sum_a = keep_a[0].astype(F32) + got_a[0].astype(F32) + last_a.astype(F32)
+            sum_b = keep_b[0].astype(F32) + got_b[0].astype(F32) + last_b.astype(F32)
+            joint = jnp.concatenate([sum_a, sum_b], axis=1)
         for piece in carried.pop(by, ()):
             joint = joint + piece.astype(F32)
         if by == 0:
-            summed[0] = joint
+            w_grad = joint * norm_scale
             return
         way = 1 if by <= depth // 2 else -1
         got = lax.ppermute(joint.astype(BF16), "ctx", at.pairs_z(way))
         carried.setdefault((by - way) % depth, []).append(got)
-        if k < 2:
+        if k < Z_PINNED:
             stages.finished(got)
-
-    mixed = gated = place = products = None
-
-    def mix():
-        nonlocal mixed, gated
-        mixed, gated = run_mix(all_filters, stages.hold(kv_product), prior, gate_values, forward, backward)
-        stages.finished(mixed)
 
     def product(part):
         nonlocal products
         diag = diag_a if 2 * part < PARTS else diag_b
-        pieces = [p for k in range(at.depth) for p in (shards[k], from_x[k], from_y[k], diag[k])]
+        pieces = [p for k in range(depth) for p in (shards[k], from_x[k], from_y[k], diag[k])]
         places = jnp.stack([c for by in near for c in at.places(-by)]).astype(jnp.int32)
         products = run_product(
             part, places, grad_full, pieces, stages.hold(mixed), gate_values, kv_product, prior,
             all_filters, forward, backward, products or (),
         )
-        stages.finished(*products[3:4])
-
-    depth = at.depth
+        stages.finished(products[3])
+
+    late = depth - 4
     plan = {}
+
+    def at_stage(stage, action, k):
+        plan.setdefault(stage, []).append((action, k))
+
+    at_stage(MIX_STAGE, lambda _: mix(), 0)
     for k in range(depth):
-        plan.setdefault(k, []).append((gather_first, k))
-        plan.setdefault(k + 2, []).append((gather_second, k))
-        plan.setdefault(depth + [0, 1, 2, 2][min(k, 3)] + max(0, k - 3), []).append((reduce_first, k))
-        plan.setdefault(depth + [2, 3, 4, 5][min(k, 3)] + max(0, k - 3), []).append((reduce_second, k))
-    for stage in range(2 * depth + 4 + 0):
-        if stage >= 2 * depth:
+        more = max(0, k - 3)
+        at_stage(WEIGHT_STAGE[min(k, 3)] + more + late, weight_part, k)
+    for k in range(depth):
+        at_stage(THIRD_STAGE[min(k, 3)] + max(0, k - 3) + late, reduce_third, k)
+    for part in range(PARTS):
+        at_stage(PRODUCT_STAGE[part] + 2 * late, lambda p: product(p), part)
+    for k in range(depth):
+        more = max(0, k - 3)
+        at_stage(k, gather_first, k)
+        at_stage(GATHER_SECOND[min(k, 3)] + more, gather_second, k)
+        at_stage(REDUCE_FIRST[min(k, 3)] + more + late, reduce_first, k)
+        at_stage(REDUCE_SECOND[min(k, 3)] + more + late, reduce_second, k)
+    for stage in range(max(plan) + 1):
+        if stage >= CLOSE_STAGE + 2 * late:
             stages.back = 1
-        if stage == 2:
-            mix()
-        for k in range(depth):
-            if stage == (2, 3, 4, 5)[min(k, 3)] + max(0, k - 3):
-                weight_part(k)
-            if stage == depth + [3, 4, 5, 6][min(k, 3)] + max(0, k - 3):
-                reduce_third(k)
-        for part in range(PARTS):
-            if stage == depth + [2, 3][part]:
-                product(part)
         for action, k in plan.get(stage, []):
             action(k)
         stages.advance()
-
-    w_grad = summed[0] * norm_scale
 
     gate_grad, kv_grad, last, head, filt_part = products
     tail = lax.ppermute(head, "ctx", to_left)
     kv_grad = lax.dynamic_update_slice(
         kv_grad, (last + tail.astype(F32)).astype(BF16), (0, seq_len - taps)
     )
-    filter_grad = reduce_filters(at, filt_part, chan_count) * norm_scale
+    filter_grad = reduce_filters(at, after(filt_part, *last_sent), chan_count) * norm_scale
     return (gate_grad, kv_grad, filter_grad.reshape(filters.shape), w_grad)
 
 

time: 373 us -> 351 us (0.941)
  waiting for transfers between devices: 145 us -> 110 us
  starting transfers between devices: 64 us -> 81.1 us
    ppermute x32 -> x24, waiting for transfers between devices: 52.8 us -> 20.2 us  [send(): lax.ppermute(after(array, *self.arrived[-self.back], *self.ready, *earlie...]
    ppermute x3, waiting for transfers between devices: 21 us -> 0.01 us  [reduce_third(): got = lax.ppermute(joint.astype(BF16), 'ctx', at.pairs_z(way))]
    ppermute x6 -> x12, starting transfers between devices: 5.91 us -> 24.3 us  [the longest x2 8.28 us: gather_second(): diag_a[k] = lax.ppermute(diag_a[0], 'ctx', pairs)]
    ppermute x3, waiting for transfers between devices: 0.01 us -> 11.1 us  [reduce_filters(): total = total + lax.ppermute(at_z(by), 'ctx', at.pairs_z(by))]
    ppermute x6 -> x12, waiting for transfers between devices: 56.6 us -> 61.8 us  [the longest x6 45.6 us: step_z(): lax.ppermute(after(held[(by - way) % depth], *earlier), 'ctx', at.pairs_z...]
    ppermute x32 -> x24, starting transfers between devices: 33.8 us -> 34 us  [send(): lax.ppermute(after(array, *self.arrived[-self.back], *self.ready, *earlie...]
  transfers between devices with their start and end apart: 51 -> 49, of which waited for: 18 -> 16; matrix products, arithmetic and copies ran while one was open for 9% -> 7% of each run, Pallas kernels for 30% -> 32%
where the time goes in v3:
time: 351 us; the launch traced here: 350 us
  Pallas kernels  112 us (32%)
  waiting for transfers between devices  110 us (31%)
  starting transfers between devices  81.1 us (23%)
  other arithmetic  21.1 us (6%)
  between operations  14.6 us (4%)
  local copies, waits for them, and re-layouts  10.8 us (3%)
    pallas_call x2, Pallas kernels, run_product(): pl.pallas_call(lambda *refs: product_kernel(count, *refs), grid_spec=pltp...  58.2 us
    ppermute x6, waiting for transfers between devices, step_z(): lax.ppermute(after(held[(by - way) % depth], *earlier), 'ctx', at.pairs_z...  45.6 us
    pallas_call x4, Pallas kernels, run_weight(): pl.pallas_call(kernel, grid_spec=pltpu.PrefetchScalarGridSpec(num_scalar_...  35.6 us
    ppermute x24, starting transfers between devices, send(): lax.ppermute(after(array, *self.arrived[-self.back], *self.ready, *earlie...  34 us
    ppermute x24, waiting for transfers between devices, send(): lax.ppermute(after(array, *self.arrived[-self.back], *self.ready, *earlie...  20.2 us
    pallas_call x1, Pallas kernels, run_mix(): pl.pallas_call(mix_kernel, grid=(chan // group,), in_specs=[rows(taps), r...  18.6 us
    ppermute x2, waiting for transfers between devices, reduce_filters(): got = lax.ppermute(pick(1 - bit, part, axis).astype(BF16), 'ctx', pairs)  12.8 us
    ppermute x3, waiting for transfers between devices, reduce_filters(): total = total + lax.ppermute(at_z(by), 'ctx', at.pairs_z(by))  11.1 us
  transfers between devices with their start and end apart: 49, of which 16 were waited for; matrix products, arithmetic and copies ran while one was open for 7% of the time, Pallas kernels for 32%

profile of v3, /device:TPU:0, one launch (start us, length us, event | category | flops | bytes accessed | tf_op | source)
XLA Modules:
  0.0 350.2 jit_solution(11098108686180094399)
XLA Ops:
  7.9 3.0 collective-permute-start.3
  23.0 19.3 %collective-permute-done.5.refs_6_ = bf16[2048,256]{1,0:T(8,128)(2,1)} collective-permute-done((bf16[2048,256]{1,0:T(8,128)(2,1)S(1)}, bf16[2048,256]{1,0:T(8,128)(2,1)}, u32[]{:S(2)}, u32[]{:S(2)}) %collective-permute-start.5) | collective-permute-done | bytes 1048608 | tf_op jit(solution)/shard_map/ppermute | solution.py:399
  42.3 3.8 %collective-permute-start.14 = (bf16[2,2,128,128]{3,2,1,0:T(8,128)(2,1)}, bf16[2,2,128,128]{3,2,1,0:T(8,128)(2,1)S(1)}, u32[]{:S(2)}, u32[]{:S(2)}) collective-permute-start(bf16[2,2,128,128]{3,2,1,0:T(8,128)(2,1)} %pad_maximum_fusion.1), channel_id=1, source_target_pairs={{0,24},{2,26},{4,28},{6,30},{8,0},{10,2},{12,4},{14,6},{16,8},{18,... | collective-permute-start | bytes 393224 | tf_op jit(solution)/shard_map/ppermute | solution.py:399
  55.7 8.2 %collective-permute-done.16 = bf16[2,2,128,128]{3,2,1,0:T(8,128)(2,1)S(1)} collective-permute-done((bf16[2,2,128,128]{3,2,1,0:T(8,128)(2,1)S(1)}, bf16[2,2,128,128]{3,2,1,0:T(8,128)(2,1)S(1)}, u32[]{:S(2)}, u32[]{:S(2)}) %collective-permute-start.16) | collective-permute-done | bytes 131104 | tf_op jit(solution)/shard_map/ppermute | solution.py:399
  65.0 18.1 %collective-permute-done.9.refs_10_ = bf16[2048,256]{1,0:T(8,128)(2,1)} collective-permute-done((bf16[2048,256]{1,0:T(8,128)(2,1)S(1)}, bf16[2048,256]{1,0:T(8,128)(2,1)}, u32[]{:S(2)}, u32[]{:S(2)}) %collective-permute-start.9) | collective-permute-done | bytes 1048608 | tf_op jit(solution)/shard_map/ppermute | solution.py:399
  84.4 9.7 %collective-permute-start.10 = (bf16[2048,256]{1,0:T(8,128)(2,1)}, bf16[2048,256]{1,0:T(8,128)(2,1)S(1)}, u32[]{:S(2)}, u32[]{:S(2)}) collective-permute-start(bf16[2048,256]{1,0:T(8,128)(2,1)} %collective-permute-done.9.refs_10_), channel_id=1, source_target_pairs={{0,2},{2,0},{4,6},{6,4},{8,10},{10,8},{12,14},{14,12},{16,18},{18,... | collective-permute-start | bytes 3145736 | tf_op jit(solution)/shard_map/ppermute | solution.py:337
  94.9 18.6 %mix_kernel.1 = (bf16[2048,1024]{1,0:T(8,128)(2,1)}, bf16[2048,1024]{1,0:T(8,128)(2,1)}) custom-call(bf16[2048,128]{1,0:T(8,128)(2,1)} %bitcast.132, bf16[2048,1024]{1,0:T(8,128)(2,1)} %refs_20_.3, bf16[2048,128]{1,0:T(8,128)(2,1)} %copy-done.20, bf16[2048,1024]{1,0:T(8,128)(2,1)} %refs_19_.3, bf16[256,256]{1,0:T(8,128)(2,1)} %constant.124.clone.forward_ref.refs_23_, ...), custom_call_target="tpu_custom_call" | custom-call | flops 7516192768 | bytes 16777216 | tf_op jit(solution)/shard_map/mix_kernel/pallas_call | solution.py:103
  113.5 4.4 %collective-permute-start.12 = (bf16[1024,256]{1,0:T(8,128)(2,1)}, bf16[1024,256]{1,0:T(8,128)(2,1)}, u32[]{:S(2)}, u32[]{:S(2)}) collective-permute-start(bf16[1024,256]{1,0:T(8,128)(2,1)} %collective-permute-done.2.refs_5_), channel_id=1, source_target_pairs={{0,24},{2,26},{4,28},{6,30},{8,0},{10,2},{12,4},{14,6},{16,8},{18,... | collective-permute-start | bytes 1572872 | tf_op jit(solution)/shard_map/ppermute | solution.py:427
  118.0 8.6 %weight_kernel.4 = (bf16[2,256,1024]{2,1,0:T(8,128)(2,1)}, bf16[2,256,1024]{2,1,0:T(8,128)(2,1)}, bf16[2,256,1024]{2,1,0:T(8,128)(2,1)}, bf16[2,256,1024]{2,1,0:T(8,128)(2,1)}) custom-call(s32[4]{0:T(128)} %get-tuple-element.133.place_ref, bf16[4096,1024]{1,0:T(8,128)(2,1)} %all-gather.2.cloned.1.call-done.g00.g01.g10.g11.refs_1_, ...), custom_call_target="tpu_custom_call" | custom-call | flops 4294967296 | bytes 10485760 | tf_op jit(solution)/shard_map/weight_kernel/pallas_call | solution.py:166
  130.7 4.4 %collective-permute-start.22 = (bf16[1024,256]{1,0:T(8,128)(2,1)}, bf16[1024,256]{1,0:T(8,128)(2,1)S(1)}, u32[]{:S(2)}, u32[]{:S(2)}) collective-permute-start(bf16[1024,256]{1,0:T(8,128)(2,1)} %collective-permute-done.20.refs_5_), channel_id=1, source_target_pairs={{0,24},{2,26},{4,28},{6,30},{8,0},{10,2},{12,4},{14,6},{16,8},{18,... | collective-permute-start | bytes 1572872 | tf_op jit(solution)/shard_map/ppermute | solution.py:426
  135.1 3.9 %collective-permute-start.21 = (bf16[1024,256]{1,0:T(8,128)(2,1)}, bf16[1024,256]{1,0:T(8,128)(2,1)S(1)}, u32[]{:S(2)}, u32[]{:S(2)}) collective-permute-start(bf16[1024,256]{1,0:T(8,128)(2,1)} %collective-permute-done.20.refs_5_), channel_id=1, source_target_pairs={{0,8},{2,10},{4,12},{6,14},{8,16},{10,18},{12,20},{14,22},{16,24},... | collective-permute-start | bytes 1572872 | tf_op jit(solution)/shard_map/ppermute | solution.py:426
  139.0 2.9 collective-permute-start.18
  141.9 8.8 %weight_kernel.6 = (bf16[256,2048]{1,0:T(8,128)(2,1)}, bf16[256,2048]{1,0:T(8,128)(2,1)}, bf16[256,2048]{1,0:T(8,128)(2,1)}, bf16[256,2048]{1,0:T(8,128)(2,1)}) custom-call(s32[4]{0:T(128)} %pad_add_fusion.2.place_ref, bf16[4096,1024]{1,0:T(8,128)(2,1)} %all-gather.2.cloned.1.call-done.g00.g01.g10.g11.refs_1_, ...), custom_call_target="tpu_custom_call" | custom-call | flops 4294967296 | bytes 10485760 | tf_op jit(solution)/shard_map/weight_kernel/pallas_call | solution.py:166
  150.8 3.1 collective-permute-done.22.refs_13_
  153.8 6.5 %collective-permute-done.21.refs_9_ = bf16[1024,256]{1,0:T(8,128)(2,1)S(1)} collective-permute-done((bf16[1024,256]{1,0:T(8,128)(2,1)}, bf16[1024,256]{1,0:T(8,128)(2,1)S(1)}, u32[]{:S(2)}, u32[]{:S(2)}) %collective-permute-start.21) | collective-permute-done | bytes 524320 | tf_op jit(solution)/shard_map/ppermute | solution.py:426
  164.3 8.8 %weight_kernel.5 = (bf16[256,2048]{1,0:T(8,128)(2,1)}, bf16[256,2048]{1,0:T(8,128)(2,1)}, bf16[256,2048]{1,0:T(8,128)(2,1)}, bf16[256,2048]{1,0:T(8,128)(2,1)}) custom-call(s32[4]{0:T(128)} %get-tuple-element.134.place_ref, bf16[4096,1024]{1,0:T(8,128)(2,1)} %all-gather.2.cloned.1.call-done.g00.g01.g10.g11.refs_1_, ...), custom_call_target="tpu_custom_call" | custom-call | flops 4294967296 | bytes 10485760 | tf_op jit(solution)/shard_map/weight_kernel/pallas_call | solution.py:166
  174.9 5.9 %collective-permute-done.27 = bf16[2,256,1024]{2,1,0:T(8,128)(2,1)S(1)} collective-permute-done((bf16[2,256,1024]{2,1,0:T(8,128)(2,1)}, bf16[2,256,1024]{2,1,0:T(8,128)(2,1)S(1)}, u32[]{:S(2)}, u32[]{:S(2)}) %collective-permute-start.27) | collective-permute-done | bytes 1048608 | tf_op jit(solution)/shard_map/ppermute | solution.py:337
  181.8 5.5 %collective-permute-start.32 = (bf16[256,2048]{1,0:T(8,128)(2,1)}, bf16[256,2048]{1,0:T(8,128)(2,1)S(1)}, u32[]{:S(2)}, u32[]{:S(2)}) collective-permute-start(bf16[256,2048]{1,0:T(8,128)(2,1)} %get-tuple-element.111), channel_id=1, source_target_pairs={{0,24},{2,26},{4,28},{6,30},{8,0},{10,2},{12,4},{14,6},{16,8},{18,... | collective-permute-start | bytes 3145736 | tf_op jit(solution)/shard_map/ppermute | solution.py:449
  189.8 12.9 %collective-permute-done.30 = bf16[256,2048]{1,0:T(8,128)(2,1)} collective-permute-done((bf16[256,2048]{1,0:T(8,128)(2,1)}, bf16[256,2048]{1,0:T(8,128)(2,1)}, u32[]{:S(2)}, u32[]{:S(2)}) %collective-permute-start.30) | collective-permute-done | bytes 1048608 | tf_op jit(solution)/shard_map/ppermute | solution.py:337
  205.1 3.1 add_convert_fusion.1
  211.5 4.2 %collective-permute-done.32.refs_0_.refs_1_ = bf16[256,2048]{1,0:T(8,128)(2,1)S(1)} collective-permute-done((bf16[256,2048]{1,0:T(8,128)(2,1)}, bf16[256,2048]{1,0:T(8,128)(2,1)S(1)}, u32[]{:S(2)}, u32[]{:S(2)}) %collective-permute-start.32) | collective-permute-done | bytes 1048608 | tf_op jit(solution)/shard_map/ppermute | solution.py:449
  216.7 9.4 %weight_kernel.7 = (bf16[2,256,1024]{2,1,0:T(8,128)(2,1)}, bf16[2,256,1024]{2,1,0:T(8,128)(2,1)}, bf16[2,256,1024]{2,1,0:T(8,128)(2,1)}, bf16[2,256,1024]{2,1,0:T(8,128)(2,1)}) custom-call(s32[4]{0:T(128)} %pad_add_fusion.3.place_ref, bf16[4096,1024]{1,0:T(8,128)(2,1)} %all-gather.2.cloned.1.call-done.g00.g01.g10.g11.refs_1_, ...), custom_call_target="tpu_custom_call" | custom-call | flops 4294967296 | bytes 10485760 | tf_op jit(solution)/shard_map/weight_kernel/pallas_call | solution.py:166
  234.8 28.9 %product_kernel.2 = (f32[2048,1024]{1,0:T(8,128)}, bf16[2048,1024]{1,0:T(8,128)(2,1)}, f32[2048,128]{1,0:T(8,128)}, bf16[2048,128]{1,0:T(8,128)(2,1)}, f32[2048,128]{1,0:T(8,128)}) custom-call(s32[16]{0:T(128)} %stack.173.refs_0_, bf16[4096,1024]{1,0:T(8,128)(2,1)} %all-gather.2.cloned.1.call-done.g00.g01.g10.g11.refs_1_, bf16[2048,256]{1,0:T(8,128)(2,1)} %bitcast.130, ...), custom_call_target="tpu_custom_call" | custom-call | flops 12884901888 | bytes 29360128 | tf_op jit(solution)/shard_map/product_kernel/pallas_call | solution.py:262
  264.9 29.3 %product_kernel.3 = (f32[2048,1024]{1,0:T(8,128)}, bf16[2048,1024]{1,0:T(8,128)(2,1)}, f32[2048,128]{1,0:T(8,128)}, bf16[2048,128]{1,0:T(8,128)(2,1)}, f32[2048,128]{1,0:T(8,128)}) custom-call(s32[16]{0:T(128)} %stack.173.refs_0_, ...), custom_call_target="tpu_custom_call", output_to_operand_aliasing={{0}: (25, {}), {1}: (26, {}), {2}: (27, {}), {3}: (28, {}),... | custom-call | flops 12884901888 | bytes 29360128 | tf_op jit(solution)/shard_map/product_kernel/pallas_call | solution.py:262
  296.8 2.7 collective-permute-start.36
  303.4 9.8 %collective-permute-done.36 = bf16[4,2,128,128]{3,2,1,0:T(8,128)(2,1)S(1)} collective-permute-done((bf16[4,2,128,128]{3,2,1,0:T(8,128)(2,1)S(1)}, bf16[4,2,128,128]{3,2,1,0:T(8,128)(2,1)S(1)}, u32[]{:S(2)}, u32[]{:S(2)}) %collective-permute-start.36) | collective-permute-done | bytes 262176 | tf_op jit(solution)/shard_map/ppermute | solution.py:361
  315.4 3.0 collective-permute-done.37
  319.0 2.7 collective-permute-start.46
  322.0 3.3 collective-permute-start.40
  325.3 8.0 %collective-permute-done.38 = f32[128,128]{1,0:T(8,128)S(1)} collective-permute-done((f32[128,128]{1,0:T(8,128)S(1)}, f32[128,128]{1,0:T(8,128)S(1)}, u32[]{:S(2)}, u32[]{:S(2)}) %collective-permute-start.38) | collective-permute-done | bytes 65568 | tf_op jit(solution)/shard_map/ppermute | solution.py:366
  336.1 3.1 collective-permute-done.39
  340.4 3.0 fusion.1
  (166 shorter events, 68.8 us)
Async XLA Ops:
  7.2 110.8 %all-gather.2.cloned.1.call-start = ((), (), s32[]{:S(2)}) async-start(), calls=%async_computation | async-start | bytes 12582912 | tf_op jit(solution)/shard_map/all_gather | solution.py:383
  17.2 25.1 %collective-permute-start.5 = (bf16[2048,256]{1,0:T(8,128)(2,1)S(1)}, bf16[2048,256]{1,0:T(8,128)(2,1)}, u32[]{:S(2)}, u32[]{:S(2)}) collective-permute-start(bf16[2048,256]{1,0:T(8,128)(2,1)S(1)} %bitcast.126), channel_id=1, source_target_pairs={{0,8},{2,10},{4,12},{6,14},{8,16},{10,18},{12,20},{14,22},{16,24},... | collective-permute-start | bytes 3145736 | tf_op jit(solution)/shard_map/ppermute | solution.py:399
  19.3 29.4 %collective-permute-start.1 = (bf16[2048,256]{1,0:T(8,128)(2,1)S(1)}, bf16[2048,256]{1,0:T(8,128)(2,1)S(1)}, u32[]{:S(2)}, u32[]{:S(2)}) collective-permute-start(bf16[2048,256]{1,0:T(8,128)(2,1)S(1)} %bitcast.127), channel_id=1, source_target_pairs={{0,4},{2,6},{4,0},{6,2},{8,12},{10,14},{12,8},{14,10},{16,20},{18,... | collective-permute-start | bytes 3145736 | tf_op jit(solution)/shard_map/ppermute | solution.py:337
  20.8 28.7 %collective-permute-start = (bf16[2048,256]{1,0:T(8,128)(2,1)S(1)}, bf16[2048,256]{1,0:T(8,128)(2,1)S(1)}, u32[]{:S(2)}, u32[]{:S(2)}) collective-permute-start(bf16[2048,256]{1,0:T(8,128)(2,1)S(1)} %bitcast.128), channel_id=1, source_target_pairs={{0,2},{2,0},{4,6},{6,4},{8,10},{10,8},{12,14},{14,12},{16,18},{18,... | collective-permute-start | bytes 3145736 | tf_op jit(solution)/shard_map/ppermute | solution.py:337
  49.6 34.8 %collective-permute-start.2 = (bf16[1024,256]{1,0:T(8,128)(2,1)S(1)}, bf16[1024,256]{1,0:T(8,128)(2,1)}, u32[]{:S(2)}, u32[]{:S(2)}) collective-permute-start(bf16[1024,256]{1,0:T(8,128)(2,1)S(1)} %slice.104), channel_id=1, source_target_pairs={{0,4},{2,6},{4,0},{6,2},{8,12},{10,14},{12,8},{14,10},{16,20},{18,... | collective-permute-start | bytes 1572872 | tf_op jit(solution)/shard_map/ppermute | solution.py:337
  51.2 62.2 %collective-permute-start.7 = (bf16[2048,256]{1,0:T(8,128)(2,1)}, bf16[2048,256]{1,0:T(8,128)(2,1)}, u32[]{:S(2)}, u32[]{:S(2)}) collective-permute-start(bf16[2048,256]{1,0:T(8,128)(2,1)} %collective-permute-done.5.refs_6_), channel_id=1, source_target_pairs={{0,4},{2,6},{4,0},{6,2},{8,12},{10,14},{12,8},{14,10},{16,20},{18,... | collective-permute-start | bytes 3145736 | tf_op jit(solution)/shard_map/ppermute | solution.py:337
  51.7 61.9 %collective-permute-start.6 = (bf16[2048,256]{1,0:T(8,128)(2,1)}, bf16[2048,256]{1,0:T(8,128)(2,1)}, u32[]{:S(2)}, u32[]{:S(2)}) collective-permute-start(bf16[2048,256]{1,0:T(8,128)(2,1)} %collective-permute-done.5.refs_6_), channel_id=1, source_target_pairs={{0,2},{2,0},{4,6},{6,4},{8,10},{10,8},{12,14},{14,12},{16,18},{18,... | collective-permute-start | bytes 3145736 | tf_op jit(solution)/shard_map/ppermute | solution.py:337
  53.2 40.9 %collective-permute-start.17 = (bf16[2048,128]{1,0:T(8,128)(2,1)S(1)}, bf16[2048,128]{1,0:T(8,128)(2,1)S(1)}, u32[]{:S(2)}, u32[]{:S(2)}) collective-permute-start(bf16[2048,128]{1,0:T(8,128)(2,1)S(1)} %copy-done.21), channel_id=1, source_target_pairs={{0,2},{2,4},{4,6},{6,8},{8,10},{10,12},{12,14},{14,16},{16,18},{18... | collective-permute-start | bytes 1572872 | tf_op jit(solution)/shard_map/ppermute | solution.py:412
  83.1 52.0 %collective-permute-start.11 = (bf16[2048,256]{1,0:T(8,128)(2,1)}, bf16[2048,256]{1,0:T(8,128)(2,1)S(1)}, u32[]{:S(2)}, u32[]{:S(2)}) collective-permute-start(bf16[2048,256]{1,0:T(8,128)(2,1)} %collective-permute-done.9.refs_10_), channel_id=1, source_target_pairs={{0,4},{2,6},{4,0},{6,2},{8,12},{10,14},{12,8},{14,10},{16,20},{18,... | collective-permute-start | bytes 3145736 | tf_op jit(solution)/shard_map/ppermute | solution.py:337
  84.4 54.6 %collective-permute-start.10 = (bf16[2048,256]{1,0:T(8,128)(2,1)}, bf16[2048,256]{1,0:T(8,128)(2,1)S(1)}, u32[]{:S(2)}, u32[]{:S(2)}) collective-permute-start(bf16[2048,256]{1,0:T(8,128)(2,1)} %collective-permute-done.9.refs_10_), channel_id=1, source_target_pairs={{0,2},{2,0},{4,6},{6,4},{8,10},{10,8},{12,14},{14,12},{16,18},{18,... | collective-permute-start | bytes 3145736 | tf_op jit(solution)/shard_map/ppermute | solution.py:337
  94.1 32.5 %collective-permute-start.13 = (bf16[2048,256]{1,0:T(8,128)(2,1)}, bf16[2048,256]{1,0:T(8,128)(2,1)S(1)}, u32[]{:S(2)}, u32[]{:S(2)}) collective-permute-start(bf16[2048,256]{1,0:T(8,128)(2,1)} %collective-permute-done.5.refs_6_), channel_id=1, source_target_pairs={{0,8},{2,10},{4,12},{6,14},{8,16},{10,18},{12,20},{14,22},{16,24},... | collective-permute-start | bytes 3145736 | tf_op jit(solution)/shard_map/ppermute | solution.py:399
  127.6 32.8 %collective-permute-start.19 = (bf16[2048,256]{1,0:T(8,128)(2,1)}, bf16[2048,256]{1,0:T(8,128)(2,1)S(1)}, u32[]{:S(2)}, u32[]{:S(2)}) collective-permute-start(bf16[2048,256]{1,0:T(8,128)(2,1)} %copy-done.19), channel_id=1, source_target_pairs={{0,4},{2,6},{4,0},{6,2},{8,12},{10,14},{12,8},{14,10},{16,20},{18,... | collective-permute-start | bytes 3145736 | tf_op jit(solution)/shard_map/ppermute | solution.py:337
  127.6 23.1 %collective-permute-start.8 = (bf16[1024,256]{1,0:T(8,128)(2,1)}, bf16[1024,256]{1,0:T(8,128)(2,1)}, u32[]{:S(2)}, u32[]{:S(2)}) collective-permute-start(bf16[1024,256]{1,0:T(8,128)(2,1)} %collective-permute-done.2.refs_5_), channel_id=1, source_target_pairs={{0,8},{2,10},{4,12},{6,14},{8,16},{10,18},{12,20},{14,22},{16,24},... | collective-permute-start | bytes 1572872 | tf_op jit(solution)/shard_map/ppermute | solution.py:427
  130.7 23.1 %collective-permute-start.22 = (bf16[1024,256]{1,0:T(8,128)(2,1)}, bf16[1024,256]{1,0:T(8,128)(2,1)S(1)}, u32[]{:S(2)}, u32[]{:S(2)}) collective-permute-start(bf16[1024,256]{1,0:T(8,128)(2,1)} %collective-permute-done.20.refs_5_), channel_id=1, source_target_pairs={{0,24},{2,26},{4,28},{6,30},{8,0},{10,2},{12,4},{14,6},{16,8},{18,... | collective-permute-start | bytes 1572872 | tf_op jit(solution)/shard_map/ppermute | solution.py:426
  135.1 25.2 %collective-permute-start.21 = (bf16[1024,256]{1,0:T(8,128)(2,1)}, bf16[1024,256]{1,0:T(8,128)(2,1)S(1)}, u32[]{:S(2)}, u32[]{:S(2)}) collective-permute-start(bf16[1024,256]{1,0:T(8,128)(2,1)} %collective-permute-done.20.refs_5_), channel_id=1, source_target_pairs={{0,8},{2,10},{4,12},{6,14},{8,16},{10,18},{12,20},{14,22},{16,24},... | collective-permute-start | bytes 1572872 | tf_op jit(solution)/shard_map/ppermute | solution.py:426
  139.0 34.1 %collective-permute-start.18 = (bf16[2048,256]{1,0:T(8,128)(2,1)}, bf16[2048,256]{1,0:T(8,128)(2,1)S(1)}, u32[]{:S(2)}, u32[]{:S(2)}) collective-permute-start(bf16[2048,256]{1,0:T(8,128)(2,1)} %copy-done.19), channel_id=1, source_target_pairs={{0,2},{2,0},{4,6},{6,4},{8,10},{10,8},{12,14},{14,12},{16,18},{18,... | collective-permute-start | bytes 3145736 | tf_op jit(solution)/shard_map/ppermute | solution.py:337
  150.7 30.1 %collective-permute-start.27 = (bf16[2,256,1024]{2,1,0:T(8,128)(2,1)}, bf16[2,256,1024]{2,1,0:T(8,128)(2,1)S(1)}, u32[]{:S(2)}, u32[]{:S(2)}) collective-permute-start(bf16[2,256,1024]{2,1,0:T(8,128)(2,1)} %get-tuple-element.92), channel_id=1, source_target_pairs={{0,2},{2,0},{4,6},{6,4},{8,10},{10,8},{12,14},{14,12},{16,18},{18,... | collective-permute-start | bytes 3145736 | tf_op jit(solution)/shard_map/ppermute | solution.py:337
  153.8 34.7 %collective-permute-start.28 = (bf16[2,256,1024]{2,1,0:T(8,128)(2,1)}, bf16[2,256,1024]{2,1,0:T(8,128)(2,1)}, u32[]{:S(2)}, u32[]{:S(2)}) collective-permute-start(bf16[2,256,1024]{2,1,0:T(8,128)(2,1)} %get-tuple-element.94), channel_id=1, source_target_pairs={{0,4},{2,6},{4,0},{6,2},{8,12},{10,14},{12,8},{14,10},{16,20},{18,... | collective-permute-start | bytes 3145736 | tf_op jit(solution)/shard_map/ppermute | solution.py:337
  160.3 42.4 %collective-permute-start.30 = (bf16[256,2048]{1,0:T(8,128)(2,1)}, bf16[256,2048]{1,0:T(8,128)(2,1)}, u32[]{:S(2)}, u32[]{:S(2)}) collective-permute-start(bf16[256,2048]{1,0:T(8,128)(2,1)} %get-tuple-element.98), channel_id=1, source_target_pairs={{0,4},{2,6},{4,0},{6,2},{8,12},{10,14},{12,8},{14,10},{16,20},{18,... | collective-permute-start | bytes 3145736 | tf_op jit(solution)/shard_map/ppermute | solution.py:337
  161.1 44.0 %collective-permute-start.29 = (bf16[256,2048]{1,0:T(8,128)(2,1)}, bf16[256,2048]{1,0:T(8,128)(2,1)}, u32[]{:S(2)}, u32[]{:S(2)}) collective-permute-start(bf16[256,2048]{1,0:T(8,128)(2,1)} %get-tuple-element.96), channel_id=1, source_target_pairs={{0,2},{2,0},{4,6},{6,4},{8,10},{10,8},{12,14},{14,12},{16,18},{18,... | collective-permute-start | bytes 3145736 | tf_op jit(solution)/shard_map/ppermute | solution.py:337
  173.2 36.3 %collective-permute-start.33 = (bf16[256,2048]{1,0:T(8,128)(2,1)}, bf16[256,2048]{1,0:T(8,128)(2,1)S(1)}, u32[]{:S(2)}, u32[]{:S(2)}) collective-permute-start(bf16[256,2048]{1,0:T(8,128)(2,1)} %get-tuple-element.112), channel_id=1, source_target_pairs={{0,8},{2,10},{4,12},{6,14},{8,16},{10,18},{12,20},{14,22},{16,24},... | collective-permute-start | bytes 3145736 | tf_op jit(solution)/shard_map/ppermute | solution.py:449
  181.8 33.9 %collective-permute-start.32 = (bf16[256,2048]{1,0:T(8,128)(2,1)}, bf16[256,2048]{1,0:T(8,128)(2,1)S(1)}, u32[]{:S(2)}, u32[]{:S(2)}) collective-permute-start(bf16[256,2048]{1,0:T(8,128)(2,1)} %get-tuple-element.111), channel_id=1, source_target_pairs={{0,24},{2,26},{4,28},{6,30},{8,0},{10,2},{12,4},{14,6},{16,8},{18,... | collective-permute-start | bytes 3145736 | tf_op jit(solution)/shard_map/ppermute | solution.py:449
  188.6 75.1 %collective-permute-start.23 = (bf16[1024,256]{1,0:T(8,128)(2,1)}, bf16[1024,256]{1,0:T(8,128)(2,1)}, u32[]{:S(2)}, u32[]{:S(2)}) collective-permute-start(bf16[1024,256]{1,0:T(8,128)(2,1)} %slice.105), channel_id=1, source_target_pairs={{0,4},{2,6},{4,0},{6,2},{8,12},{10,14},{12,8},{14,10},{16,20},{18,... | collective-permute-start | bytes 1572872 | tf_op jit(solution)/shard_map/ppermute | solution.py:337
  202.7 30.0 %collective-permute-start.26 = (bf16[1024,256]{1,0:T(8,128)(2,1)}, bf16[1024,256]{1,0:T(8,128)(2,1)}, u32[]{:S(2)}, u32[]{:S(2)}) collective-permute-start(bf16[1024,256]{1,0:T(8,128)(2,1)} %slice.107), channel_id=1, source_target_pairs={{0,2},{2,0},{4,6},{6,4},{8,10},{10,8},{12,14},{14,12},{16,18},{18,... | collective-permute-start | bytes 1572872 | tf_op jit(solution)/shard_map/ppermute | solution.py:337
  209.5 54.2 %collective-permute-start.25 = (bf16[256,2048]{1,0:T(8,128)(2,1)}, bf16[256,2048]{1,0:T(8,128)(2,1)S(1)}, u32[]{:S(2)}, u32[]{:S(2)}) collective-permute-start(bf16[256,2048]{1,0:T(8,128)(2,1)} %get-tuple-element.87), channel_id=1, source_target_pairs={{0,4},{2,6},{4,0},{6,2},{8,12},{10,14},{12,8},{14,10},{16,20},{18,... | collective-permute-start | bytes 3145736 | tf_op jit(solution)/shard_map/ppermute | solution.py:337
  226.1 37.6 %collective-permute-start.24 = (bf16[256,2048]{1,0:T(8,128)(2,1)}, bf16[256,2048]{1,0:T(8,128)(2,1)S(1)}, u32[]{:S(2)}, u32[]{:S(2)}) collective-permute-start(bf16[256,2048]{1,0:T(8,128)(2,1)} %get-tuple-element.85), channel_id=1, source_target_pairs={{0,2},{2,0},{4,6},{6,4},{8,10},{10,8},{12,14},{14,12},{16,18},{18,... | collective-permute-start | bytes 3145736 | tf_op jit(solution)/shard_map/ppermute | solution.py:337
  230.2 88.8 %collective-permute-start.44 = (bf16[256,2048]{1,0:T(8,128)(2,1)}, bf16[256,2048]{1,0:T(8,128)(2,1)}, u32[]{:S(2)}, u32[]{:S(2)}) collective-permute-start(bf16[256,2048]{1,0:T(8,128)(2,1)} %add_convert_fusion.1), channel_id=1, source_target_pairs={{0,24},{2,26},{4,28},{6,30},{8,0},{10,2},{12,4},{14,6},{16,8},{18,... | collective-permute-start | bytes 3145736 | tf_op jit(solution)/shard_map/ppermute | solution.py:480
  232.7 66.8 %collective-permute-start.43 = (bf16[256,2048]{1,0:T(8,128)(2,1)}, bf16[256,2048]{1,0:T(8,128)(2,1)}, u32[]{:S(2)}, u32[]{:S(2)}) collective-permute-start(bf16[256,2048]{1,0:T(8,128)(2,1)} %pad_maximum_fusion), channel_id=1, source_target_pairs={{0,8},{2,10},{4,12},{6,14},{8,16},{10,18},{12,20},{14,22},{16,24},... | collective-permute-start | bytes 3145736 | tf_op jit(solution)/shard_map/ppermute | solution.py:480
  263.7 31.9 %collective-permute-start.34 = (bf16[2,256,1024]{2,1,0:T(8,128)(2,1)}, bf16[2,256,1024]{2,1,0:T(8,128)(2,1)S(1)}, u32[]{:S(2)}, u32[]{:S(2)}) collective-permute-start(bf16[2,256,1024]{2,1,0:T(8,128)(2,1)} %get-tuple-element.114), channel_id=1, source_target_pairs={{0,2},{2,0},{4,6},{6,4},{8,10},{10,8},{12,14},{14,12},{16,18},{18,... | collective-permute-start | bytes 3145736 | tf_op jit(solution)/shard_map/ppermute | solution.py:337
  263.8 31.8 %collective-permute-start.35 = (bf16[2,256,1024]{2,1,0:T(8,128)(2,1)}, bf16[2,256,1024]{2,1,0:T(8,128)(2,1)S(1)}, u32[]{:S(2)}, u32[]{:S(2)}) collective-permute-start(bf16[2,256,1024]{2,1,0:T(8,128)(2,1)} %get-tuple-element.116), channel_id=1, source_target_pairs={{0,4},{2,6},{4,0},{6,2},{8,12},{10,14},{12,8},{14,10},{16,20},{18,... | collective-permute-start | bytes 3145736 | tf_op jit(solution)/shard_map/ppermute | solution.py:337
  294.2 27.8 %collective-permute-start.31 = (bf16[2048,128]{1,0:T(8,128)(2,1)}, bf16[2048,128]{1,0:T(8,128)(2,1)S(1)}, u32[]{:S(2)}, u32[]{:S(2)}) collective-permute-start(bf16[2048,128]{1,0:T(8,128)(2,1)} %get-tuple-element.108), channel_id=1, source_target_pairs={{2,0},{4,2},{6,4},{8,6},{10,8},{12,10},{14,12},{16,14},{18,16},{20... | collective-permute-start | bytes 1572872 | tf_op jit(solution)/shard_map/ppermute | solution.py:524
  301.5 38.9 %collective-permute-start.47 = (bf16[256,2048]{1,0:T(8,128)(2,1)S(1)}, bf16[256,2048]{1,0:T(8,128)(2,1)S(1)}, u32[]{:S(2)}, u32[]{:S(2)}) collective-permute-start(bf16[256,2048]{1,0:T(8,128)(2,1)S(1)} %add_convert_fusion), channel_id=1, source_target_pairs={{0,8},{2,10},{4,12},{6,14},{8,16},{10,18},{12,20},{14,22},{16,24},... | collective-permute-start | bytes 3145736 | tf_op jit(solution)/shard_map/ppermute | solution.py:480
  (42 other events, 552.9 us)
Sparse Core Ops, SparseCore 0:
  9.6 22.5 all-gather.1

commit v4 on v3

--- a/solution.py
+++ b/solution.py
@@ -12,16 +12,16 @@
 F32 = jnp.float32
 BF16 = jnp.bfloat16
 VMEM = 58 * 1024 * 1024
-PARTS = 2
 MIX_STAGE = 2
 WEIGHT_STAGE = (2, 3, 4, 6)
 THIRD_STAGE = (7, 7, 8, 9)
 PRODUCT_STAGE = (6, 7)
-GATHER_SECOND = (2, 4, 4, 5)
+GATHER_SECOND = (2, 3, 4, 5)
 REDUCE_FIRST = (4, 4, 5, 7)
 REDUCE_SECOND = (6, 6, 6, 8)
 CLOSE_STAGE = 8
 Z_PINNED = 2
+PARTS = 2
 
 
 def split_pair(matrix):
@@ -357,14 +357,16 @@
 def reduce_filters(at, part, chan_count):
     taps = part.shape[1]
     part = part.reshape(at.depth, 2, 2, chan_count, taps)
+    first = None
     for bit, pairs, axis in ((at.x, at.pairs_x, 2), (at.y, at.pairs_y, 1)):
         got = lax.ppermute(pick(1 - bit, part, axis).astype(BF16), "ctx", pairs)
+        first = got if first is None else first
         part = pick(bit, part, axis) + got.astype(F32)
     at_z = lambda by: lax.dynamic_index_in_dim(part, (at.z + by) % at.depth, 0, keepdims=False)
     total = at_z(0)
     for by in range(1, at.depth):
         total = total + lax.ppermute(at_z(by), "ctx", at.pairs_z(by))
-    return total
+    return total, first
 
 
 def on_device(out_grad, gate_values, kv_product, w_out, filters):
@@ -401,22 +403,21 @@
     before = filters_y
     for by in near[1:]:
         shards[by] = before = step_z(shards, by, before)
-        if by == near[1]:
-            for way in near[1:]:
-                ring[way] = step_z(ring, way, shards[by])
+    for way in near[1:]:
+        ring[way] = step_z(ring, way, shards[near[min(2, depth - 1)] if way not in beside and depth > 2 else near[1]])
     ring = [ring[by] for by in range(depth - 1, 0, -1)]
     shards = [shards[by] for by in near]
     ring = jnp.stack((ring + [plane]) * 2)
     ring = lax.dynamic_slice_in_dim(ring, depth - 1 - at.z, depth, axis=0)
     all_filters = ring.reshape(chan, taps)
-    prior = lax.ppermute(after(kv_product[:, seq_len - taps :], shards[1]), "ctx", to_right)
+    prior = lax.ppermute(after(kv_product[:, seq_len - taps :], filters_y), "ctx", to_right)
 
     from_x, from_y, diag_a, diag_b = {}, {}, {}, {}
     kept, carried, crossed, last_sent = {}, {}, [], []
     mixed = gated = products = w_grad = None
 
     def gather_first(k):
-        both = (from_x[0], from_y[0]) if k == 1 else ()
+        both = (from_x[0], from_y[0], prior) if k == 1 else ()
         from_x[k] = stages.swap_x(shards[k], *both)
         from_y[k] = stages.swap_y(shards[k], *both)
 
@@ -521,11 +522,12 @@
         stages.advance()
 
     gate_grad, kv_grad, last, head, filt_part = products
-    tail = lax.ppermute(head, "ctx", to_left)
+    filter_grad, crossed_x = reduce_filters(at, after(filt_part, *last_sent), chan_count)
+    filter_grad = filter_grad * norm_scale
+    tail = lax.ppermute(after(head, crossed_x), "ctx", to_left)
     kv_grad = lax.dynamic_update_slice(
         kv_grad, (last + tail.astype(F32)).astype(BF16), (0, seq_len - taps)
     )
-    filter_grad = reduce_filters(at, after(filt_part, *last_sent), chan_count) * norm_scale
     return (gate_grad, kv_grad, filter_grad.reshape(filters.shape), w_grad)
 
 

time: 351 us -> 364 us (1.037)
  the two profiles are of different devices: /device:TPU:0 before, /device:TPU:6 now
where the time goes in v4:
time: 364 us; the launch traced here: 363 us
  waiting for transfers between devices  126 us (35%)
  Pallas kernels  112 us (31%)
  starting transfers between devices  72 us (20%)
  other arithmetic  28 us (8%)
  between operations  14.6 us (4%)
  local copies, waits for them, and re-layouts  9.96 us (3%)
    pallas_call x2, Pallas kernels, run_product(): pl.pallas_call(lambda *refs: product_kernel(count, *refs), grid_spec=pltp...  58.2 us
    ppermute x24, waiting for transfers between devices, send(): lax.ppermute(after(array, *self.arrived[-self.back], *self.ready, *earlie...  39.7 us
    pallas_call x4, Pallas kernels, run_weight(): pl.pallas_call(kernel, grid_spec=pltpu.PrefetchScalarGridSpec(num_scalar_...  35.6 us
    ppermute x6, waiting for transfers between devices, step_z(): lax.ppermute(after(held[(by - way) % depth], *earlier), 'ctx', at.pairs_z...  28.8 us
    ppermute x1, waiting for transfers between devices, on_device(): lax.ppermute(after(kv_product[:, seq_len - taps:], filters_y), 'ctx', to_...  22.3 us
    ppermute x24, starting transfers between devices, send(): lax.ppermute(after(array, *self.arrived[-self.back], *self.ready, *earlie...  21.3 us
    pallas_call x1, Pallas kernels, run_mix(): pl.pallas_call(mix_kernel, grid=(chan // group,), in_specs=[rows(taps), r...  18.6 us
    ppermute x2, starting transfers between devices, gather_second(): diag_a[k] = lax.ppermute(diag_a[0], 'ctx', pairs)  17.6 us
  transfers between devices with their start and end apart: 49, of which 17 were waited for; matrix products, arithmetic and copies ran while one was open for 9% of the time, Pallas kernels for 31%

profile of v4, /device:TPU:6, one launch (start us, length us, event | category | flops | bytes accessed | tf_op | source)
XLA Modules:
  0.0 362.9 jit_solution(10830449055579387155)
XLA Ops:
  8.5 3.4 collective-permute-done.3
  13.0 3.2 collective-permute-done.4
  18.9 22.4 %collective-permute-done.5.refs_6_ = bf16[2048,256]{1,0:T(8,128)(2,1)} collective-permute-done((bf16[2048,256]{1,0:T(8,128)(2,1)S(1)}, bf16[2048,256]{1,0:T(8,128)(2,1)}, u32[]{:S(2)}, u32[]{:S(2)}) %collective-permute-start.5) | collective-permute-done | bytes 1048608 | tf_op jit(solution)/shard_map/ppermute | solution.py:401
  44.4 2.5 collective-permute-start.6
  47.8 3.7 %collective-permute-start.15 = (bf16[2,2,128,128]{3,2,1,0:T(8,128)(2,1)}, bf16[2,2,128,128]{3,2,1,0:T(8,128)(2,1)S(1)}, u32[]{:S(2)}, u32[]{:S(2)}) collective-permute-start(bf16[2,2,128,128]{3,2,1,0:T(8,128)(2,1)} %pad_maximum_fusion.1), channel_id=1, source_target_pairs={{0,24},{2,26},{4,28},{6,30},{8,0},{10,2},{12,4},{14,6},{16,8},{18,... | collective-permute-start | bytes 393224 | tf_op jit(solution)/shard_map/ppermute | solution.py:401
  53.7 22.3 %collective-permute-done.6.prior_ref.refs_21_ = bf16[2048,128]{1,0:T(8,128)(2,1)} collective-permute-done((bf16[2048,128]{1,0:T(8,128)(2,1)}, bf16[2048,128]{1,0:T(8,128)(2,1)}, u32[]{:S(2)}, u32[]{:S(2)}) %collective-permute-start.6) | collective-permute-done | bytes 524320 | tf_op jit(solution)/shard_map/ppermute | solution.py:413
  78.8 2.8 collective-permute-start.17
  81.6 4.3 %collective-permute-done.17 = bf16[2,2,128,128]{3,2,1,0:T(8,128)(2,1)S(1)} collective-permute-done((bf16[2,2,128,128]{3,2,1,0:T(8,128)(2,1)S(1)}, bf16[2,2,128,128]{3,2,1,0:T(8,128)(2,1)S(1)}, u32[]{:S(2)}, u32[]{:S(2)}) %collective-permute-start.17) | collective-permute-done | bytes 131104 | tf_op jit(solution)/shard_map/ppermute | solution.py:401
  88.1 18.6 %mix_kernel.1 = (bf16[2048,1024]{1,0:T(8,128)(2,1)}, bf16[2048,1024]{1,0:T(8,128)(2,1)}) custom-call(bf16[2048,128]{1,0:T(8,128)(2,1)} %bitcast.132, bf16[2048,1024]{1,0:T(8,128)(2,1)} %refs_20_.3, bf16[2048,128]{1,0:T(8,128)(2,1)} %collective-permute-done.6.prior_ref.refs_21_, bf16[2048,1024]{1,0:T(8,128)(2,1)} %refs_19_.3, ...), custom_call_target="tpu_custom_call" | custom-call | flops 7516192768 | bytes 16777216 | tf_op jit(solution)/shard_map/mix_kernel/pallas_call | solution.py:103
  111.4 8.5 %weight_kernel.4 = (bf16[2,256,1024]{2,1,0:T(8,128)(2,1)}, bf16[2,256,1024]{2,1,0:T(8,128)(2,1)}, bf16[2,256,1024]{2,1,0:T(8,128)(2,1)}, bf16[2,256,1024]{2,1,0:T(8,128)(2,1)}) custom-call(s32[4]{0:T(128)} %get-tuple-element.135.place_ref, bf16[4096,1024]{1,0:T(8,128)(2,1)} %all-gather.2.cloned.1.call-done.g00.g01.g10.g11.refs_1_, ...), custom_call_target="tpu_custom_call" | custom-call | flops 4294967296 | bytes 10485760 | tf_op jit(solution)/shard_map/weight_kernel/pallas_call | solution.py:166
  121.0 2.6 collective-permute-done.9.refs_9_
  123.6 3.9 %collective-permute-start.13 = (bf16[1024,256]{1,0:T(8,128)(2,1)}, bf16[1024,256]{1,0:T(8,128)(2,1)S(1)}, u32[]{:S(2)}, u32[]{:S(2)}) collective-permute-start(bf16[1024,256]{1,0:T(8,128)(2,1)} %collective-permute-done.2.refs_5_), channel_id=1, source_target_pairs={{0,24},{2,26},{4,28},{6,30},{8,0},{10,2},{12,4},{14,6},{16,8},{18,... | collective-permute-start | bytes 1572872 | tf_op jit(solution)/shard_map/ppermute | solution.py:428
  127.5 7.5 %collective-permute-done.26.refs_9_ = bf16[1024,256]{1,0:T(8,128)(2,1)S(1)} collective-permute-done((bf16[1024,256]{1,0:T(8,128)(2,1)}, bf16[1024,256]{1,0:T(8,128)(2,1)S(1)}, u32[]{:S(2)}, u32[]{:S(2)}) %collective-permute-start.26) | collective-permute-done | bytes 524320 | tf_op jit(solution)/shard_map/ppermute | solution.py:427
  134.9 16.1 %collective-permute-start.21 = (bf16[1024,256]{1,0:T(8,128)(2,1)}, bf16[1024,256]{1,0:T(8,128)(2,1)S(1)}, u32[]{:S(2)}, u32[]{:S(2)}) collective-permute-start(bf16[1024,256]{1,0:T(8,128)(2,1)} %collective-permute-done.20.refs_5_), channel_id=1, source_target_pairs={{0,24},{2,26},{4,28},{6,30},{8,0},{10,2},{12,4},{14,6},{16,8},{18,... | collective-permute-start | bytes 1572872 | tf_op jit(solution)/shard_map/ppermute | solution.py:427
  152.7 8.8 %weight_kernel.6 = (bf16[256,2048]{1,0:T(8,128)(2,1)}, bf16[256,2048]{1,0:T(8,128)(2,1)}, bf16[256,2048]{1,0:T(8,128)(2,1)}, bf16[256,2048]{1,0:T(8,128)(2,1)}) custom-call(s32[4]{0:T(128)} %pad_add_fusion.2.place_ref, bf16[4096,1024]{1,0:T(8,128)(2,1)} %all-gather.2.cloned.1.call-done.g00.g01.g10.g11.refs_1_, ...), custom_call_target="tpu_custom_call" | custom-call | flops 4294967296 | bytes 10485760 | tf_op jit(solution)/shard_map/weight_kernel/pallas_call | solution.py:166
  162.9 2.0 collective-permute-start.30
  167.9 8.8 %weight_kernel.5 = (bf16[256,2048]{1,0:T(8,128)(2,1)}, bf16[256,2048]{1,0:T(8,128)(2,1)}, bf16[256,2048]{1,0:T(8,128)(2,1)}, bf16[256,2048]{1,0:T(8,128)(2,1)}) custom-call(s32[4]{0:T(128)} %get-tuple-element.136.place_ref, bf16[4096,1024]{1,0:T(8,128)(2,1)} %all-gather.2.cloned.1.call-done.g00.g01.g10.g11.refs_1_, ...), custom_call_target="tpu_custom_call" | custom-call | flops 4294967296 | bytes 10485760 | tf_op jit(solution)/shard_map/weight_kernel/pallas_call | solution.py:166
  179.2 15.5 %collective-permute-done.27 = bf16[2,256,1024]{2,1,0:T(8,128)(2,1)S(1)} collective-permute-done((bf16[2,256,1024]{2,1,0:T(8,128)(2,1)}, bf16[2,256,1024]{2,1,0:T(8,128)(2,1)S(1)}, u32[]{:S(2)}, u32[]{:S(2)}) %collective-permute-start.27) | collective-permute-done | bytes 1048608 | tf_op jit(solution)/shard_map/ppermute | solution.py:337
  195.6 2.0 fusion.6
  197.7 2.4 collective-permute-start.25
  200.1 9.1 %collective-permute-done.29 = bf16[256,2048]{1,0:T(8,128)(2,1)} collective-permute-done((bf16[256,2048]{1,0:T(8,128)(2,1)}, bf16[256,2048]{1,0:T(8,128)(2,1)}, u32[]{:S(2)}, u32[]{:S(2)}) %collective-permute-start.29) | collective-permute-done | bytes 1048608 | tf_op jit(solution)/shard_map/ppermute | solution.py:337
  209.8 3.1 add_convert_fusion.1
  215.7 3.1 collective-permute-done.31.refs_0_.refs_1_
  219.7 9.4 %weight_kernel.7 = (bf16[2,256,1024]{2,1,0:T(8,128)(2,1)}, bf16[2,256,1024]{2,1,0:T(8,128)(2,1)}, bf16[2,256,1024]{2,1,0:T(8,128)(2,1)}, bf16[2,256,1024]{2,1,0:T(8,128)(2,1)}) custom-call(s32[4]{0:T(128)} %pad_add_fusion.3.place_ref, bf16[4096,1024]{1,0:T(8,128)(2,1)} %all-gather.2.cloned.1.call-done.g00.g01.g10.g11.refs_1_, ...), custom_call_target="tpu_custom_call" | custom-call | flops 4294967296 | bytes 10485760 | tf_op jit(solution)/shard_map/weight_kernel/pallas_call | solution.py:166
  236.5 28.9 %product_kernel.2 = (f32[2048,1024]{1,0:T(8,128)}, bf16[2048,1024]{1,0:T(8,128)(2,1)}, f32[2048,128]{1,0:T(8,128)}, bf16[2048,128]{1,0:T(8,128)(2,1)}, f32[2048,128]{1,0:T(8,128)}) custom-call(s32[16]{0:T(128)} %stack.173.refs_0_, bf16[4096,1024]{1,0:T(8,128)(2,1)} %all-gather.2.cloned.1.call-done.g00.g01.g10.g11.refs_1_, bf16[2048,256]{1,0:T(8,128)(2,1)} %bitcast.130, ...), custom_call_target="tpu_custom_call" | custom-call | flops 12884901888 | bytes 29360128 | tf_op jit(solution)/shard_map/product_kernel/pallas_call | solution.py:262
  267.5 29.3 %product_kernel.3 = (f32[2048,1024]{1,0:T(8,128)}, bf16[2048,1024]{1,0:T(8,128)(2,1)}, f32[2048,128]{1,0:T(8,128)}, bf16[2048,128]{1,0:T(8,128)(2,1)}, f32[2048,128]{1,0:T(8,128)}) custom-call(s32[16]{0:T(128)} %stack.173.refs_0_, ...), custom_call_target="tpu_custom_call", output_to_operand_aliasing={{0}: (25, {}), {1}: (26, {}), {2}: (27, {}), {3}: (28, {}),... | custom-call | flops 12884901888 | bytes 29360128 | tf_op jit(solution)/shard_map/product_kernel/pallas_call | solution.py:262
  300.7 3.0 add_convert_fusion
  311.9 4.9 %collective-permute-start.40 = (f32[128,128]{1,0:T(8,128)}, f32[128,128]{1,0:T(8,128)S(1)}, u32[]{:S(2)}, u32[]{:S(2)}) collective-permute-start(f32[128,128]{1,0:T(8,128)} %get-tuple-element.129), channel_id=1, source_target_pairs={{0,24},{2,26},{4,28},{6,30},{8,0},{10,2},{12,4},{14,6},{16,8},{18,... | collective-permute-start | bytes 196616 | tf_op jit(solution)/shard_map/ppermute | solution.py:368
  318.5 11.3 %collective-permute-done.38 = f32[128,128]{1,0:T(8,128)S(1)} collective-permute-done((f32[128,128]{1,0:T(8,128)S(1)}, f32[128,128]{1,0:T(8,128)S(1)}, u32[]{:S(2)}, u32[]{:S(2)}) %collective-permute-start.38) | collective-permute-done | bytes 65568 | tf_op jit(solution)/shard_map/ppermute | solution.py:368
  330.0 3.2 collective-permute-start.36
  336.1 14.3 %collective-permute-done.45 = bf16[256,1024]{1,0:T(8,128)(2,1)} collective-permute-done((bf16[256,1024]{1,0:T(8,128)(2,1)}, bf16[256,1024]{1,0:T(8,128)(2,1)}, u32[]{:S(2)}, u32[]{:S(2)}) %collective-permute-start.45) | collective-permute-done | bytes 524320 | tf_op jit(solution)/shard_map/ppermute | solution.py:337
  351.8 3.4 fusion.1
  (168 shorter events, 64.1 us)
Async XLA Ops:
  7.2 104.2 %all-gather.2.cloned.1.call-start = ((), (), s32[]{:S(2)}) async-start(), calls=%async_computation | async-start | bytes 12582912 | tf_op jit(solution)/shard_map/all_gather | solution.py:385
  17.8 30.0 %collective-permute-start.1 = (bf16[2048,256]{1,0:T(8,128)(2,1)S(1)}, bf16[2048,256]{1,0:T(8,128)(2,1)S(1)}, u32[]{:S(2)}, u32[]{:S(2)}) collective-permute-start(bf16[2048,256]{1,0:T(8,128)(2,1)S(1)} %bitcast.127), channel_id=1, source_target_pairs={{0,4},{2,6},{4,0},{6,2},{8,12},{10,14},{12,8},{14,10},{16,20},{18,... | collective-permute-start | bytes 3145736 | tf_op jit(solution)/shard_map/ppermute | solution.py:337
  18.4 33.9 %collective-permute-start = (bf16[2048,256]{1,0:T(8,128)(2,1)S(1)}, bf16[2048,256]{1,0:T(8,128)(2,1)S(1)}, u32[]{:S(2)}, u32[]{:S(2)}) collective-permute-start(bf16[2048,256]{1,0:T(8,128)(2,1)S(1)} %bitcast.128), channel_id=1, source_target_pairs={{0,2},{2,0},{4,6},{6,4},{8,10},{10,8},{12,14},{14,12},{16,18},{18,... | collective-permute-start | bytes 3145736 | tf_op jit(solution)/shard_map/ppermute | solution.py:337
  41.3 36.1 %collective-permute-start.10 = (bf16[2048,256]{1,0:T(8,128)(2,1)S(1)}, bf16[2048,256]{1,0:T(8,128)(2,1)}, u32[]{:S(2)}, u32[]{:S(2)}) collective-permute-start(bf16[2048,256]{1,0:T(8,128)(2,1)S(1)} %bitcast.129), channel_id=1, source_target_pairs={{0,24},{2,26},{4,28},{6,30},{8,0},{10,2},{12,4},{14,6},{16,8},{18,... | collective-permute-start | bytes 3145736 | tf_op jit(solution)/shard_map/ppermute | solution.py:401
  44.4 31.5 %collective-permute-start.6 = (bf16[2048,128]{1,0:T(8,128)(2,1)}, bf16[2048,128]{1,0:T(8,128)(2,1)}, u32[]{:S(2)}, u32[]{:S(2)}) collective-permute-start(bf16[2048,128]{1,0:T(8,128)(2,1)} %slice.80), channel_id=1, source_target_pairs={{0,2},{2,4},{4,6},{6,8},{8,10},{10,12},{12,14},{14,16},{16,18},{18... | collective-permute-start | bytes 1572872 | tf_op jit(solution)/shard_map/ppermute | solution.py:413
  47.7 29.6 %collective-permute-start.16 = (bf16[2,2,128,128]{3,2,1,0:T(8,128)(2,1)}, bf16[2,2,128,128]{3,2,1,0:T(8,128)(2,1)S(1)}, u32[]{:S(2)}, u32[]{:S(2)}) collective-permute-start(bf16[2,2,128,128]{3,2,1,0:T(8,128)(2,1)} %pad_maximum_fusion.1), channel_id=1, source_target_pairs={{0,8},{2,10},{4,12},{6,14},{8,16},{10,18},{12,20},{14,22},{16,24},... | collective-permute-start | bytes 393224 | tf_op jit(solution)/shard_map/ppermute | solution.py:401
  47.8 30.9 %collective-permute-start.15 = (bf16[2,2,128,128]{3,2,1,0:T(8,128)(2,1)}, bf16[2,2,128,128]{3,2,1,0:T(8,128)(2,1)S(1)}, u32[]{:S(2)}, u32[]{:S(2)}) collective-permute-start(bf16[2,2,128,128]{3,2,1,0:T(8,128)(2,1)} %pad_maximum_fusion.1), channel_id=1, source_target_pairs={{0,24},{2,26},{4,28},{6,30},{8,0},{10,2},{12,4},{14,6},{16,8},{18,... | collective-permute-start | bytes 393224 | tf_op jit(solution)/shard_map/ppermute | solution.py:401
  52.3 35.3 %collective-permute-start.2 = (bf16[1024,256]{1,0:T(8,128)(2,1)S(1)}, bf16[1024,256]{1,0:T(8,128)(2,1)}, u32[]{:S(2)}, u32[]{:S(2)}) collective-permute-start(bf16[1024,256]{1,0:T(8,128)(2,1)S(1)} %slice.104), channel_id=1, source_target_pairs={{0,4},{2,6},{4,0},{6,2},{8,12},{10,14},{12,8},{14,10},{16,20},{18,... | collective-permute-start | bytes 1572872 | tf_op jit(solution)/shard_map/ppermute | solution.py:337
  76.0 30.7 %collective-permute-start.20 = (bf16[1024,256]{1,0:T(8,128)(2,1)S(1)}, bf16[1024,256]{1,0:T(8,128)(2,1)}, u32[]{:S(2)}, u32[]{:S(2)}) collective-permute-start(bf16[1024,256]{1,0:T(8,128)(2,1)S(1)} %slice.106), channel_id=1, source_target_pairs={{0,2},{2,0},{4,6},{6,4},{8,10},{10,8},{12,14},{14,12},{16,18},{18,... | collective-permute-start | bytes 1572872 | tf_op jit(solution)/shard_map/ppermute | solution.py:337
  77.4 30.7 %collective-permute-start.8 = (bf16[2048,256]{1,0:T(8,128)(2,1)}, bf16[2048,256]{1,0:T(8,128)(2,1)}, u32[]{:S(2)}, u32[]{:S(2)}) collective-permute-start(bf16[2048,256]{1,0:T(8,128)(2,1)} %collective-permute-done.5.refs_6_), channel_id=1, source_target_pairs={{0,4},{2,6},{4,0},{6,2},{8,12},{10,14},{12,8},{14,10},{16,20},{18,... | collective-permute-start | bytes 3145736 | tf_op jit(solution)/shard_map/ppermute | solution.py:337
  77.4 32.2 %collective-permute-start.7 = (bf16[2048,256]{1,0:T(8,128)(2,1)}, bf16[2048,256]{1,0:T(8,128)(2,1)}, u32[]{:S(2)}, u32[]{:S(2)}) collective-permute-start(bf16[2048,256]{1,0:T(8,128)(2,1)} %collective-permute-done.5.refs_6_), channel_id=1, source_target_pairs={{0,2},{2,0},{4,6},{6,4},{8,10},{10,8},{12,14},{14,12},{16,18},{18,... | collective-permute-start | bytes 3145736 | tf_op jit(solution)/shard_map/ppermute | solution.py:337
  85.9 34.0 %collective-permute-start.14 = (bf16[2048,256]{1,0:T(8,128)(2,1)}, bf16[2048,256]{1,0:T(8,128)(2,1)}, u32[]{:S(2)}, u32[]{:S(2)}) collective-permute-start(bf16[2048,256]{1,0:T(8,128)(2,1)} %collective-permute-done.5.refs_6_), channel_id=1, source_target_pairs={{0,8},{2,10},{4,12},{6,14},{8,16},{10,18},{12,20},{14,22},{16,24},... | collective-permute-start | bytes 3145736 | tf_op jit(solution)/shard_map/ppermute | solution.py:401
  87.6 63.4 %collective-permute-start.12 = (bf16[2048,256]{1,0:T(8,128)(2,1)}, bf16[2048,256]{1,0:T(8,128)(2,1)}, u32[]{:S(2)}, u32[]{:S(2)}) collective-permute-start(bf16[2048,256]{1,0:T(8,128)(2,1)} %collective-permute-done.10.refs_10_), channel_id=1, source_target_pairs={{0,4},{2,6},{4,0},{6,2},{8,12},{10,14},{12,8},{14,10},{16,20},{18,... | collective-permute-start | bytes 3145736 | tf_op jit(solution)/shard_map/ppermute | solution.py:337
  109.6 51.9 %collective-permute-start.11 = (bf16[2048,256]{1,0:T(8,128)(2,1)}, bf16[2048,256]{1,0:T(8,128)(2,1)S(1)}, u32[]{:S(2)}, u32[]{:S(2)}) collective-permute-start(bf16[2048,256]{1,0:T(8,128)(2,1)} %collective-permute-done.10.refs_10_), channel_id=1, source_target_pairs={{0,2},{2,0},{4,6},{6,4},{8,10},{10,8},{12,14},{14,12},{16,18},{18,... | collective-permute-start | bytes 3145736 | tf_op jit(solution)/shard_map/ppermute | solution.py:337
  119.9 45.0 %collective-permute-start.19 = (bf16[2048,256]{1,0:T(8,128)(2,1)}, bf16[2048,256]{1,0:T(8,128)(2,1)S(1)}, u32[]{:S(2)}, u32[]{:S(2)}) collective-permute-start(bf16[2048,256]{1,0:T(8,128)(2,1)} %collective-permute-done.14.refs_14_), channel_id=1, source_target_pairs={{0,4},{2,6},{4,0},{6,2},{8,12},{10,14},{12,8},{14,10},{16,20},{18,... | collective-permute-start | bytes 3145736 | tf_op jit(solution)/shard_map/ppermute | solution.py:337
  123.6 39.3 %collective-permute-start.13 = (bf16[1024,256]{1,0:T(8,128)(2,1)}, bf16[1024,256]{1,0:T(8,128)(2,1)S(1)}, u32[]{:S(2)}, u32[]{:S(2)}) collective-permute-start(bf16[1024,256]{1,0:T(8,128)(2,1)} %collective-permute-done.2.refs_5_), channel_id=1, source_target_pairs={{0,24},{2,26},{4,28},{6,30},{8,0},{10,2},{12,4},{14,6},{16,8},{18,... | collective-permute-start | bytes 1572872 | tf_op jit(solution)/shard_map/ppermute | solution.py:428
  134.9 28.0 %collective-permute-start.21 = (bf16[1024,256]{1,0:T(8,128)(2,1)}, bf16[1024,256]{1,0:T(8,128)(2,1)S(1)}, u32[]{:S(2)}, u32[]{:S(2)}) collective-permute-start(bf16[1024,256]{1,0:T(8,128)(2,1)} %collective-permute-done.20.refs_5_), channel_id=1, source_target_pairs={{0,24},{2,26},{4,28},{6,30},{8,0},{10,2},{12,4},{14,6},{16,8},{18,... | collective-permute-start | bytes 1572872 | tf_op jit(solution)/shard_map/ppermute | solution.py:427
  162.5 32.2 %collective-permute-start.27 = (bf16[2,256,1024]{2,1,0:T(8,128)(2,1)}, bf16[2,256,1024]{2,1,0:T(8,128)(2,1)S(1)}, u32[]{:S(2)}, u32[]{:S(2)}) collective-permute-start(bf16[2,256,1024]{2,1,0:T(8,128)(2,1)} %get-tuple-element.93), channel_id=1, source_target_pairs={{0,2},{2,0},{4,6},{6,4},{8,10},{10,8},{12,14},{14,12},{16,18},{18,... | collective-permute-start | bytes 3145736 | tf_op jit(solution)/shard_map/ppermute | solution.py:337
  162.9 34.8 %collective-permute-start.28 = (bf16[2,256,1024]{2,1,0:T(8,128)(2,1)}, bf16[2,256,1024]{2,1,0:T(8,128)(2,1)}, u32[]{:S(2)}, u32[]{:S(2)}) collective-permute-start(bf16[2,256,1024]{2,1,0:T(8,128)(2,1)} %get-tuple-element.95), channel_id=1, source_target_pairs={{0,4},{2,6},{4,0},{6,2},{8,12},{10,14},{12,8},{14,10},{16,20},{18,... | collective-permute-start | bytes 3145736 | tf_op jit(solution)/shard_map/ppermute | solution.py:337
  162.9 34.7 %collective-permute-start.30 = (bf16[256,2048]{1,0:T(8,128)(2,1)}, bf16[256,2048]{1,0:T(8,128)(2,1)}, u32[]{:S(2)}, u32[]{:S(2)}) collective-permute-start(bf16[256,2048]{1,0:T(8,128)(2,1)} %get-tuple-element.99), channel_id=1, source_target_pairs={{0,4},{2,6},{4,0},{6,2},{8,12},{10,14},{12,8},{14,10},{16,20},{18,... | collective-permute-start | bytes 3145736 | tf_op jit(solution)/shard_map/ppermute | solution.py:337
  165.0 44.3 %collective-permute-start.29 = (bf16[256,2048]{1,0:T(8,128)(2,1)}, bf16[256,2048]{1,0:T(8,128)(2,1)}, u32[]{:S(2)}, u32[]{:S(2)}) collective-permute-start(bf16[256,2048]{1,0:T(8,128)(2,1)} %get-tuple-element.97), channel_id=1, source_target_pairs={{0,2},{2,0},{4,6},{6,4},{8,10},{10,8},{12,14},{14,12},{16,18},{18,... | collective-permute-start | bytes 3145736 | tf_op jit(solution)/shard_map/ppermute | solution.py:337
  177.4 36.7 %collective-permute-start.32 = (bf16[256,2048]{1,0:T(8,128)(2,1)}, bf16[256,2048]{1,0:T(8,128)(2,1)S(1)}, u32[]{:S(2)}, u32[]{:S(2)}) collective-permute-start(bf16[256,2048]{1,0:T(8,128)(2,1)} %get-tuple-element.113), channel_id=1, source_target_pairs={{0,8},{2,10},{4,12},{6,14},{8,16},{10,18},{12,20},{14,22},{16,24},... | collective-permute-start | bytes 3145736 | tf_op jit(solution)/shard_map/ppermute | solution.py:450
  197.7 67.7 %collective-permute-start.22 = (bf16[1024,256]{1,0:T(8,128)(2,1)}, bf16[1024,256]{1,0:T(8,128)(2,1)}, u32[]{:S(2)}, u32[]{:S(2)}) collective-permute-start(bf16[1024,256]{1,0:T(8,128)(2,1)} %slice.105), channel_id=1, source_target_pairs={{0,4},{2,6},{4,0},{6,2},{8,12},{10,14},{12,8},{14,10},{16,20},{18,... | collective-permute-start | bytes 1572872 | tf_op jit(solution)/shard_map/ppermute | solution.py:337
  197.7 37.5 %collective-permute-start.25 = (bf16[1024,256]{1,0:T(8,128)(2,1)}, bf16[1024,256]{1,0:T(8,128)(2,1)}, u32[]{:S(2)}, u32[]{:S(2)}) collective-permute-start(bf16[1024,256]{1,0:T(8,128)(2,1)} %slice.107), channel_id=1, source_target_pairs={{0,2},{2,0},{4,6},{6,4},{8,10},{10,8},{12,14},{14,12},{16,18},{18,... | collective-permute-start | bytes 1572872 | tf_op jit(solution)/shard_map/ppermute | solution.py:337
  214.1 51.2 %collective-permute-start.24 = (bf16[256,2048]{1,0:T(8,128)(2,1)}, bf16[256,2048]{1,0:T(8,128)(2,1)S(1)}, u32[]{:S(2)}, u32[]{:S(2)}) collective-permute-start(bf16[256,2048]{1,0:T(8,128)(2,1)} %get-tuple-element.88), channel_id=1, source_target_pairs={{0,4},{2,6},{4,0},{6,2},{8,12},{10,14},{12,8},{14,10},{16,20},{18,... | collective-permute-start | bytes 3145736 | tf_op jit(solution)/shard_map/ppermute | solution.py:337
  229.2 36.2 %collective-permute-start.23 = (bf16[256,2048]{1,0:T(8,128)(2,1)}, bf16[256,2048]{1,0:T(8,128)(2,1)S(1)}, u32[]{:S(2)}, u32[]{:S(2)}) collective-permute-start(bf16[256,2048]{1,0:T(8,128)(2,1)} %get-tuple-element.86), channel_id=1, source_target_pairs={{0,2},{2,0},{4,6},{6,4},{8,10},{10,8},{12,14},{14,12},{16,18},{18,... | collective-permute-start | bytes 3145736 | tf_op jit(solution)/shard_map/ppermute | solution.py:337
  231.8 75.9 %collective-permute-start.44 = (bf16[256,2048]{1,0:T(8,128)(2,1)}, bf16[256,2048]{1,0:T(8,128)(2,1)}, u32[]{:S(2)}, u32[]{:S(2)}) collective-permute-start(bf16[256,2048]{1,0:T(8,128)(2,1)} %add_convert_fusion.1), channel_id=1, source_target_pairs={{0,24},{2,26},{4,28},{6,30},{8,0},{10,2},{12,4},{14,6},{16,8},{18,... | collective-permute-start | bytes 3145736 | tf_op jit(solution)/shard_map/ppermute | solution.py:481
  235.2 65.5 %collective-permute-start.43 = (bf16[256,2048]{1,0:T(8,128)(2,1)}, bf16[256,2048]{1,0:T(8,128)(2,1)}, u32[]{:S(2)}, u32[]{:S(2)}) collective-permute-start(bf16[256,2048]{1,0:T(8,128)(2,1)} %pad_maximum_fusion), channel_id=1, source_target_pairs={{0,8},{2,10},{4,12},{6,14},{8,16},{10,18},{12,20},{14,22},{16,24},... | collective-permute-start | bytes 3145736 | tf_op jit(solution)/shard_map/ppermute | solution.py:481
  265.4 31.5 %collective-permute-start.33 = (bf16[2,256,1024]{2,1,0:T(8,128)(2,1)}, bf16[2,256,1024]{2,1,0:T(8,128)(2,1)S(1)}, u32[]{:S(2)}, u32[]{:S(2)}) collective-permute-start(bf16[2,256,1024]{2,1,0:T(8,128)(2,1)} %get-tuple-element.115), channel_id=1, source_target_pairs={{0,2},{2,0},{4,6},{6,4},{8,10},{10,8},{12,14},{14,12},{16,18},{18,... | collective-permute-start | bytes 3145736 | tf_op jit(solution)/shard_map/ppermute | solution.py:337
  266.4 30.4 %collective-permute-start.34 = (bf16[2,256,1024]{2,1,0:T(8,128)(2,1)}, bf16[2,256,1024]{2,1,0:T(8,128)(2,1)S(1)}, u32[]{:S(2)}, u32[]{:S(2)}) collective-permute-start(bf16[2,256,1024]{2,1,0:T(8,128)(2,1)} %get-tuple-element.117), channel_id=1, source_target_pairs={{0,4},{2,6},{4,0},{6,2},{8,12},{10,14},{12,8},{14,10},{16,20},{18,... | collective-permute-start | bytes 3145736 | tf_op jit(solution)/shard_map/ppermute | solution.py:337
  303.7 48.1 %collective-permute-start.47 = (bf16[256,2048]{1,0:T(8,128)(2,1)}, bf16[256,2048]{1,0:T(8,128)(2,1)}, u32[]{:S(2)}, u32[]{:S(2)}) collective-permute-start(bf16[256,2048]{1,0:T(8,128)(2,1)} %add_convert_fusion), channel_id=1, source_target_pairs={{0,8},{2,10},{4,12},{6,14},{8,16},{10,18},{12,20},{14,22},{16,24},... | collective-permute-start | bytes 3145736 | tf_op jit(solution)/shard_map/ppermute | solution.py:481
  307.7 26.9 %collective-permute-start.46 = (bf16[256,1024]{1,0:T(8,128)(2,1)}, bf16[256,1024]{1,0:T(8,128)(2,1)}, u32[]{:S(2)}, u32[]{:S(2)}) collective-permute-start(bf16[256,1024]{1,0:T(8,128)(2,1)} %fusion.8), channel_id=1, source_target_pairs={{0,2},{2,0},{4,6},{6,4},{8,10},{10,8},{12,14},{14,12},{16,18},{18,... | collective-permute-start | bytes 1572872 | tf_op jit(solution)/shard_map/ppermute | solution.py:337
  (43 other events, 679.5 us)
Sparse Core Ops, SparseCore 0:
  9.6 21.2 all-gather.1

commit v5 on v4

--- a/solution.py
+++ b/solution.py
@@ -17,7 +17,7 @@
 THIRD_STAGE = (7, 7, 8, 9)
 PRODUCT_STAGE = (6, 7)
 GATHER_SECOND = (2, 3, 4, 5)
-REDUCE_FIRST = (4, 4, 5, 7)
+REDUCE_FIRST = (4, 5, 5, 7)
 REDUCE_SECOND = (6, 6, 6, 8)
 CLOSE_STAGE = 8
 Z_PINNED = 2
@@ -404,20 +404,20 @@
     for by in near[1:]:
         shards[by] = before = step_z(shards, by, before)
     for way in near[1:]:
-        ring[way] = step_z(ring, way, shards[near[min(2, depth - 1)] if way not in beside and depth > 2 else near[1]])
+        ring[way] = step_z(ring, way, shards[near[min(1, depth - 1)] if way not in beside and depth > 2 else near[1]])
     ring = [ring[by] for by in range(depth - 1, 0, -1)]
     shards = [shards[by] for by in near]
     ring = jnp.stack((ring + [plane]) * 2)
     ring = lax.dynamic_slice_in_dim(ring, depth - 1 - at.z, depth, axis=0)
     all_filters = ring.reshape(chan, taps)
-    prior = lax.ppermute(after(kv_product[:, seq_len - taps :], filters_y), "ctx", to_right)
+    prior = lax.ppermute(after(kv_product[:, seq_len - taps :], shards[1]), "ctx", to_right)
 
     from_x, from_y, diag_a, diag_b = {}, {}, {}, {}
     kept, carried, crossed, last_sent = {}, {}, [], []
     mixed = gated = products = w_grad = None
 
     def gather_first(k):
-        both = (from_x[0], from_y[0], prior) if k == 1 else ()
+        both = (from_x[0], from_y[0]) if k == 1 else ()
         from_x[k] = stages.swap_x(shards[k], *both)
         from_y[k] = stages.swap_y(shards[k], *both)
 
@@ -446,7 +446,8 @@
         by = far[k]
         if by in beside:
             keep, send_x, send_y, send_z = kept[k]
-            kept[k] = (keep, stages.swap_x(send_x), stages.swap_y(send_y))
+            behind = (diag_a[depth - 1], diag_b[depth - 1])
+            kept[k] = (keep, stages.swap_x(send_x, *behind), stages.swap_y(send_y, *behind))
             crossed.append(lax.ppermute(send_z, "ctx", at.pairs_z(1 if by == 1 else -1)))
         else:
             send_a, keep_a, send_b, keep_b = kept[k]
@@ -512,6 +513,8 @@
         more = max(0, k - 3)
         at_stage(k, gather_first, k)
         at_stage(GATHER_SECOND[min(k, 3)] + more, gather_second, k)
+    for k in range(depth):
+        more = max(0, k - 3)
         at_stage(REDUCE_FIRST[min(k, 3)] + more + late, reduce_first, k)
         at_stage(REDUCE_SECOND[min(k, 3)] + more + late, reduce_second, k)
     for stage in range(max(plan) + 1):
@@ -524,7 +527,7 @@
     gate_grad, kv_grad, last, head, filt_part = products
     filter_grad, crossed_x = reduce_filters(at, after(filt_part, *last_sent), chan_count)
     filter_grad = filter_grad * norm_scale
-    tail = lax.ppermute(after(head, crossed_x), "ctx", to_left)
+    tail = lax.ppermute(head, "ctx", to_left)
     kv_grad = lax.dynamic_update_slice(
         kv_grad, (last + tail.astype(F32)).astype(BF16), (0, seq_len - taps)
     )

time: 364 us -> 354 us (0.973)
  the two profiles are of different devices: /device:TPU:6 before, /device:TPU:0 now
where the time goes in v5:
time: 354 us
  waiting for transfers between devices  129 us (36%)
  Pallas kernels  112 us (32%)
  starting transfers between devices  69.2 us (20%)
  other arithmetic  18.2 us (5%)
  between operations  14.6 us (4%)
  local copies, waits for them, and re-layouts  10.4 us (3%)
    ppermute x6, waiting for transfers between devices, step_z(): lax.ppermute(after(held[(by - way) % depth], *earlier), 'ctx', at.pairs_z...  67.7 us
    pallas_call x2, Pallas kernels, run_product(): pl.pallas_call(lambda *refs: product_kernel(count, *refs), grid_spec=pltp...  57.9 us
    pallas_call x4, Pallas kernels, run_weight(): pl.pallas_call(kernel, grid_spec=pltpu.PrefetchScalarGridSpec(num_scalar_...  35.6 us
    ppermute x24, starting transfers between devices, send(): lax.ppermute(after(array, *self.arrived[-self.back], *self.ready, *earlie...  23.7 us
    pallas_call x1, Pallas kernels, run_mix(): pl.pallas_call(mix_kernel, grid=(chan // group,), in_specs=[rows(taps), r...  18.6 us
    ppermute x3, waiting for transfers between devices, reduce_third(): got = lax.ppermute(joint.astype(BF16), 'ctx', at.pairs_z(way))  13.6 us
    ppermute x2, waiting for transfers between devices, reduce_first(): lax.ppermute(send_z, 'ctx', at.pairs_z(1 if by == 1 else -1))  13.5 us
    ppermute x2, waiting for transfers between devices, gather_second(): diag_a[k] = lax.ppermute(diag_a[0], 'ctx', pairs)  10.7 us
  transfers between devices with their start and end apart: 49, of which 16 were waited for; matrix products, arithmetic and copies ran while one was open for 7% of the time, Pallas kernels for 32%

profile of v5, /device:TPU:0, one launch (start us, length us, event | category | flops | bytes accessed | tf_op | source)
XLA Modules:
  0.0 353.6 jit_solution(1361193227883832532)
XLA Ops:
  7.9 3.0 collective-permute-start.3
  12.9 2.1 collective-permute-start.4
  17.2 2.1 collective-permute-start.5
  23.0 19.3 %collective-permute-done.5.refs_6_ = bf16[2048,256]{1,0:T(8,128)(2,1)} collective-permute-done((bf16[2048,256]{1,0:T(8,128)(2,1)S(1)}, bf16[2048,256]{1,0:T(8,128)(2,1)}, u32[]{:S(2)}, u32[]{:S(2)}) %collective-permute-start.5) | collective-permute-done | bytes 1048608 | tf_op jit(solution)/shard_map/ppermute | solution.py:401
  42.3 3.8 %collective-permute-start.14 = (bf16[2,2,128,128]{3,2,1,0:T(8,128)(2,1)}, bf16[2,2,128,128]{3,2,1,0:T(8,128)(2,1)S(1)}, u32[]{:S(2)}, u32[]{:S(2)}) collective-permute-start(bf16[2,2,128,128]{3,2,1,0:T(8,128)(2,1)} %pad_maximum_fusion.1), channel_id=1, source_target_pairs={{0,24},{2,26},{4,28},{6,30},{8,0},{10,2},{12,4},{14,6},{16,8},{18,... | collective-permute-start | bytes 393224 | tf_op jit(solution)/shard_map/ppermute | solution.py:401
  52.9 8.2 %collective-permute-done.16 = bf16[2,2,128,128]{3,2,1,0:T(8,128)(2,1)S(1)} collective-permute-done((bf16[2,2,128,128]{3,2,1,0:T(8,128)(2,1)S(1)}, bf16[2,2,128,128]{3,2,1,0:T(8,128)(2,1)S(1)}, u32[]{:S(2)}, u32[]{:S(2)}) %collective-permute-start.16) | collective-permute-done | bytes 131104 | tf_op jit(solution)/shard_map/ppermute | solution.py:401
  61.2 2.5 collective-permute-done.2.refs_5_
  63.8 3.4 collective-permute-start.17
  68.2 40.2 %collective-permute-done.9.refs_10_ = bf16[2048,256]{1,0:T(8,128)(2,1)} collective-permute-done((bf16[2048,256]{1,0:T(8,128)(2,1)S(1)}, bf16[2048,256]{1,0:T(8,128)(2,1)}, u32[]{:S(2)}, u32[]{:S(2)}) %collective-permute-start.9) | collective-permute-done | bytes 1048608 | tf_op jit(solution)/shard_map/ppermute | solution.py:401
  111.3 18.6 %mix_kernel.1 = (bf16[2048,1024]{1,0:T(8,128)(2,1)}, bf16[2048,1024]{1,0:T(8,128)(2,1)}) custom-call(bf16[2048,128]{1,0:T(8,128)(2,1)} %bitcast.132, bf16[2048,1024]{1,0:T(8,128)(2,1)} %refs_20_.3, bf16[2048,128]{1,0:T(8,128)(2,1)} %copy-done.18, bf16[2048,1024]{1,0:T(8,128)(2,1)} %refs_19_.3, bf16[256,256]{1,0:T(8,128)(2,1)} %constant.124.clone.forward_ref.refs_23_, ...), custom_call_target="tpu_custom_call" | custom-call | flops 7516192768 | bytes 16777216 | tf_op jit(solution)/shard_map/mix_kernel/pallas_call | solution.py:103
  129.8 8.7 %weight_kernel.4 = (bf16[2,256,1024]{2,1,0:T(8,128)(2,1)}, bf16[2,256,1024]{2,1,0:T(8,128)(2,1)}, bf16[2,256,1024]{2,1,0:T(8,128)(2,1)}, bf16[2,256,1024]{2,1,0:T(8,128)(2,1)}) custom-call(s32[4]{0:T(128)} %get-tuple-element.133.place_ref, bf16[4096,1024]{1,0:T(8,128)(2,1)} %all-gather.2.cloned.1.call-done.g00.g01.g10.g11.refs_1_, ...), custom_call_target="tpu_custom_call" | custom-call | flops 4294967296 | bytes 10485760 | tf_op jit(solution)/shard_map/weight_kernel/pallas_call | solution.py:166
  140.6 3.8 %collective-permute-start.12 = (bf16[1024,256]{1,0:T(8,128)(2,1)}, bf16[1024,256]{1,0:T(8,128)(2,1)S(1)}, u32[]{:S(2)}, u32[]{:S(2)}) collective-permute-start(bf16[1024,256]{1,0:T(8,128)(2,1)} %collective-permute-done.2.refs_5_), channel_id=1, source_target_pairs={{0,24},{2,26},{4,28},{6,30},{8,0},{10,2},{12,4},{14,6},{16,8},{18,... | collective-permute-start | bytes 1572872 | tf_op jit(solution)/shard_map/ppermute | solution.py:428
  145.2 8.7 %weight_kernel.6 = (bf16[256,2048]{1,0:T(8,128)(2,1)}, bf16[256,2048]{1,0:T(8,128)(2,1)}, bf16[256,2048]{1,0:T(8,128)(2,1)}, bf16[256,2048]{1,0:T(8,128)(2,1)}) custom-call(s32[4]{0:T(128)} %pad_add_fusion.2.place_ref, bf16[4096,1024]{1,0:T(8,128)(2,1)} %all-gather.2.cloned.1.call-done.g00.g01.g10.g11.refs_1_, ...), custom_call_target="tpu_custom_call" | custom-call | flops 4294967296 | bytes 10485760 | tf_op jit(solution)/shard_map/weight_kernel/pallas_call | solution.py:166
  158.8 8.8 %weight_kernel.5 = (bf16[256,2048]{1,0:T(8,128)(2,1)}, bf16[256,2048]{1,0:T(8,128)(2,1)}, bf16[256,2048]{1,0:T(8,128)(2,1)}, bf16[256,2048]{1,0:T(8,128)(2,1)}) custom-call(s32[4]{0:T(128)} %get-tuple-element.134.place_ref, bf16[4096,1024]{1,0:T(8,128)(2,1)} %all-gather.2.cloned.1.call-done.g00.g01.g10.g11.refs_1_, ...), custom_call_target="tpu_custom_call" | custom-call | flops 4294967296 | bytes 10485760 | tf_op jit(solution)/shard_map/weight_kernel/pallas_call | solution.py:166
  167.6 10.7 %collective-permute-done.21.refs_13_ = bf16[1024,256]{1,0:T(8,128)(2,1)S(1)} collective-permute-done((bf16[1024,256]{1,0:T(8,128)(2,1)}, bf16[1024,256]{1,0:T(8,128)(2,1)S(1)}, u32[]{:S(2)}, u32[]{:S(2)}) %collective-permute-start.21) | collective-permute-done | bytes 524320 | tf_op jit(solution)/shard_map/ppermute | solution.py:427
  179.1 3.3 collective-permute-start.32
  189.6 3.7 %collective-permute-done.29 = bf16[2,256,1024]{2,1,0:T(8,128)(2,1)} collective-permute-done((bf16[2,256,1024]{2,1,0:T(8,128)(2,1)}, bf16[2,256,1024]{2,1,0:T(8,128)(2,1)}, u32[]{:S(2)}, u32[]{:S(2)}) %collective-permute-start.29) | collective-permute-done | bytes 1048608 | tf_op jit(solution)/shard_map/ppermute | solution.py:337
  194.1 2.0 fusion.6
  196.1 2.8 collective-permute-done.33.refs_2_.refs_3_
  198.9 10.8 %collective-permute-done.32.refs_0_.refs_1_ = bf16[256,2048]{1,0:T(8,128)(2,1)S(1)} collective-permute-done((bf16[256,2048]{1,0:T(8,128)(2,1)}, bf16[256,2048]{1,0:T(8,128)(2,1)S(1)}, u32[]{:S(2)}, u32[]{:S(2)}) %collective-permute-start.32) | collective-permute-done | bytes 1048608 | tf_op jit(solution)/shard_map/ppermute | solution.py:451
  210.7 9.4 %weight_kernel.7 = (bf16[2,256,1024]{2,1,0:T(8,128)(2,1)}, bf16[2,256,1024]{2,1,0:T(8,128)(2,1)}, bf16[2,256,1024]{2,1,0:T(8,128)(2,1)}, bf16[2,256,1024]{2,1,0:T(8,128)(2,1)}) custom-call(s32[4]{0:T(128)} %pad_add_fusion.3.place_ref, bf16[4096,1024]{1,0:T(8,128)(2,1)} %all-gather.2.cloned.1.call-done.g00.g01.g10.g11.refs_1_, ...), custom_call_target="tpu_custom_call" | custom-call | flops 4294967296 | bytes 10485760 | tf_op jit(solution)/shard_map/weight_kernel/pallas_call | solution.py:166
  228.1 28.9 %product_kernel.2 = (f32[2048,1024]{1,0:T(8,128)}, bf16[2048,1024]{1,0:T(8,128)(2,1)}, f32[2048,128]{1,0:T(8,128)}, bf16[2048,128]{1,0:T(8,128)(2,1)}, f32[2048,128]{1,0:T(8,128)}) custom-call(s32[16]{0:T(128)} %stack.173.refs_0_, bf16[4096,1024]{1,0:T(8,128)(2,1)} %all-gather.2.cloned.1.call-done.g00.g01.g10.g11.refs_1_, bf16[2048,256]{1,0:T(8,128)(2,1)} %bitcast.130, ...), custom_call_target="tpu_custom_call" | custom-call | flops 12884901888 | bytes 29360128 | tf_op jit(solution)/shard_map/product_kernel/pallas_call | solution.py:262
  257.7 4.6 %collective-permute-start.47 = (bf16[256,2048]{1,0:T(8,128)(2,1)S(1)}, bf16[256,2048]{1,0:T(8,128)(2,1)S(1)}, u32[]{:S(2)}, u32[]{:S(2)}) collective-permute-start(bf16[256,2048]{1,0:T(8,128)(2,1)S(1)} %add_convert_fusion), channel_id=1, source_target_pairs={{0,8},{2,10},{4,12},{6,14},{8,16},{10,18},{12,20},{14,22},{16,24},... | collective-permute-start | bytes 3145736 | tf_op jit(solution)/shard_map/ppermute | solution.py:482
  262.4 4.1 %collective-permute-done.25 = bf16[256,2048]{1,0:T(8,128)(2,1)} collective-permute-done((bf16[256,2048]{1,0:T(8,128)(2,1)}, bf16[256,2048]{1,0:T(8,128)(2,1)}, u32[]{:S(2)}, u32[]{:S(2)}) %collective-permute-start.25) | collective-permute-done | bytes 1048608 | tf_op jit(solution)/shard_map/ppermute | solution.py:337
  270.0 29.1 %product_kernel.3 = (f32[2048,1024]{1,0:T(8,128)}, bf16[2048,1024]{1,0:T(8,128)(2,1)}, f32[2048,128]{1,0:T(8,128)}, bf16[2048,128]{1,0:T(8,128)(2,1)}, f32[2048,128]{1,0:T(8,128)}) custom-call(s32[16]{0:T(128)} %stack.173.refs_0_, ...), custom_call_target="tpu_custom_call", output_to_operand_aliasing={{0}: (25, {}), {1}: (26, {}), {2}: (27, {}), {3}: (28, {}),... | custom-call | flops 12884901888 | bytes 29360128 | tf_op jit(solution)/shard_map/product_kernel/pallas_call | solution.py:262
  300.7 2.2 add_convert_fusion.1
  302.9 3.0 collective-permute-start.44
  309.1 2.1 collective-permute-start.37
  311.4 2.8 collective-permute-done.37
  316.2 13.6 %collective-permute-done.44 = bf16[256,2048]{1,0:T(8,128)(2,1)S(1)} collective-permute-done((bf16[256,2048]{1,0:T(8,128)(2,1)S(1)}, bf16[256,2048]{1,0:T(8,128)(2,1)S(1)}, u32[]{:S(2)}, u32[]{:S(2)}) %collective-permute-start.44) | collective-permute-done | bytes 1048608 | tf_op jit(solution)/shard_map/ppermute | solution.py:482
  332.9 7.3 %collective-permute-start.39 = (f32[128,128]{1,0:T(8,128)S(1)}, f32[128,128]{1,0:T(8,128)S(1)}, u32[]{:S(2)}, u32[]{:S(2)}) collective-permute-start(f32[128,128]{1,0:T(8,128)S(1)} %get-tuple-element.128), channel_id=1, source_target_pairs={{0,16},{2,18},{4,20},{6,22},{8,24},{10,26},{12,28},{14,30},{16,0},... | collective-permute-start | bytes 196616 | tf_op jit(solution)/shard_map/ppermute | solution.py:368
  341.0 2.7 collective-permute-done.39
  (166 shorter events, 62.8 us)
Async XLA Ops:
  7.2 122.7 %all-gather.2.cloned.1.call-start = ((), (), s32[]{:S(2)}) async-start(), calls=%async_computation | async-start | bytes 12582912 | tf_op jit(solution)/shard_map/all_gather | solution.py:385
  17.2 25.1 %collective-permute-start.5 = (bf16[2048,256]{1,0:T(8,128)(2,1)S(1)}, bf16[2048,256]{1,0:T(8,128)(2,1)}, u32[]{:S(2)}, u32[]{:S(2)}) collective-permute-start(bf16[2048,256]{1,0:T(8,128)(2,1)S(1)} %bitcast.126), channel_id=1, source_target_pairs={{0,8},{2,10},{4,12},{6,14},{8,16},{10,18},{12,20},{14,22},{16,24},... | collective-permute-start | bytes 3145736 | tf_op jit(solution)/shard_map/ppermute | solution.py:401
  19.3 29.4 %collective-permute-start.1 = (bf16[2048,256]{1,0:T(8,128)(2,1)S(1)}, bf16[2048,256]{1,0:T(8,128)(2,1)S(1)}, u32[]{:S(2)}, u32[]{:S(2)}) collective-permute-start(bf16[2048,256]{1,0:T(8,128)(2,1)S(1)} %bitcast.127), channel_id=1, source_target_pairs={{0,4},{2,6},{4,0},{6,2},{8,12},{10,14},{12,8},{14,10},{16,20},{18,... | collective-permute-start | bytes 3145736 | tf_op jit(solution)/shard_map/ppermute | solution.py:337
  20.8 27.9 %collective-permute-start = (bf16[2048,256]{1,0:T(8,128)(2,1)S(1)}, bf16[2048,256]{1,0:T(8,128)(2,1)S(1)}, u32[]{:S(2)}, u32[]{:S(2)}) collective-permute-start(bf16[2048,256]{1,0:T(8,128)(2,1)S(1)} %bitcast.128), channel_id=1, source_target_pairs={{0,2},{2,0},{4,6},{6,4},{8,10},{10,8},{12,14},{14,12},{16,18},{18,... | collective-permute-start | bytes 3145736 | tf_op jit(solution)/shard_map/ppermute | solution.py:337
  51.9 57.9 %collective-permute-start.7 = (bf16[2048,256]{1,0:T(8,128)(2,1)}, bf16[2048,256]{1,0:T(8,128)(2,1)}, u32[]{:S(2)}, u32[]{:S(2)}) collective-permute-start(bf16[2048,256]{1,0:T(8,128)(2,1)} %collective-permute-done.5.refs_6_), channel_id=1, source_target_pairs={{0,4},{2,6},{4,0},{6,2},{8,12},{10,14},{12,8},{14,10},{16,20},{18,... | collective-permute-start | bytes 3145736 | tf_op jit(solution)/shard_map/ppermute | solution.py:337
  52.4 58.9 %collective-permute-start.6 = (bf16[2048,256]{1,0:T(8,128)(2,1)}, bf16[2048,256]{1,0:T(8,128)(2,1)}, u32[]{:S(2)}, u32[]{:S(2)}) collective-permute-start(bf16[2048,256]{1,0:T(8,128)(2,1)} %collective-permute-done.5.refs_6_), channel_id=1, source_target_pairs={{0,2},{2,0},{4,6},{6,4},{8,10},{10,8},{12,14},{14,12},{16,18},{18,... | collective-permute-start | bytes 3145736 | tf_op jit(solution)/shard_map/ppermute | solution.py:337
  61.1 47.2 %collective-permute-start.9 = (bf16[2048,256]{1,0:T(8,128)(2,1)S(1)}, bf16[2048,256]{1,0:T(8,128)(2,1)}, u32[]{:S(2)}, u32[]{:S(2)}) collective-permute-start(bf16[2048,256]{1,0:T(8,128)(2,1)S(1)} %bitcast.129), channel_id=1, source_target_pairs={{0,24},{2,26},{4,28},{6,30},{8,0},{10,2},{12,4},{14,6},{16,8},{18,... | collective-permute-start | bytes 3145736 | tf_op jit(solution)/shard_map/ppermute | solution.py:401
  63.8 44.6 %collective-permute-start.17 = (bf16[2048,128]{1,0:T(8,128)(2,1)S(1)}, bf16[2048,128]{1,0:T(8,128)(2,1)S(1)}, u32[]{:S(2)}, u32[]{:S(2)}) collective-permute-start(bf16[2048,128]{1,0:T(8,128)(2,1)S(1)} %copy-done.22), channel_id=1, source_target_pairs={{0,2},{2,4},{4,6},{6,8},{8,10},{10,12},{12,14},{14,16},{16,18},{18... | collective-permute-start | bytes 1572872 | tf_op jit(solution)/shard_map/ppermute | solution.py:413
  68.2 72.4 %collective-permute-start.8 = (bf16[1024,256]{1,0:T(8,128)(2,1)}, bf16[1024,256]{1,0:T(8,128)(2,1)}, u32[]{:S(2)}, u32[]{:S(2)}) collective-permute-start(bf16[1024,256]{1,0:T(8,128)(2,1)} %collective-permute-done.2.refs_5_), channel_id=1, source_target_pairs={{0,8},{2,10},{4,12},{6,14},{8,16},{10,18},{12,20},{14,22},{16,24},... | collective-permute-start | bytes 1572872 | tf_op jit(solution)/shard_map/ppermute | solution.py:428
  108.4 36.1 %collective-permute-start.28 = (bf16[1024,256]{1,0:T(8,128)(2,1)}, bf16[1024,256]{1,0:T(8,128)(2,1)}, u32[]{:S(2)}, u32[]{:S(2)}) collective-permute-start(bf16[1024,256]{1,0:T(8,128)(2,1)} %collective-permute-done.20.refs_5_), channel_id=1, source_target_pairs={{0,8},{2,10},{4,12},{6,14},{8,16},{10,18},{12,20},{14,22},{16,24},... | collective-permute-start | bytes 1572872 | tf_op jit(solution)/shard_map/ppermute | solution.py:427
  108.4 45.6 %collective-permute-start.11 = (bf16[2048,256]{1,0:T(8,128)(2,1)}, bf16[2048,256]{1,0:T(8,128)(2,1)S(1)}, u32[]{:S(2)}, u32[]{:S(2)}) collective-permute-start(bf16[2048,256]{1,0:T(8,128)(2,1)} %collective-permute-done.9.refs_10_), channel_id=1, source_target_pairs={{0,4},{2,6},{4,0},{6,2},{8,12},{10,14},{12,8},{14,10},{16,20},{18,... | collective-permute-start | bytes 3145736 | tf_op jit(solution)/shard_map/ppermute | solution.py:337
  109.7 44.2 %collective-permute-start.10 = (bf16[2048,256]{1,0:T(8,128)(2,1)}, bf16[2048,256]{1,0:T(8,128)(2,1)S(1)}, u32[]{:S(2)}, u32[]{:S(2)}) collective-permute-start(bf16[2048,256]{1,0:T(8,128)(2,1)} %collective-permute-done.9.refs_10_), channel_id=1, source_target_pairs={{0,2},{2,0},{4,6},{6,4},{8,10},{10,8},{12,14},{14,12},{16,18},{18,... | collective-permute-start | bytes 3145736 | tf_op jit(solution)/shard_map/ppermute | solution.py:337
  111.2 27.3 %collective-permute-start.13 = (bf16[2048,256]{1,0:T(8,128)(2,1)}, bf16[2048,256]{1,0:T(8,128)(2,1)S(1)}, u32[]{:S(2)}, u32[]{:S(2)}) collective-permute-start(bf16[2048,256]{1,0:T(8,128)(2,1)} %collective-permute-done.5.refs_6_), channel_id=1, source_target_pairs={{0,8},{2,10},{4,12},{6,14},{8,16},{10,18},{12,20},{14,22},{16,24},... | collective-permute-start | bytes 3145736 | tf_op jit(solution)/shard_map/ppermute | solution.py:401
  139.5 38.8 %collective-permute-start.19 = (bf16[2048,256]{1,0:T(8,128)(2,1)}, bf16[2048,256]{1,0:T(8,128)(2,1)S(1)}, u32[]{:S(2)}, u32[]{:S(2)}) collective-permute-start(bf16[2048,256]{1,0:T(8,128)(2,1)} %copy-done.17), channel_id=1, source_target_pairs={{0,4},{2,6},{4,0},{6,2},{8,12},{10,14},{12,8},{14,10},{16,20},{18,... | collective-permute-start | bytes 3145736 | tf_op jit(solution)/shard_map/ppermute | solution.py:337
  144.4 40.1 %collective-permute-start.18 = (bf16[2048,256]{1,0:T(8,128)(2,1)}, bf16[2048,256]{1,0:T(8,128)(2,1)}, u32[]{:S(2)}, u32[]{:S(2)}) collective-permute-start(bf16[2048,256]{1,0:T(8,128)(2,1)} %copy-done.17), channel_id=1, source_target_pairs={{0,2},{2,0},{4,6},{6,4},{8,10},{10,8},{12,14},{14,12},{16,18},{18,... | collective-permute-start | bytes 3145736 | tf_op jit(solution)/shard_map/ppermute | solution.py:337
  154.0 32.4 %collective-permute-start.30 = (bf16[2,256,1024]{2,1,0:T(8,128)(2,1)}, bf16[2,256,1024]{2,1,0:T(8,128)(2,1)}, u32[]{:S(2)}, u32[]{:S(2)}) collective-permute-start(bf16[2,256,1024]{2,1,0:T(8,128)(2,1)} %get-tuple-element.98), channel_id=1, source_target_pairs={{0,4},{2,6},{4,0},{6,2},{8,12},{10,14},{12,8},{14,10},{16,20},{18,... | collective-permute-start | bytes 3145736 | tf_op jit(solution)/shard_map/ppermute | solution.py:337
  157.3 36.0 %collective-permute-start.29 = (bf16[2,256,1024]{2,1,0:T(8,128)(2,1)}, bf16[2,256,1024]{2,1,0:T(8,128)(2,1)}, u32[]{:S(2)}, u32[]{:S(2)}) collective-permute-start(bf16[2,256,1024]{2,1,0:T(8,128)(2,1)} %get-tuple-element.96), channel_id=1, source_target_pairs={{0,2},{2,0},{4,6},{6,4},{8,10},{10,8},{12,14},{14,12},{16,18},{18,... | collective-permute-start | bytes 3145736 | tf_op jit(solution)/shard_map/ppermute | solution.py:337
  179.1 30.5 %collective-permute-start.32 = (bf16[256,2048]{1,0:T(8,128)(2,1)}, bf16[256,2048]{1,0:T(8,128)(2,1)S(1)}, u32[]{:S(2)}, u32[]{:S(2)}) collective-permute-start(bf16[256,2048]{1,0:T(8,128)(2,1)} %get-tuple-element.111), channel_id=1, source_target_pairs={{0,24},{2,26},{4,28},{6,30},{8,0},{10,2},{12,4},{14,6},{16,8},{18,... | collective-permute-start | bytes 3145736 | tf_op jit(solution)/shard_map/ppermute | solution.py:451
  186.4 33.7 %collective-permute-start.22 = (bf16[1024,256]{1,0:T(8,128)(2,1)}, bf16[1024,256]{1,0:T(8,128)(2,1)S(1)}, u32[]{:S(2)}, u32[]{:S(2)}) collective-permute-start(bf16[1024,256]{1,0:T(8,128)(2,1)} %slice.105), channel_id=1, source_target_pairs={{0,4},{2,6},{4,0},{6,2},{8,12},{10,14},{12,8},{14,10},{16,20},{18,... | collective-permute-start | bytes 1572872 | tf_op jit(solution)/shard_map/ppermute | solution.py:337
  186.4 33.7 %collective-permute-start.23 = (bf16[1024,256]{1,0:T(8,128)(2,1)}, bf16[1024,256]{1,0:T(8,128)(2,1)}, u32[]{:S(2)}, u32[]{:S(2)}) collective-permute-start(bf16[1024,256]{1,0:T(8,128)(2,1)} %slice.107), channel_id=1, source_target_pairs={{0,2},{2,0},{4,6},{6,4},{8,10},{10,8},{12,14},{14,12},{16,18},{18,... | collective-permute-start | bytes 1572872 | tf_op jit(solution)/shard_map/ppermute | solution.py:337
  193.3 29.5 %collective-permute-start.42 = (bf16[256,1024]{1,0:T(8,128)(2,1)}, bf16[256,1024]{1,0:T(8,128)(2,1)}, u32[]{:S(2)}, u32[]{:S(2)}) collective-permute-start(bf16[256,1024]{1,0:T(8,128)(2,1)} %fusion.7), channel_id=1, source_target_pairs={{0,2},{2,0},{4,6},{6,4},{8,10},{10,8},{12,14},{14,12},{16,18},{18,... | collective-permute-start | bytes 1572872 | tf_op jit(solution)/shard_map/ppermute | solution.py:337
  198.9 25.4 %collective-permute-start.41 = (bf16[256,1024]{1,0:T(8,128)(2,1)}, bf16[256,1024]{1,0:T(8,128)(2,1)}, u32[]{:S(2)}, u32[]{:S(2)}) collective-permute-start(bf16[256,1024]{1,0:T(8,128)(2,1)} %fusion.6), channel_id=1, source_target_pairs={{0,4},{2,6},{4,0},{6,2},{8,12},{10,14},{12,8},{14,10},{16,20},{18,... | collective-permute-start | bytes 1572872 | tf_op jit(solution)/shard_map/ppermute | solution.py:337
  220.8 36.1 %collective-permute-start.26 = (bf16[256,2048]{1,0:T(8,128)(2,1)}, bf16[256,2048]{1,0:T(8,128)(2,1)S(1)}, u32[]{:S(2)}, u32[]{:S(2)}) collective-permute-start(bf16[256,2048]{1,0:T(8,128)(2,1)} %get-tuple-element.91), channel_id=1, source_target_pairs={{0,2},{2,0},{4,6},{6,4},{8,10},{10,8},{12,14},{14,12},{16,18},{18,... | collective-permute-start | bytes 3145736 | tf_op jit(solution)/shard_map/ppermute | solution.py:337
  222.3 34.6 %collective-permute-start.27 = (bf16[256,2048]{1,0:T(8,128)(2,1)}, bf16[256,2048]{1,0:T(8,128)(2,1)S(1)}, u32[]{:S(2)}, u32[]{:S(2)}) collective-permute-start(bf16[256,2048]{1,0:T(8,128)(2,1)} %get-tuple-element.93), channel_id=1, source_target_pairs={{0,4},{2,6},{4,0},{6,2},{8,12},{10,14},{12,8},{14,10},{16,20},{18,... | collective-permute-start | bytes 3145736 | tf_op jit(solution)/shard_map/ppermute | solution.py:337
  225.9 31.1 %collective-permute-start.43 = (bf16[256,2048]{1,0:T(8,128)(2,1)S(1)}, bf16[256,2048]{1,0:T(8,128)(2,1)S(1)}, u32[]{:S(2)}, u32[]{:S(2)}) collective-permute-start(bf16[256,2048]{1,0:T(8,128)(2,1)S(1)} %pad_maximum_fusion), channel_id=1, source_target_pairs={{0,8},{2,10},{4,12},{6,14},{8,16},{10,18},{12,20},{14,22},{16,24},... | collective-permute-start | bytes 3145736 | tf_op jit(solution)/shard_map/ppermute | solution.py:482
  225.9 40.6 %collective-permute-start.25 = (bf16[256,2048]{1,0:T(8,128)(2,1)}, bf16[256,2048]{1,0:T(8,128)(2,1)}, u32[]{:S(2)}, u32[]{:S(2)}) collective-permute-start(bf16[256,2048]{1,0:T(8,128)(2,1)} %get-tuple-element.89), channel_id=1, source_target_pairs={{0,4},{2,6},{4,0},{6,2},{8,12},{10,14},{12,8},{14,10},{16,20},{18,... | collective-permute-start | bytes 3145736 | tf_op jit(solution)/shard_map/ppermute | solution.py:337
  227.5 39.0 %collective-permute-start.24 = (bf16[256,2048]{1,0:T(8,128)(2,1)}, bf16[256,2048]{1,0:T(8,128)(2,1)}, u32[]{:S(2)}, u32[]{:S(2)}) collective-permute-start(bf16[256,2048]{1,0:T(8,128)(2,1)} %get-tuple-element.87), channel_id=1, source_target_pairs={{0,2},{2,0},{4,6},{6,4},{8,10},{10,8},{12,14},{14,12},{16,18},{18,... | collective-permute-start | bytes 3145736 | tf_op jit(solution)/shard_map/ppermute | solution.py:337
  257.7 87.3 %collective-permute-start.47 = (bf16[256,2048]{1,0:T(8,128)(2,1)S(1)}, bf16[256,2048]{1,0:T(8,128)(2,1)S(1)}, u32[]{:S(2)}, u32[]{:S(2)}) collective-permute-start(bf16[256,2048]{1,0:T(8,128)(2,1)S(1)} %add_convert_fusion), channel_id=1, source_target_pairs={{0,8},{2,10},{4,12},{6,14},{8,16},{10,18},{12,20},{14,22},{16,24},... | collective-permute-start | bytes 3145736 | tf_op jit(solution)/shard_map/ppermute | solution.py:482
  266.5 32.6 %collective-permute-start.34 = (bf16[2,256,1024]{2,1,0:T(8,128)(2,1)}, bf16[2,256,1024]{2,1,0:T(8,128)(2,1)S(1)}, u32[]{:S(2)}, u32[]{:S(2)}) collective-permute-start(bf16[2,256,1024]{2,1,0:T(8,128)(2,1)} %get-tuple-element.114), channel_id=1, source_target_pairs={{0,2},{2,0},{4,6},{6,4},{8,10},{10,8},{12,14},{14,12},{16,18},{18,... | collective-permute-start | bytes 3145736 | tf_op jit(solution)/shard_map/ppermute | solution.py:337
  268.2 30.8 %collective-permute-start.35 = (bf16[2,256,1024]{2,1,0:T(8,128)(2,1)}, bf16[2,256,1024]{2,1,0:T(8,128)(2,1)S(1)}, u32[]{:S(2)}, u32[]{:S(2)}) collective-permute-start(bf16[2,256,1024]{2,1,0:T(8,128)(2,1)} %get-tuple-element.116), channel_id=1, source_target_pairs={{0,4},{2,6},{4,0},{6,2},{8,12},{10,14},{12,8},{14,10},{16,20},{18,... | collective-permute-start | bytes 3145736 | tf_op jit(solution)/shard_map/ppermute | solution.py:337
  302.9 26.8 %collective-permute-start.44 = (bf16[256,2048]{1,0:T(8,128)(2,1)S(1)}, bf16[256,2048]{1,0:T(8,128)(2,1)S(1)}, u32[]{:S(2)}, u32[]{:S(2)}) collective-permute-start(bf16[256,2048]{1,0:T(8,128)(2,1)S(1)} %add_convert_fusion.1), channel_id=1, source_target_pairs={{0,24},{2,26},{4,28},{6,30},{8,0},{10,2},{12,4},{14,6},{16,8},{18,... | collective-permute-start | bytes 3145736 | tf_op jit(solution)/shard_map/ppermute | solution.py:482
  305.9 23.8 %collective-permute-start.31 = (bf16[2048,128]{1,0:T(8,128)(2,1)S(1)}, bf16[2048,128]{1,0:T(8,128)(2,1)S(1)}, u32[]{:S(2)}, u32[]{:S(2)}) collective-permute-start(bf16[2048,128]{1,0:T(8,128)(2,1)S(1)} %copy-done.21), channel_id=1, source_target_pairs={{2,0},{4,2},{6,4},{8,6},{10,8},{12,10},{14,12},{16,14},{18,16},{20... | collective-permute-start | bytes 1572872 | tf_op jit(solution)/shard_map/ppermute | solution.py:530
  (42 other events, 531.3 us)
Sparse Core Ops, SparseCore 0:
  9.6 22.5 all-gather.1

commit v6 on v5

--- a/solution.py
+++ b/solution.py
@@ -16,7 +16,7 @@
 WEIGHT_STAGE = (2, 3, 4, 6)
 THIRD_STAGE = (7, 7, 8, 9)
 PRODUCT_STAGE = (6, 7)
-GATHER_SECOND = (2, 3, 4, 5)
+GATHER_SECOND = (2, 4, 4, 5)
 REDUCE_FIRST = (4, 5, 5, 7)
 REDUCE_SECOND = (6, 6, 6, 8)
 CLOSE_STAGE = 8
@@ -446,7 +446,7 @@
         by = far[k]
         if by in beside:
             keep, send_x, send_y, send_z = kept[k]
-            behind = (diag_a[depth - 1], diag_b[depth - 1])
+            behind = (diag_a[depth - 1], diag_b[depth - 1]) if by == 1 else ()
             kept[k] = (keep, stages.swap_x(send_x, *behind), stages.swap_y(send_y, *behind))
             crossed.append(lax.ppermute(send_z, "ctx", at.pairs_z(1 if by == 1 else -1)))
         else:

time: 354 us -> 356 us (level)
  waiting for transfers between devices: 129 us -> 97.6 us
  starting transfers between devices: 69.2 us -> 98.8 us
  other arithmetic: 18.2 us -> 22.3 us
    ppermute x6, waiting for transfers between devices: 67.7 us -> 45.6 us  [step_z(): lax.ppermute(after(held[(by - way) % depth], *earlier), 'ctx', at.pairs_z...]
    ppermute x24, starting transfers between devices: 23.7 us -> 45.4 us  [send(): lax.ppermute(after(array, *self.arrived[-self.back], *self.ready, *earlie...]
    ppermute x3, waiting for transfers between devices: 13.6 us -> 0.01 us  [reduce_third(): got = lax.ppermute(joint.astype(BF16), 'ctx', at.pairs_z(way))]
    ppermute x3, starting transfers between devices: 10.5 us -> 18.1 us  [reduce_filters(): total = total + lax.ppermute(at_z(by), 'ctx', at.pairs_z(by))]
    ppermute x2, waiting for transfers between devices: 13.5 us -> 19.9 us  [reduce_first(): lax.ppermute(send_z, 'ctx', at.pairs_z(1 if by == 1 else -1))]
    ppermute x2, waiting for transfers between devices: 10.7 us -> 5.64 us  [gather_second(): diag_a[k] = lax.ppermute(diag_a[0], 'ctx', pairs)]
    ppermute x2, starting transfers between devices: 1.96 us -> 6.37 us  [gather_second(): diag_a[k] = lax.ppermute(diag_a[0], 'ctx', pairs)]
  transfers between devices with their start and end apart: 49 -> 49, of which waited for: 16 -> 17; matrix products, arithmetic and copies ran while one was open for 7% -> 8% of each run, Pallas kernels for 32% -> 32%
where the time goes in v6:
time: 356 us
  Pallas kernels  112 us (31%)
  starting transfers between devices  98.8 us (28%)
  waiting for transfers between devices  97.6 us (27%)
  other arithmetic  22.3 us (6%)
  between operations  14.5 us (4%)
  local copies, waits for them, and re-layouts  10.2 us (3%)
    pallas_call x2, Pallas kernels, run_product(): pl.pallas_call(lambda *refs: product_kernel(count, *refs), grid_spec=pltp...  57.9 us
    ppermute x6, waiting for transfers between devices, step_z(): lax.ppermute(after(held[(by - way) % depth], *earlier), 'ctx', at.pairs_z...  45.6 us
    ppermute x24, starting transfers between devices, send(): lax.ppermute(after(array, *self.arrived[-self.back], *self.ready, *earlie...  45.4 us
    pallas_call x4, Pallas kernels, run_weight(): pl.pallas_call(kernel, grid_spec=pltpu.PrefetchScalarGridSpec(num_scalar_...  35.6 us
    ppermute x2, waiting for transfers between devices, reduce_first(): lax.ppermute(send_z, 'ctx', at.pairs_z(1 if by == 1 else -1))  19.9 us
    pallas_call x1, Pallas kernels, run_mix(): pl.pallas_call(mix_kernel, grid=(chan // group,), in_specs=[rows(taps), r...  18.6 us
    ppermute x3, starting transfers between devices, reduce_filters(): total = total + lax.ppermute(at_z(by), 'ctx', at.pairs_z(by))  18.1 us
    ppermute x24, waiting for transfers between devices, send(): lax.ppermute(after(array, *self.arrived[-self.back], *self.ready, *earlie...  9.66 us
  transfers between devices with their start and end apart: 49, of which 17 were waited for; matrix products, arithmetic and copies ran while one was open for 8% of the time, Pallas kernels for 32%

profile of v6, /device:TPU:0, one launch (start us, length us, event | category | flops | bytes accessed | tf_op | source)
XLA Modules:
  0.0 355.6 jit_solution(11856346968142122450)
XLA Ops:
  7.9 3.0 collective-permute-start.3
  23.0 19.3 %collective-permute-done.5.refs_6_ = bf16[2048,256]{1,0:T(8,128)(2,1)} collective-permute-done((bf16[2048,256]{1,0:T(8,128)(2,1)S(1)}, bf16[2048,256]{1,0:T(8,128)(2,1)}, u32[]{:S(2)}, u32[]{:S(2)}) %collective-permute-start.5) | collective-permute-done | bytes 1048608 | tf_op jit(solution)/shard_map/ppermute | solution.py:401
  42.3 3.8 %collective-permute-start.14 = (bf16[2,2,128,128]{3,2,1,0:T(8,128)(2,1)}, bf16[2,2,128,128]{3,2,1,0:T(8,128)(2,1)S(1)}, u32[]{:S(2)}, u32[]{:S(2)}) collective-permute-start(bf16[2,2,128,128]{3,2,1,0:T(8,128)(2,1)} %pad_maximum_fusion.1), channel_id=1, source_target_pairs={{0,24},{2,26},{4,28},{6,30},{8,0},{10,2},{12,4},{14,6},{16,8},{18,... | collective-permute-start | bytes 393224 | tf_op jit(solution)/shard_map/ppermute | solution.py:401
  55.8 8.2 %collective-permute-done.16 = bf16[2,2,128,128]{3,2,1,0:T(8,128)(2,1)S(1)} collective-permute-done((bf16[2,2,128,128]{3,2,1,0:T(8,128)(2,1)S(1)}, bf16[2,2,128,128]{3,2,1,0:T(8,128)(2,1)S(1)}, u32[]{:S(2)}, u32[]{:S(2)}) %collective-permute-start.16) | collective-permute-done | bytes 131104 | tf_op jit(solution)/shard_map/ppermute | solution.py:401
  65.1 18.1 %collective-permute-done.9.refs_10_ = bf16[2048,256]{1,0:T(8,128)(2,1)} collective-permute-done((bf16[2048,256]{1,0:T(8,128)(2,1)S(1)}, bf16[2048,256]{1,0:T(8,128)(2,1)}, u32[]{:S(2)}, u32[]{:S(2)}) %collective-permute-start.9) | collective-permute-done | bytes 1048608 | tf_op jit(solution)/shard_map/ppermute | solution.py:401
  85.3 7.3 %collective-permute-start.11 = (bf16[2048,256]{1,0:T(8,128)(2,1)}, bf16[2048,256]{1,0:T(8,128)(2,1)S(1)}, u32[]{:S(2)}, u32[]{:S(2)}) collective-permute-start(bf16[2048,256]{1,0:T(8,128)(2,1)} %collective-permute-done.9.refs_10_), channel_id=1, source_target_pairs={{0,4},{2,6},{4,0},{6,2},{8,12},{10,14},{12,8},{14,10},{16,20},{18,... | collective-permute-start | bytes 3145736 | tf_op jit(solution)/shard_map/ppermute | solution.py:337
  92.7 4.7 %collective-permute-done.7.refs_8_ = bf16[2048,256]{1,0:T(8,128)(2,1)} collective-permute-done((bf16[2048,256]{1,0:T(8,128)(2,1)}, bf16[2048,256]{1,0:T(8,128)(2,1)}, u32[]{:S(2)}, u32[]{:S(2)}) %collective-permute-start.7) | collective-permute-done | bytes 1048608 | tf_op jit(solution)/shard_map/ppermute | solution.py:337
  97.4 18.6 %mix_kernel.1 = (bf16[2048,1024]{1,0:T(8,128)(2,1)}, bf16[2048,1024]{1,0:T(8,128)(2,1)}) custom-call(bf16[2048,128]{1,0:T(8,128)(2,1)} %bitcast.132, bf16[2048,1024]{1,0:T(8,128)(2,1)} %refs_20_.3, bf16[2048,128]{1,0:T(8,128)(2,1)} %copy-done.18, bf16[2048,1024]{1,0:T(8,128)(2,1)} %refs_19_.3, bf16[256,256]{1,0:T(8,128)(2,1)} %constant.124.clone.forward_ref.refs_23_, ...), custom_call_target="tpu_custom_call" | custom-call | flops 7516192768 | bytes 16777216 | tf_op jit(solution)/shard_map/mix_kernel/pallas_call | solution.py:103
  116.0 3.9 %collective-permute-start.12 = (bf16[1024,256]{1,0:T(8,128)(2,1)}, bf16[1024,256]{1,0:T(8,128)(2,1)}, u32[]{:S(2)}, u32[]{:S(2)}) collective-permute-start(bf16[1024,256]{1,0:T(8,128)(2,1)} %collective-permute-done.2.refs_5_), channel_id=1, source_target_pairs={{0,24},{2,26},{4,28},{6,30},{8,0},{10,2},{12,4},{14,6},{16,8},{18,... | collective-permute-start | bytes 1572872 | tf_op jit(solution)/shard_map/ppermute | solution.py:428
  119.9 8.7 %weight_kernel.4 = (bf16[2,256,1024]{2,1,0:T(8,128)(2,1)}, bf16[2,256,1024]{2,1,0:T(8,128)(2,1)}, bf16[2,256,1024]{2,1,0:T(8,128)(2,1)}, bf16[2,256,1024]{2,1,0:T(8,128)(2,1)}) custom-call(s32[4]{0:T(128)} %get-tuple-element.133.place_ref, bf16[4096,1024]{1,0:T(8,128)(2,1)} %all-gather.2.cloned.1.call-done.g00.g01.g10.g11.refs_1_, ...), custom_call_target="tpu_custom_call" | custom-call | flops 4294967296 | bytes 10485760 | tf_op jit(solution)/shard_map/weight_kernel/pallas_call | solution.py:166
  132.6 2.9 collective-permute-start.22
  135.5 8.8 %weight_kernel.6 = (bf16[256,2048]{1,0:T(8,128)(2,1)}, bf16[256,2048]{1,0:T(8,128)(2,1)}, bf16[256,2048]{1,0:T(8,128)(2,1)}, bf16[256,2048]{1,0:T(8,128)(2,1)}) custom-call(s32[4]{0:T(128)} %pad_add_fusion.2.place_ref, bf16[4096,1024]{1,0:T(8,128)(2,1)} %all-gather.2.cloned.1.call-done.g00.g01.g10.g11.refs_1_, ...), custom_call_target="tpu_custom_call" | custom-call | flops 4294967296 | bytes 10485760 | tf_op jit(solution)/shard_map/weight_kernel/pallas_call | solution.py:166
  145.7 3.5 collective-permute-start.21
  149.2 3.9 %collective-permute-done.22.refs_13_ = bf16[1024,256]{1,0:T(8,128)(2,1)S(1)} collective-permute-done((bf16[1024,256]{1,0:T(8,128)(2,1)}, bf16[1024,256]{1,0:T(8,128)(2,1)S(1)}, u32[]{:S(2)}, u32[]{:S(2)}) %collective-permute-start.22) | collective-permute-done | bytes 524320 | tf_op jit(solution)/shard_map/ppermute | solution.py:427
  153.1 8.8 %weight_kernel.5 = (bf16[256,2048]{1,0:T(8,128)(2,1)}, bf16[256,2048]{1,0:T(8,128)(2,1)}, bf16[256,2048]{1,0:T(8,128)(2,1)}, bf16[256,2048]{1,0:T(8,128)(2,1)}) custom-call(s32[4]{0:T(128)} %get-tuple-element.134.place_ref, bf16[4096,1024]{1,0:T(8,128)(2,1)} %all-gather.2.cloned.1.call-done.g00.g01.g10.g11.refs_1_, ...), custom_call_target="tpu_custom_call" | custom-call | flops 4294967296 | bytes 10485760 | tf_op jit(solution)/shard_map/weight_kernel/pallas_call | solution.py:166
  164.5 3.3 collective-permute-start.32
  171.8 4.4 %collective-permute-start.23 = (bf16[1024,256]{1,0:T(8,128)(2,1)}, bf16[1024,256]{1,0:T(8,128)(2,1)S(1)}, u32[]{:S(2)}, u32[]{:S(2)}) collective-permute-start(bf16[1024,256]{1,0:T(8,128)(2,1)} %slice.105), channel_id=1, source_target_pairs={{0,4},{2,6},{4,0},{6,2},{8,12},{10,14},{12,8},{14,10},{16,20},{18,... | collective-permute-start | bytes 1572872 | tf_op jit(solution)/shard_map/ppermute | solution.py:337
  182.3 9.5 %collective-permute-done.33.refs_2_.refs_3_ = bf16[256,2048]{1,0:T(8,128)(2,1)S(1)} collective-permute-done((bf16[256,2048]{1,0:T(8,128)(2,1)}, bf16[256,2048]{1,0:T(8,128)(2,1)S(1)}, u32[]{:S(2)}, u32[]{:S(2)}) %collective-permute-start.33) | collective-permute-done | bytes 1048608 | tf_op jit(solution)/shard_map/ppermute | solution.py:451
  191.8 3.8 %collective-permute-start.41 = (bf16[256,1024]{1,0:T(8,128)(2,1)}, bf16[256,1024]{1,0:T(8,128)(2,1)}, u32[]{:S(2)}, u32[]{:S(2)}) collective-permute-start(bf16[256,1024]{1,0:T(8,128)(2,1)} %fusion.6), channel_id=1, source_target_pairs={{0,4},{2,6},{4,0},{6,2},{8,12},{10,14},{12,8},{14,10},{16,20},{18,... | collective-permute-start | bytes 1572872 | tf_op jit(solution)/shard_map/ppermute | solution.py:337
  195.6 10.4 %collective-permute-done.32.refs_0_.refs_1_ = bf16[256,2048]{1,0:T(8,128)(2,1)S(1)} collective-permute-done((bf16[256,2048]{1,0:T(8,128)(2,1)}, bf16[256,2048]{1,0:T(8,128)(2,1)S(1)}, u32[]{:S(2)}, u32[]{:S(2)}) %collective-permute-start.32) | collective-permute-done | bytes 1048608 | tf_op jit(solution)/shard_map/ppermute | solution.py:451
  205.9 2.8 collective-permute-start.26
  208.7 9.4 %weight_kernel.7 = (bf16[2,256,1024]{2,1,0:T(8,128)(2,1)}, bf16[2,256,1024]{2,1,0:T(8,128)(2,1)}, bf16[2,256,1024]{2,1,0:T(8,128)(2,1)}, bf16[2,256,1024]{2,1,0:T(8,128)(2,1)}) custom-call(s32[4]{0:T(128)} %pad_add_fusion.3.place_ref, bf16[4096,1024]{1,0:T(8,128)(2,1)} %all-gather.2.cloned.1.call-done.g00.g01.g10.g11.refs_1_, ...), custom_call_target="tpu_custom_call" | custom-call | flops 4294967296 | bytes 10485760 | tf_op jit(solution)/shard_map/weight_kernel/pallas_call | solution.py:166
  225.7 28.9 %product_kernel.2 = (f32[2048,1024]{1,0:T(8,128)}, bf16[2048,1024]{1,0:T(8,128)(2,1)}, f32[2048,128]{1,0:T(8,128)}, bf16[2048,128]{1,0:T(8,128)(2,1)}, f32[2048,128]{1,0:T(8,128)}) custom-call(s32[16]{0:T(128)} %stack.173.refs_0_, bf16[4096,1024]{1,0:T(8,128)(2,1)} %all-gather.2.cloned.1.call-done.g00.g01.g10.g11.refs_1_, bf16[2048,256]{1,0:T(8,128)(2,1)} %bitcast.130, ...), custom_call_target="tpu_custom_call" | custom-call | flops 12884901888 | bytes 29360128 | tf_op jit(solution)/shard_map/product_kernel/pallas_call | solution.py:262
  254.6 2.8 add_convert_fusion.1
  257.4 3.4 collective-permute-start.44
  260.8 4.9 %collective-permute-done.27 = bf16[256,2048]{1,0:T(8,128)(2,1)S(1)} collective-permute-done((bf16[256,2048]{1,0:T(8,128)(2,1)}, bf16[256,2048]{1,0:T(8,128)(2,1)S(1)}, u32[]{:S(2)}, u32[]{:S(2)}) %collective-permute-start.27) | collective-permute-done | bytes 1048608 | tf_op jit(solution)/shard_map/ppermute | solution.py:337
  267.2 29.1 %product_kernel.3 = (f32[2048,1024]{1,0:T(8,128)}, bf16[2048,1024]{1,0:T(8,128)(2,1)}, f32[2048,128]{1,0:T(8,128)}, bf16[2048,128]{1,0:T(8,128)(2,1)}, f32[2048,128]{1,0:T(8,128)}) custom-call(s32[16]{0:T(128)} %stack.173.refs_0_, ...), custom_call_target="tpu_custom_call", output_to_operand_aliasing={{0}: (25, {}), {1}: (26, {}), {2}: (27, {}), {3}: (28, {}),... | custom-call | flops 12884901888 | bytes 29360128 | tf_op jit(solution)/shard_map/product_kernel/pallas_call | solution.py:262
  306.1 4.2 %collective-permute-done.37 = bf16[4,128,128]{2,1,0:T(8,128)(2,1)S(1)} collective-permute-done((bf16[4,128,128]{2,1,0:T(8,128)(2,1)S(1)}, bf16[4,128,128]{2,1,0:T(8,128)(2,1)S(1)}, u32[]{:S(2)}, u32[]{:S(2)}) %collective-permute-start.37) | collective-permute-done | bytes 131104 | tf_op jit(solution)/shard_map/ppermute | solution.py:362
  311.4 9.8 %collective-permute-start.46 = (bf16[256,1024]{1,0:T(8,128)(2,1)S(1)}, bf16[256,1024]{1,0:T(8,128)(2,1)S(1)}, u32[]{:S(2)}, u32[]{:S(2)}) collective-permute-start(bf16[256,1024]{1,0:T(8,128)(2,1)S(1)} %fusion.8), channel_id=1, source_target_pairs={{0,2},{2,0},{4,6},{6,4},{8,10},{10,8},{12,14},{14,12},{16,18},{18,... | collective-permute-start | bytes 1572872 | tf_op jit(solution)/shard_map/ppermute | solution.py:337
  321.3 17.0 %collective-permute-start.40 = (f32[128,128]{1,0:T(8,128)S(1)}, f32[128,128]{1,0:T(8,128)S(1)}, u32[]{:S(2)}, u32[]{:S(2)}) collective-permute-start(f32[128,128]{1,0:T(8,128)S(1)} %get-tuple-element.127), channel_id=1, source_target_pairs={{0,24},{2,26},{4,28},{6,30},{8,0},{10,2},{12,4},{14,6},{16,8},{18,... | collective-permute-start | bytes 196616 | tf_op jit(solution)/shard_map/ppermute | solution.py:368
  340.8 3.8 %collective-permute-done.39 = f32[128,128]{1,0:T(8,128)S(1)} collective-permute-done((f32[128,128]{1,0:T(8,128)S(1)}, f32[128,128]{1,0:T(8,128)S(1)}, u32[]{:S(2)}, u32[]{:S(2)}) %collective-permute-start.39) | collective-permute-done | bytes 65568 | tf_op jit(solution)/shard_map/ppermute | solution.py:368
  345.8 3.0 fusion.1
  (166 shorter events, 67.5 us)
Async XLA Ops:
  7.2 112.7 %all-gather.2.cloned.1.call-start = ((), (), s32[]{:S(2)}) async-start(), calls=%async_computation | async-start | bytes 12582912 | tf_op jit(solution)/shard_map/all_gather | solution.py:385
  19.3 29.4 %collective-permute-start.1 = (bf16[2048,256]{1,0:T(8,128)(2,1)S(1)}, bf16[2048,256]{1,0:T(8,128)(2,1)S(1)}, u32[]{:S(2)}, u32[]{:S(2)}) collective-permute-start(bf16[2048,256]{1,0:T(8,128)(2,1)S(1)} %bitcast.127), channel_id=1, source_target_pairs={{0,4},{2,6},{4,0},{6,2},{8,12},{10,14},{12,8},{14,10},{16,20},{18,... | collective-permute-start | bytes 3145736 | tf_op jit(solution)/shard_map/ppermute | solution.py:337
  20.8 28.7 %collective-permute-start = (bf16[2048,256]{1,0:T(8,128)(2,1)S(1)}, bf16[2048,256]{1,0:T(8,128)(2,1)S(1)}, u32[]{:S(2)}, u32[]{:S(2)}) collective-permute-start(bf16[2048,256]{1,0:T(8,128)(2,1)S(1)} %bitcast.128), channel_id=1, source_target_pairs={{0,2},{2,0},{4,6},{6,4},{8,10},{10,8},{12,14},{14,12},{16,18},{18,... | collective-permute-start | bytes 3145736 | tf_op jit(solution)/shard_map/ppermute | solution.py:337
  49.6 35.7 %collective-permute-start.2 = (bf16[1024,256]{1,0:T(8,128)(2,1)S(1)}, bf16[1024,256]{1,0:T(8,128)(2,1)}, u32[]{:S(2)}, u32[]{:S(2)}) collective-permute-start(bf16[1024,256]{1,0:T(8,128)(2,1)S(1)} %slice.104), channel_id=1, source_target_pairs={{0,4},{2,6},{4,0},{6,2},{8,12},{10,14},{12,8},{14,10},{16,20},{18,... | collective-permute-start | bytes 1572872 | tf_op jit(solution)/shard_map/ppermute | solution.py:337
  51.2 46.2 %collective-permute-start.7 = (bf16[2048,256]{1,0:T(8,128)(2,1)}, bf16[2048,256]{1,0:T(8,128)(2,1)}, u32[]{:S(2)}, u32[]{:S(2)}) collective-permute-start(bf16[2048,256]{1,0:T(8,128)(2,1)} %collective-permute-done.5.refs_6_), channel_id=1, source_target_pairs={{0,4},{2,6},{4,0},{6,2},{8,12},{10,14},{12,8},{14,10},{16,20},{18,... | collective-permute-start | bytes 3145736 | tf_op jit(solution)/shard_map/ppermute | solution.py:337
  51.7 64.3 %collective-permute-start.6 = (bf16[2048,256]{1,0:T(8,128)(2,1)}, bf16[2048,256]{1,0:T(8,128)(2,1)}, u32[]{:S(2)}, u32[]{:S(2)}) collective-permute-start(bf16[2048,256]{1,0:T(8,128)(2,1)} %collective-permute-done.5.refs_6_), channel_id=1, source_target_pairs={{0,2},{2,0},{4,6},{6,4},{8,10},{10,8},{12,14},{14,12},{16,18},{18,... | collective-permute-start | bytes 3145736 | tf_op jit(solution)/shard_map/ppermute | solution.py:337
  53.2 39.4 %collective-permute-start.17 = (bf16[2048,128]{1,0:T(8,128)(2,1)S(1)}, bf16[2048,128]{1,0:T(8,128)(2,1)S(1)}, u32[]{:S(2)}, u32[]{:S(2)}) collective-permute-start(bf16[2048,128]{1,0:T(8,128)(2,1)S(1)} %copy-done.21), channel_id=1, source_target_pairs={{0,2},{2,4},{4,6},{6,8},{8,10},{10,12},{12,14},{14,16},{16,18},{18... | collective-permute-start | bytes 1572872 | tf_op jit(solution)/shard_map/ppermute | solution.py:413
  83.1 46.4 %collective-permute-start.20 = (bf16[1024,256]{1,0:T(8,128)(2,1)}, bf16[1024,256]{1,0:T(8,128)(2,1)}, u32[]{:S(2)}, u32[]{:S(2)}) collective-permute-start(bf16[1024,256]{1,0:T(8,128)(2,1)} %slice.106), channel_id=1, source_target_pairs={{0,2},{2,0},{4,6},{6,4},{8,10},{10,8},{12,14},{14,12},{16,18},{18,... | collective-permute-start | bytes 1572872 | tf_op jit(solution)/shard_map/ppermute | solution.py:337
  85.3 47.3 %collective-permute-start.11 = (bf16[2048,256]{1,0:T(8,128)(2,1)}, bf16[2048,256]{1,0:T(8,128)(2,1)S(1)}, u32[]{:S(2)}, u32[]{:S(2)}) collective-permute-start(bf16[2048,256]{1,0:T(8,128)(2,1)} %collective-permute-done.9.refs_10_), channel_id=1, source_target_pairs={{0,4},{2,6},{4,0},{6,2},{8,12},{10,14},{12,8},{14,10},{16,20},{18,... | collective-permute-start | bytes 3145736 | tf_op jit(solution)/shard_map/ppermute | solution.py:337
  92.7 42.8 %collective-permute-start.10 = (bf16[2048,256]{1,0:T(8,128)(2,1)}, bf16[2048,256]{1,0:T(8,128)(2,1)S(1)}, u32[]{:S(2)}, u32[]{:S(2)}) collective-permute-start(bf16[2048,256]{1,0:T(8,128)(2,1)} %collective-permute-done.9.refs_10_), channel_id=1, source_target_pairs={{0,2},{2,0},{4,6},{6,4},{8,10},{10,8},{12,14},{14,12},{16,18},{18,... | collective-permute-start | bytes 3145736 | tf_op jit(solution)/shard_map/ppermute | solution.py:337
  97.4 31.1 %collective-permute-start.13 = (bf16[2048,256]{1,0:T(8,128)(2,1)}, bf16[2048,256]{1,0:T(8,128)(2,1)S(1)}, u32[]{:S(2)}, u32[]{:S(2)}) collective-permute-start(bf16[2048,256]{1,0:T(8,128)(2,1)} %collective-permute-done.5.refs_6_), channel_id=1, source_target_pairs={{0,8},{2,10},{4,12},{6,14},{8,16},{10,18},{12,20},{14,22},{16,24},... | collective-permute-start | bytes 3145736 | tf_op jit(solution)/shard_map/ppermute | solution.py:401
  116.0 28.3 %collective-permute-start.12 = (bf16[1024,256]{1,0:T(8,128)(2,1)}, bf16[1024,256]{1,0:T(8,128)(2,1)}, u32[]{:S(2)}, u32[]{:S(2)}) collective-permute-start(bf16[1024,256]{1,0:T(8,128)(2,1)} %collective-permute-done.2.refs_5_), channel_id=1, source_target_pairs={{0,24},{2,26},{4,28},{6,30},{8,0},{10,2},{12,4},{14,6},{16,8},{18,... | collective-permute-start | bytes 1572872 | tf_op jit(solution)/shard_map/ppermute | solution.py:428
  129.5 34.1 %collective-permute-start.19 = (bf16[2048,256]{1,0:T(8,128)(2,1)}, bf16[2048,256]{1,0:T(8,128)(2,1)S(1)}, u32[]{:S(2)}, u32[]{:S(2)}) collective-permute-start(bf16[2048,256]{1,0:T(8,128)(2,1)} %copy-done.17), channel_id=1, source_target_pairs={{0,4},{2,6},{4,0},{6,2},{8,12},{10,14},{12,8},{14,10},{16,20},{18,... | collective-permute-start | bytes 3145736 | tf_op jit(solution)/shard_map/ppermute | solution.py:337
  135.5 34.4 %collective-permute-start.18 = (bf16[2048,256]{1,0:T(8,128)(2,1)}, bf16[2048,256]{1,0:T(8,128)(2,1)}, u32[]{:S(2)}, u32[]{:S(2)}) collective-permute-start(bf16[2048,256]{1,0:T(8,128)(2,1)} %copy-done.17), channel_id=1, source_target_pairs={{0,2},{2,0},{4,6},{6,4},{8,10},{10,8},{12,14},{14,12},{16,18},{18,... | collective-permute-start | bytes 3145736 | tf_op jit(solution)/shard_map/ppermute | solution.py:337
  144.3 31.9 %collective-permute-start.30 = (bf16[2,256,1024]{2,1,0:T(8,128)(2,1)}, bf16[2,256,1024]{2,1,0:T(8,128)(2,1)}, u32[]{:S(2)}, u32[]{:S(2)}) collective-permute-start(bf16[2,256,1024]{2,1,0:T(8,128)(2,1)} %get-tuple-element.98), channel_id=1, source_target_pairs={{0,4},{2,6},{4,0},{6,2},{8,12},{10,14},{12,8},{14,10},{16,20},{18,... | collective-permute-start | bytes 3145736 | tf_op jit(solution)/shard_map/ppermute | solution.py:337
  163.7 28.1 %collective-permute-start.33 = (bf16[256,2048]{1,0:T(8,128)(2,1)}, bf16[256,2048]{1,0:T(8,128)(2,1)S(1)}, u32[]{:S(2)}, u32[]{:S(2)}) collective-permute-start(bf16[256,2048]{1,0:T(8,128)(2,1)} %get-tuple-element.112), channel_id=1, source_target_pairs={{0,8},{2,10},{4,12},{6,14},{8,16},{10,18},{12,20},{14,22},{16,24},... | collective-permute-start | bytes 3145736 | tf_op jit(solution)/shard_map/ppermute | solution.py:451
  164.5 41.5 %collective-permute-start.32 = (bf16[256,2048]{1,0:T(8,128)(2,1)}, bf16[256,2048]{1,0:T(8,128)(2,1)S(1)}, u32[]{:S(2)}, u32[]{:S(2)}) collective-permute-start(bf16[256,2048]{1,0:T(8,128)(2,1)} %get-tuple-element.111), channel_id=1, source_target_pairs={{0,24},{2,26},{4,28},{6,30},{8,0},{10,2},{12,4},{14,6},{16,8},{18,... | collective-permute-start | bytes 3145736 | tf_op jit(solution)/shard_map/ppermute | solution.py:451
  171.8 46.3 %collective-permute-start.23 = (bf16[1024,256]{1,0:T(8,128)(2,1)}, bf16[1024,256]{1,0:T(8,128)(2,1)S(1)}, u32[]{:S(2)}, u32[]{:S(2)}) collective-permute-start(bf16[1024,256]{1,0:T(8,128)(2,1)} %slice.105), channel_id=1, source_target_pairs={{0,4},{2,6},{4,0},{6,2},{8,12},{10,14},{12,8},{14,10},{16,20},{18,... | collective-permute-start | bytes 1572872 | tf_op jit(solution)/shard_map/ppermute | solution.py:337
  176.2 42.0 %collective-permute-start.24 = (bf16[1024,256]{1,0:T(8,128)(2,1)}, bf16[1024,256]{1,0:T(8,128)(2,1)}, u32[]{:S(2)}, u32[]{:S(2)}) collective-permute-start(bf16[1024,256]{1,0:T(8,128)(2,1)} %slice.107), channel_id=1, source_target_pairs={{0,2},{2,0},{4,6},{6,4},{8,10},{10,8},{12,14},{14,12},{16,18},{18,... | collective-permute-start | bytes 1572872 | tf_op jit(solution)/shard_map/ppermute | solution.py:337
  178.2 42.0 %collective-permute-start.42 = (bf16[256,1024]{1,0:T(8,128)(2,1)}, bf16[256,1024]{1,0:T(8,128)(2,1)}, u32[]{:S(2)}, u32[]{:S(2)}) collective-permute-start(bf16[256,1024]{1,0:T(8,128)(2,1)} %fusion.7), channel_id=1, source_target_pairs={{0,2},{2,0},{4,6},{6,4},{8,10},{10,8},{12,14},{14,12},{16,18},{18,... | collective-permute-start | bytes 1572872 | tf_op jit(solution)/shard_map/ppermute | solution.py:337
  191.8 30.9 %collective-permute-start.41 = (bf16[256,1024]{1,0:T(8,128)(2,1)}, bf16[256,1024]{1,0:T(8,128)(2,1)}, u32[]{:S(2)}, u32[]{:S(2)}) collective-permute-start(bf16[256,1024]{1,0:T(8,128)(2,1)} %fusion.6), channel_id=1, source_target_pairs={{0,4},{2,6},{4,0},{6,2},{8,12},{10,14},{12,8},{14,10},{16,20},{18,... | collective-permute-start | bytes 1572872 | tf_op jit(solution)/shard_map/ppermute | solution.py:337
  205.9 48.6 %collective-permute-start.26 = (bf16[256,2048]{1,0:T(8,128)(2,1)}, bf16[256,2048]{1,0:T(8,128)(2,1)}, u32[]{:S(2)}, u32[]{:S(2)}) collective-permute-start(bf16[256,2048]{1,0:T(8,128)(2,1)} %get-tuple-element.89), channel_id=1, source_target_pairs={{0,4},{2,6},{4,0},{6,2},{8,12},{10,14},{12,8},{14,10},{16,20},{18,... | collective-permute-start | bytes 3145736 | tf_op jit(solution)/shard_map/ppermute | solution.py:337
  218.1 36.5 %collective-permute-start.25 = (bf16[256,2048]{1,0:T(8,128)(2,1)}, bf16[256,2048]{1,0:T(8,128)(2,1)S(1)}, u32[]{:S(2)}, u32[]{:S(2)}) collective-permute-start(bf16[256,2048]{1,0:T(8,128)(2,1)} %get-tuple-element.87), channel_id=1, source_target_pairs={{0,2},{2,0},{4,6},{6,4},{8,10},{10,8},{12,14},{14,12},{16,18},{18,... | collective-permute-start | bytes 3145736 | tf_op jit(solution)/shard_map/ppermute | solution.py:337
  218.9 46.7 %collective-permute-start.27 = (bf16[256,2048]{1,0:T(8,128)(2,1)}, bf16[256,2048]{1,0:T(8,128)(2,1)S(1)}, u32[]{:S(2)}, u32[]{:S(2)}) collective-permute-start(bf16[256,2048]{1,0:T(8,128)(2,1)} %get-tuple-element.91), channel_id=1, source_target_pairs={{0,2},{2,0},{4,6},{6,4},{8,10},{10,8},{12,14},{14,12},{16,18},{18,... | collective-permute-start | bytes 3145736 | tf_op jit(solution)/shard_map/ppermute | solution.py:337
  220.2 45.4 %collective-permute-start.28 = (bf16[256,2048]{1,0:T(8,128)(2,1)}, bf16[256,2048]{1,0:T(8,128)(2,1)S(1)}, u32[]{:S(2)}, u32[]{:S(2)}) collective-permute-start(bf16[256,2048]{1,0:T(8,128)(2,1)} %get-tuple-element.93), channel_id=1, source_target_pairs={{0,4},{2,6},{4,0},{6,2},{8,12},{10,14},{12,8},{14,10},{16,20},{18,... | collective-permute-start | bytes 3145736 | tf_op jit(solution)/shard_map/ppermute | solution.py:337
  225.2 74.1 %collective-permute-start.43 = (bf16[256,2048]{1,0:T(8,128)(2,1)}, bf16[256,2048]{1,0:T(8,128)(2,1)}, u32[]{:S(2)}, u32[]{:S(2)}) collective-permute-start(bf16[256,2048]{1,0:T(8,128)(2,1)} %pad_maximum_fusion), channel_id=1, source_target_pairs={{0,8},{2,10},{4,12},{6,14},{8,16},{10,18},{12,20},{14,22},{16,24},... | collective-permute-start | bytes 3145736 | tf_op jit(solution)/shard_map/ppermute | solution.py:482
  257.4 54.0 %collective-permute-start.44 = (bf16[256,2048]{1,0:T(8,128)(2,1)}, bf16[256,2048]{1,0:T(8,128)(2,1)}, u32[]{:S(2)}, u32[]{:S(2)}) collective-permute-start(bf16[256,2048]{1,0:T(8,128)(2,1)} %add_convert_fusion.1), channel_id=1, source_target_pairs={{0,24},{2,26},{4,28},{6,30},{8,0},{10,2},{12,4},{14,6},{16,8},{18,... | collective-permute-start | bytes 3145736 | tf_op jit(solution)/shard_map/ppermute | solution.py:482
  265.7 30.6 %collective-permute-start.34 = (bf16[2,256,1024]{2,1,0:T(8,128)(2,1)}, bf16[2,256,1024]{2,1,0:T(8,128)(2,1)S(1)}, u32[]{:S(2)}, u32[]{:S(2)}) collective-permute-start(bf16[2,256,1024]{2,1,0:T(8,128)(2,1)} %get-tuple-element.114), channel_id=1, source_target_pairs={{0,2},{2,0},{4,6},{6,4},{8,10},{10,8},{12,14},{14,12},{16,18},{18,... | collective-permute-start | bytes 3145736 | tf_op jit(solution)/shard_map/ppermute | solution.py:337
  265.9 30.3 %collective-permute-start.35 = (bf16[2,256,1024]{2,1,0:T(8,128)(2,1)}, bf16[2,256,1024]{2,1,0:T(8,128)(2,1)S(1)}, u32[]{:S(2)}, u32[]{:S(2)}) collective-permute-start(bf16[2,256,1024]{2,1,0:T(8,128)(2,1)} %get-tuple-element.116), channel_id=1, source_target_pairs={{0,4},{2,6},{4,0},{6,2},{8,12},{10,14},{12,8},{14,10},{16,20},{18,... | collective-permute-start | bytes 3145736 | tf_op jit(solution)/shard_map/ppermute | solution.py:337
  301.3 44.5 %collective-permute-start.47 = (bf16[256,2048]{1,0:T(8,128)(2,1)S(1)}, bf16[256,2048]{1,0:T(8,128)(2,1)S(1)}, u32[]{:S(2)}, u32[]{:S(2)}) collective-permute-start(bf16[256,2048]{1,0:T(8,128)(2,1)S(1)} %add_convert_fusion), channel_id=1, source_target_pairs={{0,8},{2,10},{4,12},{6,14},{8,16},{10,18},{12,20},{14,22},{16,24},... | collective-permute-start | bytes 3145736 | tf_op jit(solution)/shard_map/ppermute | solution.py:482
  310.3 29.1 %collective-permute-start.38 = (f32[128,128]{1,0:T(8,128)S(1)}, f32[128,128]{1,0:T(8,128)S(1)}, u32[]{:S(2)}, u32[]{:S(2)}) collective-permute-start(f32[128,128]{1,0:T(8,128)S(1)} %get-tuple-element.126), channel_id=1, source_target_pairs={{0,8},{2,10},{4,12},{6,14},{8,16},{10,18},{12,20},{14,22},{16,24},... | collective-permute-start | bytes 196616 | tf_op jit(solution)/shard_map/ppermute | solution.py:368
  311.4 33.9 %collective-permute-start.46 = (bf16[256,1024]{1,0:T(8,128)(2,1)S(1)}, bf16[256,1024]{1,0:T(8,128)(2,1)S(1)}, u32[]{:S(2)}, u32[]{:S(2)}) collective-permute-start(bf16[256,1024]{1,0:T(8,128)(2,1)S(1)} %fusion.8), channel_id=1, source_target_pairs={{0,2},{2,0},{4,6},{6,4},{8,10},{10,8},{12,14},{14,12},{16,18},{18,... | collective-permute-start | bytes 1572872 | tf_op jit(solution)/shard_map/ppermute | solution.py:337
  (42 other events, 552.5 us)
Sparse Core Ops, SparseCore 0:
  9.6 22.5 all-gather.1
